TPU v7x, 32 devices: a whole 2x2x4 slice. The times are simulated.
32 devices in a mesh: ctx: 16 (over z, y, core), fsdp: 2 (over x).
Axes of the slice: x: 2, y: 2, z: 4, core: 2. Of those that a mesh axis runs over, the one named last changes fastest.
Arguments:
- tokens: bfloat16 [4096, 1024], P(('ctx', 'fsdp')), may hold values from -6 to 6
- cotangent: bfloat16 [4096, 1024], P(('ctx', 'fsdp')), may hold values from -6 to 6
- lengths: int32 [2, 2], P('fsdp'), may hold values from 256 to 1024, as said below
- stretch_ids: int32 [16, 2, 2], P(None, 'fsdp'), may hold values from 0 to 31, as said below
- w_query: bfloat16 [2, 1024, 2048], P(None, 'fsdp'), may hold values from -0.1875 to 0.1875
- key_projection_weight: bfloat16 [2, 1024, 1024], P(None, 'fsdp'), may hold values from -0.1875 to 0.1875
- value_projection_weight: bfloat16 [2, 1024, 1024], P(None, 'fsdp'), may hold values from -0.1875 to 0.1875
- w_out: bfloat16 [2, 2048, 1024], P(None, 'fsdp'), may hold values from -1 to 1
- w_gate: bfloat16 [2, 1024, 3072], P(None, 'fsdp'), may hold values from -0.1875 to 0.1875
- w_up: bfloat16 [2, 1024, 3072], P(None, 'fsdp'), may hold values from -0.1875 to 0.1875
- w_down: bfloat16 [2, 3072, 1024], P(None, 'fsdp'), may hold values from -0.109375 to 0.109375
- g_attn: bfloat16 [2, 1024], P(None, 'fsdp'), may hold values from 0.5 to 1.5
- g_mlp: bfloat16 [2, 1024], P(None, 'fsdp'), may hold values from 0.5 to 1.5
- g_query: bfloat16 [2, 128], P(None, 'fsdp'), may hold values from 0.099609375 to 1.8984375
- g_key: bfloat16 [2, 128], P(None, 'fsdp'), may hold values from 0.099609375 to 1.8984375
Outputs:
- output: bfloat16 [4096, 1024], P(('ctx', 'fsdp'))
- grad_tokens: float32 [4096, 1024], P(('ctx', 'fsdp'))
- grad_query: float32 [2, 1024, 2048], P(None, ('ctx', 'fsdp'))
- grad_key: float32 [2, 1024, 1024], P(None, ('ctx', 'fsdp'))
- grad_value: float32 [2, 1024, 1024], P(None, ('ctx', 'fsdp'))
- grad_out: float32 [2, 2048, 1024], P(None, ('ctx', 'fsdp'))
- grad_gate: float32 [2, 1024, 3072], P(None, ('ctx', 'fsdp'))
- grad_up: float32 [2, 1024, 3072], P(None, ('ctx', 'fsdp'))
- grad_down: float32 [2, 3072, 1024], P(None, ('ctx', 'fsdp'))
- grad_attn_gain: float32 [2, 1024], P(None, ('ctx', 'fsdp'))
- grad_mlp_gain: float32 [2, 1024], P(None, ('ctx', 'fsdp'))
- grad_query_gain: float32 [2, 128], P(None, ('ctx', 'fsdp'))
- grad_key_gain: float32 [2, 128], P(None, ('ctx', 'fsdp'))
Inputs may be any that keep to these rules, and one draw needn't show every extreme that they name: `lengths`: in each fsdp group at least one of its two slots is full. `stretch_ids`: in each fsdp group every number 0 to 31 occurs once; number s * 16 + j is stretch j of slot s; ctx device c holds two stretches of slot c // 8, numbers j and 15 - j of that slot, the smaller first.
All inputs are finite; a program needn't handle non-finite values.
Results may differ from a plain program's by a relative error of at most 0.033.
Values may be sent and summed in bfloat16 or wider, within the bound.
A program may use at most 384 MiB of HBM per device.

v0:
```python
import math

import jax
import jax.numpy as jnp
from jax import lax
from jax.sharding import PartitionSpec as P

QUERY_HEADS = 16
KEY_VALUE_HEADS = 8
HEAD_SIZE = 128
DECODER_LAYERS = 2
STRETCH = 64


norm_epsilon = 1e-06
rope_base = 1000000.0
masked_logits = -1e30


def from_partner(shard, axis, apart):
    return lax.ppermute(shard, axis, [(i, i ^ 1 << apart) for i in range(lax.axis_size(axis))])


def token_places(stretch_table, slot_lengths):
    ctx_count = stretch_table.shape[0]
    stretch_order = stretch_table.reshape(-1)
    within = jnp.arange(STRETCH, dtype=jnp.int32)
    places = (stretch_order % ctx_count * STRETCH)[:, None] + within[None, :]
    slot_ids = jnp.broadcast_to((stretch_order // ctx_count)[:, None], places.shape).reshape(-1)
    places = places.reshape(-1)
    limits = jnp.where(slot_ids == 0, slot_lengths[0], slot_lengths[1])
    return (places, slot_ids, places < limits)


def rotary_tables(places):
    half_dim = HEAD_SIZE // 2
    spread = jnp.arange(half_dim, dtype=jnp.int32).astype(jnp.float32) * (2.0 / HEAD_SIZE)
    inverse = jnp.exp(spread * -math.log(rope_base))
    angles = places.astype(jnp.float32)[:, None] * inverse[None, :]
    return (
        jnp.concatenate([jnp.cos(angles)] * 2, axis=-1),
        jnp.concatenate([jnp.sin(angles)] * 2, axis=-1),
    )


def rotate(values, cosine_table, sine_table):
    half_dim = values.shape[-1] // 2
    turned = jnp.concatenate([-values[..., half_dim:], values[..., :half_dim]], axis=-1)
    return values * cosine_table[:, None, :] + turned * sine_table[:, None, :]


def unrotate(upstream, cosine_table, sine_table):
    half_dim = upstream.shape[-1] // 2
    scaled_sine = upstream * sine_table[:, None, :]
    turned_back = jnp.concatenate(
        [scaled_sine[..., half_dim:], -scaled_sine[..., :half_dim]], axis=-1
    )
    return upstream * cosine_table[:, None, :] + turned_back


def norm_forward(values, gain_vec):
    scale_inv = lax.rsqrt(jnp.mean(values * values, axis=-1, keepdims=True) + norm_epsilon)
    return (values * scale_inv * gain_vec, scale_inv)


def norm_backward(values, scale_inv, gain_vec, upstream):
    weighted = upstream * gain_vec
    grad_input = scale_inv * weighted - values * scale_inv**3 * jnp.mean(
        weighted * values, axis=-1, keepdims=True
    )
    gain_term = jnp.sum((upstream * values * scale_inv).reshape(-1, values.shape[-1]), axis=0)
    return (grad_input, gain_term)


def upper_bit(local_index, bit_number):
    return local_index // 2**bit_number % 2 == 1


def joined_rows(mine, received, upper_side):
    first_rows = jnp.where(upper_side, received, mine)
    second_rows = jnp.where(upper_side, mine, received)
    return jnp.concatenate([first_rows, second_rows], axis=0)


def half_gather(pair, local_index):
    gathered_rows = pair
    for bit_number in range(lax.axis_size("ctx").bit_length() - 2):
        received = from_partner(gathered_rows, "ctx", bit_number)
        gathered_rows = joined_rows(gathered_rows, received, upper_bit(local_index, bit_number))
    return gathered_rows


def half_reduce(term, local_index):
    for bit_number in reversed(range(lax.axis_size("ctx").bit_length() - 2)):
        span = term.shape[0] // 2
        lower_rows = term[:span]
        upper_rows = term[span:]
        upper_side = upper_bit(local_index, bit_number)
        kept_rows = jnp.where(upper_side, upper_rows, lower_rows)
        sent_rows = jnp.where(upper_side, lower_rows, upper_rows)
        term = kept_rows + from_partner(sent_rows, "ctx", bit_number)
    return term


def over_keys(update, carried, count_rows):
    block_length = math.gcd(count_rows, 512)

    def inner_step(current, block_index):
        return (update(current, block_index * block_length, block_length), None)

    carried, unused = lax.scan(
        inner_step, carried, jnp.arange(count_rows // block_length, dtype=jnp.int32)
    )
    return carried


def allowed_mask(key_meta, query_meta, row_start, block_length):
    key_places = lax.dynamic_slice_in_dim(key_meta[0], row_start, block_length)
    key_slots = lax.dynamic_slice_in_dim(key_meta[1], row_start, block_length)
    key_live = lax.dynamic_slice_in_dim(key_meta[2], row_start, block_length)
    allowed = (
        (key_slots[None, :] == query_meta[1][:, None])
        & (key_places[None, :] <= query_meta[0][:, None])
        & key_live[None, :]
    )
    return allowed[None, None]


def forward_update(
    current, query_head_group, key_tile_block, value_tile_block, allowed, score_scale
):
    running_max, running_sum, running_acc = current
    block_length = key_tile_block.shape[0]
    key_head_list = key_tile_block.reshape(block_length, KEY_VALUE_HEADS, HEAD_SIZE)
    value_head_list = value_tile_block.reshape(block_length, KEY_VALUE_HEADS, HEAD_SIZE)
    scores = (
        jnp.einsum(
            "qhgd,khd->hgqk", query_head_group, key_head_list, preferred_element_type=jnp.float32
        )
        * score_scale
    )
    scores = jnp.where(allowed, scores, masked_logits)
    new_max = jnp.maximum(running_max, jnp.max(scores, axis=-1))
    factor = jnp.exp(running_max - new_max)
    prob_block = jnp.where(allowed, jnp.exp(scores - new_max[..., None]), 0.0)
    new_sum = running_sum * factor + jnp.sum(prob_block, axis=-1)
    new_acc = running_acc * factor[..., None] + jnp.einsum(
        "hgqk,khd->hgqd",
        prob_block.astype(jnp.bfloat16),
        value_head_list,
        preferred_element_type=jnp.float32,
    )
    return (new_max, new_sum, new_acc)


def score_parts(
    query_head_group,
    output_grad_group,
    key_tile_block,
    value_tile_block,
    allowed,
    log_total,
    row_delta,
    score_scale,
):
    block_length = key_tile_block.shape[0]
    key_head_list = key_tile_block.reshape(block_length, KEY_VALUE_HEADS, HEAD_SIZE)
    value_head_list = value_tile_block.reshape(block_length, KEY_VALUE_HEADS, HEAD_SIZE)
    scores = (
        jnp.einsum(
            "qhgd,khd->hgqk", query_head_group, key_head_list, preferred_element_type=jnp.float32
        )
        * score_scale
    )
    prob_block = jnp.where(allowed, jnp.exp(scores - log_total[..., None]), 0.0)
    dprob = jnp.einsum(
        "qhgd,khd->hgqk", output_grad_group, value_head_list, preferred_element_type=jnp.float32
    )
    dscore_low = (prob_block * (dprob - row_delta[..., None])).astype(jnp.bfloat16)
    return (prob_block, dscore_low, key_head_list)


def attention_inputs(stream, gathered, cosine_table, sine_table):
    count_rows = stream.shape[0]
    normalized, inv_attn = norm_forward(stream, gathered[7].astype(jnp.float32))
    normed_low = normalized.astype(jnp.bfloat16)
    query_heads = jnp.dot(normed_low, gathered[0], preferred_element_type=jnp.float32).reshape(
        count_rows, QUERY_HEADS, HEAD_SIZE
    )
    key_head_list = jnp.dot(normed_low, gathered[1], preferred_element_type=jnp.float32).reshape(
        count_rows, KEY_VALUE_HEADS, HEAD_SIZE
    )
    value_low = jnp.dot(normed_low, gathered[2], preferred_element_type=jnp.float32).astype(
        jnp.bfloat16
    )
    query_normed, inv_query = norm_forward(query_heads, gathered[9].astype(jnp.float32))
    key_normed, inv_key = norm_forward(key_head_list, gathered[10].astype(jnp.float32))
    query_lowered = rotate(query_normed, cosine_table, sine_table).astype(jnp.bfloat16)
    key_low = (
        rotate(key_normed, cosine_table, sine_table)
        .astype(jnp.bfloat16)
        .reshape(count_rows, KEY_VALUE_HEADS * HEAD_SIZE)
    )
    return {
        "normed_low": normed_low,
        "inv_attn": inv_attn,
        "query_heads": query_heads,
        "inv_query": inv_query,
        "key_heads": key_head_list,
        "inv_key": inv_key,
        "query_low": query_lowered,
        "key_low": key_low,
        "value_low": value_low,
    }


def block_rest(stream, gathered, attn_low):
    middle = stream + jnp.dot(attn_low, gathered[3], preferred_element_type=jnp.float32)
    normed_mid, inv_mid = norm_forward(middle, gathered[8].astype(jnp.float32))
    normed_mid_low = normed_mid.astype(jnp.bfloat16)
    gate_act = jnp.dot(normed_mid_low, gathered[4], preferred_element_type=jnp.float32)
    upward = jnp.dot(normed_mid_low, gathered[5], preferred_element_type=jnp.float32)
    hidden_low = (jax.nn.silu(gate_act) * upward).astype(jnp.bfloat16)
    result = middle + jnp.dot(hidden_low, gathered[6], preferred_element_type=jnp.float32)
    return {
        "middle": middle,
        "inv_mid": inv_mid,
        "normed_mid_low": normed_mid_low,
        "gate_act": gate_act,
        "upward": upward,
        "hidden_low": hidden_low,
        "result": result,
    }


def per_device(
    tokens,
    cotangent,
    lengths,
    stretch_ids,
    w_query,
    key_projection_weight,
    value_projection_weight,
    w_out,
    w_gate,
    w_up,
    w_down,
    g_attn,
    g_mlp,
    g_query,
    g_key,
):
    count_rows = tokens.shape[0]
    ctx_count = lax.axis_size("ctx")
    half_count = ctx_count // 2
    key_value_width = KEY_VALUE_HEADS * HEAD_SIZE
    key_meta = token_places(stretch_ids[:, 0, :], lengths[0])
    ctx_index = lax.axis_index("ctx")
    local_index = ctx_index % half_count
    base_row = ctx_index // half_count * half_count * count_rows
    half_row_set = half_count * count_rows
    offset_mine = ctx_index * count_rows
    query_meta = tuple(
        (lax.dynamic_slice_in_dim(meta_array, offset_mine, count_rows) for meta_array in key_meta)
    )
    live_mine = query_meta[2].astype(jnp.float32)[:, None]
    cosine_table, sine_table = rotary_tables(query_meta[0])
    group_count = QUERY_HEADS // KEY_VALUE_HEADS
    score_scale = HEAD_SIZE ** (-0.5)

    def attend_forward(query_head_group, key_source, value_source, current):

        def update(carried, local_row, block_length):
            key_tile_block = lax.dynamic_slice_in_dim(key_source, local_row, block_length)
            value_tile_block = lax.dynamic_slice_in_dim(value_source, local_row, block_length)
            allowed = allowed_mask(key_meta, query_meta, base_row + local_row, block_length)
            return forward_update(
                carried, query_head_group, key_tile_block, value_tile_block, allowed, score_scale
            )

        return over_keys(update, current, key_source.shape[0])

    saved = []
    stream = tokens.astype(jnp.float32)
    for layer_index in range(DECODER_LAYERS):
        gathered = (
            lax.all_gather(w_query[layer_index], "fsdp", axis=0, tiled=True),
            lax.all_gather(key_projection_weight[layer_index], "fsdp", axis=0, tiled=True),
            lax.all_gather(value_projection_weight[layer_index], "fsdp", axis=0, tiled=True),
            lax.all_gather(w_out[layer_index], "fsdp", axis=0, tiled=True),
            lax.all_gather(w_gate[layer_index], "fsdp", axis=0, tiled=True),
            lax.all_gather(w_up[layer_index], "fsdp", axis=0, tiled=True),
            lax.all_gather(w_down[layer_index], "fsdp", axis=0, tiled=True),
            lax.all_gather(g_attn[layer_index], "fsdp", axis=0, tiled=True),
            lax.all_gather(g_mlp[layer_index], "fsdp", axis=0, tiled=True),
            lax.all_gather(g_query[layer_index], "fsdp", axis=0, tiled=True),
            lax.all_gather(g_key[layer_index], "fsdp", axis=0, tiled=True),
        )
        present_inputs = attention_inputs(stream, gathered, cosine_table, sine_table)
        query_head_group = present_inputs["query_low"].reshape(
            count_rows, KEY_VALUE_HEADS, group_count, HEAD_SIZE
        )
        start_state = (
            jnp.full((KEY_VALUE_HEADS, group_count, count_rows), masked_logits, jnp.float32),
            jnp.zeros((KEY_VALUE_HEADS, group_count, count_rows), jnp.float32),
            jnp.zeros((KEY_VALUE_HEADS, group_count, count_rows, HEAD_SIZE), jnp.float32),
        )
        pair_all = half_gather(
            jnp.concatenate([present_inputs["key_low"], present_inputs["value_low"]], axis=-1),
            local_index,
        )
        key_all = pair_all[:, :key_value_width]
        value_all = pair_all[:, key_value_width:]
        final_state = attend_forward(query_head_group, key_all, value_all, start_state)
        attended = final_state[2] / final_state[1][..., None]
        log_total = final_state[0] + jnp.log(final_state[1])
        attn_low = (
            jnp.transpose(attended, (2, 0, 1, 3))
            .reshape(count_rows, QUERY_HEADS * HEAD_SIZE)
            .astype(jnp.bfloat16)
        )
        rest = block_rest(stream, gathered, attn_low)
        kept = (gathered, key_all, value_all, present_inputs, rest)
        saved.append((stream, attended, log_total, kept))
        stream = rest["result"]
    output_low = (stream * live_mine).astype(jnp.bfloat16)
    grad_stream = cotangent.astype(jnp.float32) * live_mine
    layer_grads = [None] * DECODER_LAYERS
    for layer_index in reversed(range(DECODER_LAYERS)):
        stream_in, attended, log_total, kept = saved[layer_index]
        attn_low = (
            jnp.transpose(attended, (2, 0, 1, 3))
            .reshape(count_rows, QUERY_HEADS * HEAD_SIZE)
            .astype(jnp.bfloat16)
        )
        gathered, key_all, value_all, present_inputs, rest = kept
        ffn_grad_low = grad_stream.astype(jnp.bfloat16)
        grad_down = jnp.einsum(
            "tf,td->fd", rest["hidden_low"], ffn_grad_low, preferred_element_type=jnp.float32
        )
        hidden_grad = jnp.einsum(
            "td,fd->tf", ffn_grad_low, gathered[6], preferred_element_type=jnp.float32
        )
        gate_act = rest["gate_act"]
        sigmoid_gate = jax.nn.sigmoid(gate_act)
        gate_grad_low = (
            hidden_grad * rest["upward"] * sigmoid_gate * (1.0 + gate_act * (1.0 - sigmoid_gate))
        ).astype(jnp.bfloat16)
        up_grad_low = (hidden_grad * gate_act * sigmoid_gate).astype(jnp.bfloat16)
        grad_gate = jnp.einsum(
            "td,tf->df", rest["normed_mid_low"], gate_grad_low, preferred_element_type=jnp.float32
        )
        grad_up = jnp.einsum(
            "td,tf->df", rest["normed_mid_low"], up_grad_low, preferred_element_type=jnp.float32
        )
        normed_mid_grad = jnp.einsum(
            "tf,df->td", gate_grad_low, gathered[4], preferred_element_type=jnp.float32
        ) + jnp.einsum("tf,df->td", up_grad_low, gathered[5], preferred_element_type=jnp.float32)
        mid_norm_grad, mlp_gain_term = norm_backward(
            rest["middle"], rest["inv_mid"], gathered[8].astype(jnp.float32), normed_mid_grad
        )
        middle_grad = grad_stream + mid_norm_grad
        attn_grad_low = middle_grad.astype(jnp.bfloat16)
        grad_out = jnp.einsum(
            "tq,td->qd", attn_low, attn_grad_low, preferred_element_type=jnp.float32
        )
        output_gradient_lowered = jnp.einsum(
            "td,qd->tq", attn_grad_low, gathered[3], preferred_element_type=jnp.float32
        ).astype(jnp.bfloat16)
        output_grad_group = output_gradient_lowered.reshape(
            count_rows, KEY_VALUE_HEADS, group_count, HEAD_SIZE
        )
        row_delta = jnp.sum(
            jnp.transpose(output_grad_group.astype(jnp.float32), (1, 2, 0, 3)) * attended, axis=-1
        )
        query_head_group = present_inputs["query_low"].reshape(
            count_rows, KEY_VALUE_HEADS, group_count, HEAD_SIZE
        )
        key_block_size = math.gcd(half_row_set, 512)

        def backward_step(query_acc, block_index):
            row_start = block_index * key_block_size
            key_tile_block = lax.dynamic_slice_in_dim(key_all, row_start, key_block_size)
            value_tile_block = lax.dynamic_slice_in_dim(value_all, row_start, key_block_size)
            allowed = allowed_mask(key_meta, query_meta, base_row + row_start, key_block_size)
            prob_block, dscore_low, key_head_list = score_parts(
                query_head_group,
                output_grad_group,
                key_tile_block,
                value_tile_block,
                allowed,
                log_total,
                row_delta,
                score_scale,
            )
            query_next = (query_acc, jnp.zeros((key_block_size, 2 * key_value_width), jnp.float32))[
                0
            ] + jnp.einsum(
                "hgqk,khd->qhgd", dscore_low, key_head_list, preferred_element_type=jnp.float32
            ) * score_scale
            value_grad = jnp.einsum(
                "hgqk,qhgd->khd",
                prob_block.astype(jnp.bfloat16),
                output_grad_group,
                preferred_element_type=jnp.float32,
            )
            key_grad = (
                jnp.einsum(
                    "hgqk,qhgd->khd",
                    dscore_low,
                    query_head_group,
                    preferred_element_type=jnp.float32,
                )
                * score_scale
            )
            block_rows = jnp.concatenate(
                [
                    key_grad.reshape(key_block_size, key_value_width),
                    value_grad.reshape(key_block_size, key_value_width),
                ],
                axis=-1,
            )
            return (query_next, block_rows)

        query_grad, key_value_rows = lax.scan(
            backward_step,
            jnp.zeros((count_rows, KEY_VALUE_HEADS, group_count, HEAD_SIZE), jnp.float32),
            jnp.arange(half_row_set // key_block_size, dtype=jnp.int32),
        )
        key_value_term = key_value_rows.reshape(half_row_set, 2 * key_value_width)
        key_value_gradient = half_reduce(key_value_term, local_index)
        key_gradient_rows = key_value_gradient[:, :key_value_width].reshape(
            count_rows, KEY_VALUE_HEADS, HEAD_SIZE
        )
        value_grad_low = key_value_gradient[:, key_value_width:].astype(jnp.bfloat16)
        query_pre, query_gain_term = norm_backward(
            present_inputs["query_heads"],
            present_inputs["inv_query"],
            gathered[9].astype(jnp.float32),
            unrotate(
                query_grad.reshape(count_rows, QUERY_HEADS, HEAD_SIZE), cosine_table, sine_table
            ),
        )
        key_pre, key_gain_term = norm_backward(
            present_inputs["key_heads"],
            present_inputs["inv_key"],
            gathered[10].astype(jnp.float32),
            unrotate(key_gradient_rows, cosine_table, sine_table),
        )
        query_grad_low = query_pre.reshape(count_rows, QUERY_HEADS * HEAD_SIZE).astype(jnp.bfloat16)
        key_grad_low = key_pre.reshape(count_rows, key_value_width).astype(jnp.bfloat16)
        normed_low = present_inputs["normed_low"]
        grad_query = jnp.einsum(
            "td,tq->dq", normed_low, query_grad_low, preferred_element_type=jnp.float32
        )
        grad_key = jnp.einsum(
            "td,tq->dq", normed_low, key_grad_low, preferred_element_type=jnp.float32
        )
        grad_value = jnp.einsum(
            "td,tq->dq", normed_low, value_grad_low, preferred_element_type=jnp.float32
        )
        normed_grad = jnp.einsum(
            "tq,dq->td", query_grad_low, gathered[0], preferred_element_type=jnp.float32
        )
        normed_grad = normed_grad + jnp.einsum(
            "tq,dq->td", key_grad_low, gathered[1], preferred_element_type=jnp.float32
        )
        normed_grad = normed_grad + jnp.einsum(
            "tq,dq->td", value_grad_low, gathered[2], preferred_element_type=jnp.float32
        )
        in_norm_grad, attn_gain_term = norm_backward(
            stream_in, present_inputs["inv_attn"], gathered[7].astype(jnp.float32), normed_grad
        )
        grad_stream = middle_grad + in_norm_grad
        layer_grads[layer_index] = (
            lax.psum_scatter(grad_query, ("ctx", "fsdp"), scatter_dimension=0, tiled=True),
            lax.psum_scatter(grad_key, ("ctx", "fsdp"), scatter_dimension=0, tiled=True),
            lax.psum_scatter(grad_value, ("ctx", "fsdp"), scatter_dimension=0, tiled=True),
            lax.psum_scatter(grad_out, ("ctx", "fsdp"), scatter_dimension=0, tiled=True),
            lax.psum_scatter(grad_gate, ("ctx", "fsdp"), scatter_dimension=0, tiled=True),
            lax.psum_scatter(grad_up, ("ctx", "fsdp"), scatter_dimension=0, tiled=True),
            lax.psum_scatter(grad_down, ("ctx", "fsdp"), scatter_dimension=0, tiled=True),
            lax.psum_scatter(attn_gain_term, ("ctx", "fsdp"), scatter_dimension=0, tiled=True),
            lax.psum_scatter(mlp_gain_term, ("ctx", "fsdp"), scatter_dimension=0, tiled=True),
            lax.psum_scatter(query_gain_term, ("ctx", "fsdp"), scatter_dimension=0, tiled=True),
            lax.psum_scatter(key_gain_term, ("ctx", "fsdp"), scatter_dimension=0, tiled=True),
        )
    stacked = tuple(
        (jnp.stack([layer_sums[member] for layer_sums in layer_grads]) for member in range(11))
    )
    return (output_low, grad_stream) + stacked


def solution(mesh):
    in_specs = (
        P(("ctx", "fsdp"), None),
        P(("ctx", "fsdp"), None),
        P("fsdp", None),
        P(None, "fsdp", None),
        P(None, "fsdp", None),
        P(None, "fsdp", None),
        P(None, "fsdp", None),
        P(None, "fsdp", None),
        P(None, "fsdp", None),
        P(None, "fsdp", None),
        P(None, "fsdp", None),
        P(None, "fsdp"),
        P(None, "fsdp"),
        P(None, "fsdp"),
        P(None, "fsdp"),
    )
    out_specs = (
        P(("ctx", "fsdp"), None),
        P(("ctx", "fsdp"), None),
        P(None, ("ctx", "fsdp"), None),
        P(None, ("ctx", "fsdp"), None),
        P(None, ("ctx", "fsdp"), None),
        P(None, ("ctx", "fsdp"), None),
        P(None, ("ctx", "fsdp"), None),
        P(None, ("ctx", "fsdp"), None),
        P(None, ("ctx", "fsdp"), None),
        P(None, ("ctx", "fsdp")),
        P(None, ("ctx", "fsdp")),
        P(None, ("ctx", "fsdp")),
        P(None, ("ctx", "fsdp")),
    )
    return jax.shard_map(
        per_device, mesh=mesh, in_specs=in_specs, out_specs=out_specs, check_vma=False
    )
```

profile of v0, /device:TPU:0, one launch (start us, length us, event | category | flops | bytes accessed | tf_op | source)
XLA Modules:
  0.0 3545.0 jit_solution(11401264201152946272)
XLA Ops:
  119.2 20.5 all-gather.41.cloned.1.call-done
  174.1 31.2 while.56
  213.7 65.9 %all-gather.45.cloned.1.call-done = bf16[1,1024,3072]{2,1,0:T(8,128)(2,1)} async-done(((bf16[1,512,3072]{2,1,0:T(8,128)(2,1)}), bf16[1,1024,3072]{2,1,0:T(8,128)(2,1)}) %all-gather.45.cloned.1.call-update) | async-done | bytes 6291472 | tf_op jit(solution)/shard_map/all_gather | solution.py:291
  284.6 76.8 %all-gather.47.cloned.1.call-done = bf16[1,1024,3072]{2,1,0:T(8,128)(2,1)} async-done(((bf16[1,512,3072]{2,1,0:T(8,128)(2,1)}), bf16[1,1024,3072]{2,1,0:T(8,128)(2,1)}) %all-gather.47.cloned.1.call-update) | async-done | bytes 6291472 | tf_op jit(solution)/shard_map/all_gather | solution.py:292
  367.0 76.4 %all-gather.49.cloned.1.call-done = bf16[1,3072,1024]{2,1,0:T(8,128)(2,1)} async-done(((bf16[1,1536,1024]{2,1,0:T(8,128)(2,1)}), bf16[1,3072,1024]{2,1,0:T(8,128)(2,1)}) %all-gather.49.cloned.1.call-update) | async-done | bytes 6291472 | tf_op jit(solution)/shard_map/all_gather | solution.py:293
  448.2 29.9 all-gather.51.cloned.1.call-done
  483.2 29.6 all-gather.53.cloned.1.call-done
  524.3 18.2 collective-permute-done.4
  548.3 22.7 all-gather.55.cloned.1.call-done
  577.8 75.1 %all-gather.63.cloned.1.call-done = bf16[1,3072,1024]{2,1,0:T(8,128)(2,1)} async-done(((bf16[1,1536,1024]{2,1,0:T(8,128)(2,1)}), bf16[1,3072,1024]{2,1,0:T(8,128)(2,1)}) %all-gather.63.cloned.1.call-update) | async-done | bytes 6291472 | tf_op jit(solution)/shard_map/all_gather | solution.py:293
  671.5 33.2 while.57
  714.6 78.5 %all-gather.61.cloned.1.call-done = bf16[1,1024,3072]{2,1,0:T(8,128)(2,1)} async-done(((bf16[1,512,3072]{2,1,0:T(8,128)(2,1)}), bf16[1,1024,3072]{2,1,0:T(8,128)(2,1)}) %all-gather.61.cloned.1.call-update) | async-done | bytes 6291472 | tf_op jit(solution)/shard_map/all_gather | solution.py:292
  798.0 76.9 %all-gather.59.cloned.1.call-done = bf16[1,1024,3072]{2,1,0:T(8,128)(2,1)} async-done(((bf16[1,512,3072]{2,1,0:T(8,128)(2,1)}), bf16[1,1024,3072]{2,1,0:T(8,128)(2,1)}) %all-gather.59.cloned.1.call-update) | async-done | bytes 6291472 | tf_op jit(solution)/shard_map/all_gather | solution.py:291
  898.0 65.4 %while.58 = (s32[]{:T(128)}, f32[128,8,2,128]{0,3,2,1:T(8,128)}, f32[2,512,2048]{2,1,0:T(8,128)}, s32[2]{0:T(128)S(1)}, bf16[1024,1024]{0,1:T(8,128)(2,1)S(1)}, ...) while((s32[]{:T(128)}, f32[128,8,2,128]{0,3,2,1:T(8,128)}, ...), condition=%wide.region_19.20_spmd.clone, body=%wide.region_18.19_spmd.clone.sunk | while | flops 1355284480 | bytes 101948424 | solution.py:425
  969.4 90.8 %collective-permute-done.6 = f32[512,2048]{1,0:T(8,128)S(1)} collective-permute-done((f32[512,2048]{1,0:T(8,128)S(1)}, f32[512,2048]{1,0:T(8,128)S(1)}, u32[]{:S(2)}, u32[]{:S(2)}) %collective-permute-start.6) | collective-permute-done | bytes 4194336 | tf_op jit(solution)/shard_map/ppermute | solution.py:21
  1070.1 42.2 %collective-permute-done.7 = f32[256,2048]{1,0:T(8,128)} collective-permute-done((f32[256,2048]{1,0:T(8,128)}, f32[256,2048]{1,0:T(8,128)}, u32[]{:S(2)}, u32[]{:S(2)}) %collective-permute-start.7) | collective-permute-done | bytes 2097184 | tf_op jit(solution)/shard_map/ppermute | solution.py:21
  1151.4 65.1 %while.59 = (s32[]{:T(128)}, f32[128,8,2,128]{0,3,2,1:T(8,128)}, f32[2,512,2048]{2,1,0:T(8,128)}, s32[2]{0:T(128)S(1)}, bf16[1024,1024]{0,1:T(8,128)(2,1)}, /*in...) while((s32[]{:T(128)}, f32[128,8,2,128]{0,3,2,1:T(8,128)}, ...), condition=%wide.region_26.27_spmd.clone, body=%wide.region_25.26_spmd.clone.sunk | while | flops 1355284480 | bytes 83074112 | solution.py:425
  1227.6 106.1 %collective-permute-done.9 = f32[512,2048]{1,0:T(8,128)} collective-permute-done((f32[512,2048]{1,0:T(8,128)}, f32[512,2048]{1,0:T(8,128)}, u32[]{:S(2)}, u32[]{:S(2)}) %collective-permute-start.9) | collective-permute-done | bytes 4194336 | tf_op jit(solution)/shard_map/ppermute | solution.py:21
  1340.2 52.7 %collective-permute-done.10 = f32[256,2048]{1,0:T(8,128)S(1)} collective-permute-done((f32[256,2048]{1,0:T(8,128)S(1)}, f32[256,2048]{1,0:T(8,128)S(1)}, u32[]{:S(2)}, u32[]{:S(2)}) %collective-permute-start.10) | collective-permute-done | bytes 2097184 | tf_op jit(solution)/shard_map/ppermute | solution.py:21
  1531.6 38.6 %all-reduce.12 = (f32[1024]{0:T(1024)S(1)}, f32[1024]{0:T(1024)S(1)}, f32[1024]{0:T(1024)S(1)}, f32[1024]{0:T(1024)S(1)}, f32[128]{0:T(128)S(1)}, /*index=5*/f32[128]{0:T(128)S(1)}, f32[128]{0:T(128)S(1)}, f32[128]{0:T(128)S(1)}) all-reduce(f32[1024]{0:T(1024)S(1)} %copy-done.179, ...), channel_id=39, replica_groups=mesh['ctx'=16,'fsdp'=2] {'ctx','fsdp'}, use_global_device_ids=true, to_apply=%region_47.48.clone | all-reduce | flops 4608 | bytes 36864
  1575.6 110.4 %reduce-scatter.25.cloned.1.call-done = f32[32,1024]{1,0:T(8,128)} async-done(((f32[1024,1024]{1,0:T(8,128)}), f32[32,1024]{1,0:T(8,128)}) %reduce-scatter.25.cloned.1.call-update) | async-done | bytes 131088 | tf_op jit(solution)/shard_map/reduce_scatter | solution.py:478
  1686.0 140.9 %reduce-scatter.23.cloned.1.call-done = f32[32,1024]{1,0:T(8,128)} async-done(((f32[1024,1024]{1,0:T(8,128)}), f32[32,1024]{1,0:T(8,128)}) %reduce-scatter.23.cloned.1.call-update) | async-done | bytes 131088 | tf_op jit(solution)/shard_map/reduce_scatter | solution.py:478
  1828.5 180.6 %reduce-scatter.29.cloned.1.call-done = f32[64,1024]{1,0:T(8,128)} async-done(((f32[2048,1024]{1,0:T(8,128)}), f32[64,1024]{1,0:T(8,128)}) %reduce-scatter.29.cloned.1.call-update) | async-done | bytes 262160 | tf_op jit(solution)/shard_map/reduce_scatter | solution.py:479
  2009.1 186.2 %reduce-scatter.27.cloned.1.call-done = f32[64,1024]{1,0:T(8,128)} async-done(((f32[2048,1024]{1,0:T(8,128)}), f32[64,1024]{1,0:T(8,128)}) %reduce-scatter.27.cloned.1.call-update) | async-done | bytes 262160 | tf_op jit(solution)/shard_map/reduce_scatter | solution.py:479
  2197.1 184.5 %reduce-scatter.17.cloned.1.call-done = f32[32,2048]{1,0:T(8,128)} async-done(((f32[1024,2048]{1,0:T(8,128)}), f32[32,2048]{1,0:T(8,128)}) %reduce-scatter.17.cloned.1.call-update) | async-done | bytes 262160 | tf_op jit(solution)/shard_map/reduce_scatter | solution.py:476
  2381.7 186.4 %reduce-scatter.15.cloned.1.call-done = f32[32,2048]{1,0:T(8,128)} async-done(((f32[1024,2048]{1,0:T(8,128)}), f32[32,2048]{1,0:T(8,128)}) %reduce-scatter.15.cloned.1.call-update) | async-done | bytes 262160 | tf_op jit(solution)/shard_map/reduce_scatter | solution.py:476
  2569.9 160.5 %reduce-scatter.33.cloned.1.call-done = f32[32,3072]{1,0:T(8,128)} async-done(((f32[1024,3072]{1,0:T(8,128)}), f32[32,3072]{1,0:T(8,128)}) %reduce-scatter.33.cloned.1.call-update) | async-done | bytes 393232 | tf_op jit(solution)/shard_map/reduce_scatter | solution.py:480
  2730.4 161.5 %reduce-scatter.31.cloned.1.call-done = f32[32,3072]{1,0:T(8,128)} async-done(((f32[1024,3072]{1,0:T(8,128)}), f32[32,3072]{1,0:T(8,128)}) %reduce-scatter.31.cloned.1.call-update) | async-done | bytes 393232 | tf_op jit(solution)/shard_map/reduce_scatter | solution.py:480
  2894.0 158.5 %reduce-scatter.37.cloned.1.call-done = f32[32,3072]{1,0:T(8,128)} async-done(((f32[1024,3072]{1,0:T(8,128)}), f32[32,3072]{1,0:T(8,128)}) %reduce-scatter.37.cloned.1.call-update) | async-done | bytes 393232 | tf_op jit(solution)/shard_map/reduce_scatter | solution.py:481
  3052.5 161.4 %reduce-scatter.35.cloned.1.call-done = f32[32,3072]{1,0:T(8,128)} async-done(((f32[1024,3072]{1,0:T(8,128)}), f32[32,3072]{1,0:T(8,128)}) %reduce-scatter.35.cloned.1.call-update) | async-done | bytes 393232 | tf_op jit(solution)/shard_map/reduce_scatter | solution.py:481
  3216.0 158.3 %reduce-scatter.41.cloned.1.call-done = f32[96,1024]{1,0:T(8,128)} async-done(((f32[3072,1024]{1,0:T(8,128)}), f32[96,1024]{1,0:T(8,128)}) %reduce-scatter.41.cloned.1.call-update) | async-done | bytes 393232 | tf_op jit(solution)/shard_map/reduce_scatter | solution.py:482
  3374.3 161.6 %reduce-scatter.39.cloned.1.call-done = f32[96,1024]{1,0:T(8,128)} async-done(((f32[3072,1024]{1,0:T(8,128)}), f32[96,1024]{1,0:T(8,128)}) %reduce-scatter.39.cloned.1.call-update) | async-done | bytes 393232 | tf_op jit(solution)/shard_map/reduce_scatter | solution.py:482
  (947 shorter events, 668.3 us)
Async XLA Ops:
  7.2 53.6 %all-gather.37.cloned.1.call-start = ((), (), s32[]{:S(2)}) async-start(), calls=%async_computation.28 | async-start | bytes 3145728 | tf_op jit(solution)/shard_map/all_gather | solution.py:288
  10.4 70.7 %all-gather.39.cloned.1.call-start = ((), (), s32[]{:S(2)}) async-start(), calls=%async_computation.29 | async-start | bytes 3145728 | tf_op jit(solution)/shard_map/all_gather | solution.py:289
  12.0 127.6 %all-gather.41.cloned.1.call-start = ((), (), s32[]{:S(2)}) async-start(), calls=%async_computation.30 | async-start | bytes 6291456 | tf_op jit(solution)/shard_map/all_gather | solution.py:287
  17.0 192.4 %all-gather.43.cloned.1.call-start = ((), (), s32[]{:S(2)}) async-start(), calls=%async_computation.31 | async-start | bytes 6291456 | tf_op jit(solution)/shard_map/all_gather | solution.py:290
  21.9 257.8 %all-gather.45.cloned.1.call-start = ((), (), s32[]{:S(2)}) async-start(), calls=%async_computation.32 | async-start | bytes 9437184 | tf_op jit(solution)/shard_map/all_gather | solution.py:291
  28.1 333.4 %all-gather.47.cloned.1.call-start = ((), (), s32[]{:S(2)}) async-start(), calls=%async_computation.33 | async-start | bytes 9437184 | tf_op jit(solution)/shard_map/all_gather | solution.py:292
  34.0 409.4 %all-gather.49.cloned.1.call-start = ((), (), s32[]{:S(2)}) async-start(), calls=%async_computation.34 | async-start | bytes 9437184 | tf_op jit(solution)/shard_map/all_gather | solution.py:293
  40.3 437.8 %all-gather.51.cloned.1.call-start = ((), (), s32[]{:S(2)}) async-start(), calls=%async_computation.35 | async-start | bytes 3145728 | tf_op jit(solution)/shard_map/all_gather | solution.py:288
  41.0 471.8 %all-gather.53.cloned.1.call-start = ((), (), s32[]{:S(2)}) async-start(), calls=%async_computation.36 | async-start | bytes 3145728 | tf_op jit(solution)/shard_map/all_gather | solution.py:289
  41.8 529.2 %all-gather.55.cloned.1.call-start = ((), (), s32[]{:S(2)}) async-start(), calls=%async_computation.37 | async-start | bytes 6291456 | tf_op jit(solution)/shard_map/all_gather | solution.py:287
  42.4 610.6 %all-gather.63.cloned.1.call-start = ((), (), s32[]{:S(2)}) async-start(), calls=%async_computation.41 | async-start | bytes 9437184 | tf_op jit(solution)/shard_map/all_gather | solution.py:293
  43.1 668.0 %all-gather.57.cloned.1.call-start = ((), (), s32[]{:S(2)}) async-start(), calls=%async_computation.38 | async-start | bytes 6291456 | tf_op jit(solution)/shard_map/all_gather | solution.py:290
  43.7 749.4 %all-gather.61.cloned.1.call-start = ((), (), s32[]{:S(2)}) async-start(), calls=%async_computation.40 | async-start | bytes 9437184 | tf_op jit(solution)/shard_map/all_gather | solution.py:292
  87.2 787.7 %all-gather.59.cloned.1.call-start = ((), (), s32[]{:S(2)}) async-start(), calls=%async_computation.39 | async-start | bytes 9437184 | tf_op jit(solution)/shard_map/all_gather | solution.py:291
  518.8 1055.1 %reduce-scatter.21.cloned.1.call-start = ((), (), s32[]{:S(2)}) async-start(), calls=%async_computation.17 | async-start | bytes 4325376 | tf_op jit(solution)/shard_map/reduce_scatter | solution.py:477
  545.5 113.7 %collective-permute-start.5 = (bf16[512,2048]{1,0:T(8,128)(2,1)}, bf16[512,2048]{1,0:T(8,128)(2,1)}, u32[]{:S(2)}, u32[]{:S(2)}) collective-permute-start(bf16[512,2048]{1,0:T(8,128)(2,1)} %pad_maximum_fusion.3), channel_id=1, source_target_pairs={{0,8},{2,10},{4,12},{6,14},{8,0},{10,2},{12,4},{14,6},{16,24},{18,... | collective-permute-start | bytes 6291464 | tf_op jit(solution)/shard_map/ppermute | solution.py:21
  967.8 92.4 %collective-permute-start.6 = (f32[512,2048]{1,0:T(8,128)S(1)}, f32[512,2048]{1,0:T(8,128)S(1)}, u32[]{:S(2)}, u32[]{:S(2)}) collective-permute-start(f32[512,2048]{1,0:T(8,128)S(1)} %select_bitcast_fusion.1), channel_id=1, source_target_pairs={{0,8},{2,10},{4,12},{6,14},{8,0},{10,2},{12,4},{14,6},{16,24},{18,... | collective-permute-start | bytes 12582920 | tf_op jit(solution)/shard_map/ppermute | solution.py:21
  1223.1 110.7 %collective-permute-start.9 = (f32[512,2048]{1,0:T(8,128)}, f32[512,2048]{1,0:T(8,128)}, u32[]{:S(2)}, u32[]{:S(2)}) collective-permute-start(f32[512,2048]{1,0:T(8,128)} %select_bitcast_fusion), channel_id=1, source_target_pairs={{0,8},{2,10},{4,12},{6,14},{8,0},{10,2},{12,4},{14,6},{16,24},{18,... | collective-permute-start | bytes 12582920 | tf_op jit(solution)/shard_map/ppermute | solution.py:21
  1227.4 346.5 %reduce-scatter.19.cloned.1.call-start = ((), (), s32[]{:S(2)}) async-start(), calls=%async_computation.16 | async-start | bytes 4325376 | tf_op jit(solution)/shard_map/reduce_scatter | solution.py:477
  1340.1 52.8 %collective-permute-start.10 = (f32[256,2048]{1,0:T(8,128)S(1)}, f32[256,2048]{1,0:T(8,128)S(1)}, u32[]{:S(2)}, u32[]{:S(2)}) collective-permute-start(f32[256,2048]{1,0:T(8,128)S(1)} %slice_select_fusion), channel_id=1, source_target_pairs={{0,4},{2,6},{4,0},{6,2},{8,12},{10,14},{12,8},{14,10},{16,20},{18,... | collective-permute-start | bytes 6291464 | tf_op jit(solution)/shard_map/ppermute | solution.py:21
  1403.2 282.8 %reduce-scatter.25.cloned.1.call-start = ((), (), s32[]{:S(2)}) async-start(), calls=%async_computation.19 | async-start | bytes 4325376 | tf_op jit(solution)/shard_map/reduce_scatter | solution.py:478
  1406.0 420.9 %reduce-scatter.23.cloned.1.call-start = ((), (), s32[]{:S(2)}) async-start(), calls=%async_computation.18 | async-start | bytes 4325376 | tf_op jit(solution)/shard_map/reduce_scatter | solution.py:478
  1408.9 600.2 %reduce-scatter.29.cloned.1.call-start = ((), (), s32[]{:S(2)}) async-start(), calls=%async_computation.21 | async-start | bytes 8650752 | tf_op jit(solution)/shard_map/reduce_scatter | solution.py:479
  1413.5 781.8 %reduce-scatter.27.cloned.1.call-start = ((), (), s32[]{:S(2)}) async-start(), calls=%async_computation.20 | async-start | bytes 8650752 | tf_op jit(solution)/shard_map/reduce_scatter | solution.py:479
  1419.2 962.5 %reduce-scatter.17.cloned.1.call-start = ((), (), s32[]{:S(2)}) async-start(), calls=%async_computation.15 | async-start | bytes 8650752 | tf_op jit(solution)/shard_map/reduce_scatter | solution.py:476
  1424.7 1143.4 %reduce-scatter.15.cloned.1.call-start = ((), (), s32[]{:S(2)}) async-start(), calls=%async_computation.14 | async-start | bytes 8650752 | tf_op jit(solution)/shard_map/reduce_scatter | solution.py:476
  1444.7 1285.7 %reduce-scatter.33.cloned.1.call-start = ((), (), s32[]{:S(2)}) async-start(), calls=%async_computation.23 | async-start | bytes 12976128 | tf_op jit(solution)/shard_map/reduce_scatter | solution.py:480
  1453.1 1438.8 %reduce-scatter.31.cloned.1.call-start = ((), (), s32[]{:S(2)}) async-start(), calls=%async_computation.22 | async-start | bytes 12976128 | tf_op jit(solution)/shard_map/reduce_scatter | solution.py:480
  1461.5 1591.0 %reduce-scatter.37.cloned.1.call-start = ((), (), s32[]{:S(2)}) async-start(), calls=%async_computation.25 | async-start | bytes 12976128 | tf_op jit(solution)/shard_map/reduce_scatter | solution.py:481
  1469.0 1744.9 %reduce-scatter.35.cloned.1.call-start = ((), (), s32[]{:S(2)}) async-start(), calls=%async_computation.24 | async-start | bytes 12976128 | tf_op jit(solution)/shard_map/reduce_scatter | solution.py:481
  1476.5 1897.8 %reduce-scatter.41.cloned.1.call-start = ((), (), s32[]{:S(2)}) async-start(), calls=%async_computation.27 | async-start | bytes 12976128 | tf_op jit(solution)/shard_map/reduce_scatter | solution.py:482
  1484.1 2051.8 %reduce-scatter.39.cloned.1.call-start = ((), (), s32[]{:S(2)}) async-start(), calls=%async_computation.26 | async-start | bytes 12976128 | tf_op jit(solution)/shard_map/reduce_scatter | solution.py:482
  (247 other events, 3498.3 us)
Sparse Core Ops, SparseCore 0:
  10.6 35.8 all-gather.36
  48.0 33.1 all-gather.38
  82.7 56.9 all-gather.40
  141.1 56.7 all-gather.42
  199.2 80.3 all-gather.44
  281.0 80.3 all-gather.46
  363.0 80.3 all-gather.48
  444.9 33.1 all-gather.50
  479.6 33.1 all-gather.52
  514.2 56.7 all-gather.54
  572.5 80.3 all-gather.62
  654.3 56.7 all-gather.56
  712.7 80.3 all-gather.60
  794.5 80.3 all-gather.58
  1227.5 150.0 reduce-scatter.20
  1403.3 141.5 reduce-scatter.18
  1547.0 138.9 reduce-scatter.24
  1688.1 138.6 reduce-scatter.22
  1829.1 179.9 reduce-scatter.28
  2011.2 183.9 reduce-scatter.26
  2197.6 184.0 reduce-scatter.16
  2384.0 184.0 reduce-scatter.14
  2574.1 156.2 reduce-scatter.32
  2737.4 154.5 reduce-scatter.30
  2897.9 154.4 reduce-scatter.36
  3059.4 154.4 reduce-scatter.34
  3219.8 154.4 reduce-scatter.40
  3381.3 154.5 reduce-scatter.38
where the time goes:
time: 3560 us; the launch traced here: 3540 us
  waiting for transfers between devices  2860 us (80%)
  matrix products  231 us (6%)
  local copies, waits for them, and re-layouts  219 us (6%)
  other arithmetic  134 us (4%)
  blocking collectives  63.1 us (2%)
    reduce_scatter x2, waiting for transfers between devices, per_device(): lax.psum_scatter(grad_query, ('ctx', 'fsdp'), scatter_dimension=0, tiled=...  371 us
    reduce_scatter x2, waiting for transfers between devices, per_device(): lax.psum_scatter(grad_out, ('ctx', 'fsdp'), scatter_dimension=0, tiled=True)  367 us
    ppermute x12, waiting for transfers between devices, from_partner(): lax.ppermute(shard, axis, [(i, i ^ 1 << apart) for i in range(lax.axis_si...  337 us
    reduce_scatter x2, waiting for transfers between devices, per_device(): lax.psum_scatter(grad_gate, ('ctx', 'fsdp'), scatter_dimension=0, tiled=T...  322 us
    reduce_scatter x2, waiting for transfers between devices, per_device(): lax.psum_scatter(grad_up, ('ctx', 'fsdp'), scatter_dimension=0, tiled=True)  320 us
    reduce_scatter x2, waiting for transfers between devices, per_device(): lax.psum_scatter(grad_down, ('ctx', 'fsdp'), scatter_dimension=0, tiled=T...  320 us
    reduce_scatter x2, waiting for transfers between devices, per_device(): lax.psum_scatter(grad_value, ('ctx', 'fsdp'), scatter_dimension=0, tiled=...  251 us
    all_gather x2, waiting for transfers between devices, per_device(): lax.all_gather(w_up[layer_index], 'fsdp', axis=0, tiled=True)  155 us
  transfers between devices with their start and end apart: 40, of which 34 were waited for; matrix products, arithmetic and copies ran while one was open for 10% of the time, Pallas kernels for 0%

commit v1 on v0

--- a/solution.py
+++ b/solution.py
@@ -3,6 +3,8 @@
 import jax
 import jax.numpy as jnp
 from jax import lax
+from jax.experimental import pallas as pl
+from jax.experimental.pallas import tpu as pltpu
 from jax.sharding import PartitionSpec as P
 
 QUERY_HEADS = 16
@@ -15,6 +17,297 @@
 norm_epsilon = 1e-06
 rope_base = 1000000.0
 masked_logits = -1e30
+
+MESH = pl.DeviceIdType.MESH
+TILES = 15
+GRADS = 12
+AHEAD = 3
+
+
+def grad_index(t):
+    return jnp.maximum(t - 3, jnp.where(t < 3, 0, 1))
+
+
+def act_index(t):
+    return jnp.minimum(t, 5) + jnp.where(t >= 11, 1, 0)
+
+
+def is_new(t):
+    return (t == 0) | (t == 3) | ((t >= 5) & (t < TILES))
+
+
+def rs_kernel(
+    acts, grads, out, abuf, afwd, gbuf, ysend, yrecv, own, zsend, zrecv, zown,
+    a_local, a_xs, a_xr, a_cs, a_cr, g_local, g_xs, g_xr, g_cs, g_cr, g_fs, g_fr,
+    y_s, y_r, z_s, z_r,
+):
+    c = lax.axis_index("ctx")
+    x = lax.axis_index("fsdp")
+    core = c % 2
+    y = c // 2 % 2
+    z = c // 4
+    sibling = (c + 1 - 2 * core, x)
+    across = (c, 1 - x)
+    aside = (c + 2 - 4 * y, x)
+
+    def along(o):
+        return ((z + o) % 4 * 4 + c % 4, x)
+
+    barrier = pltpu.get_barrier_semaphore()
+    for other in (sibling, across, aside, along(1), along(2), along(3)):
+        pl.semaphore_signal(barrier, inc=1, device_id=other, device_id_type=MESH)
+    pl.semaphore_wait(barrier, 6)
+
+    def remote(src, dst, s, r, dev):
+        return pltpu.make_async_remote_copy(
+            src_ref=src, dst_ref=dst, send_sem=s, recv_sem=r, device_id=dev, device_id_type=MESH
+        )
+
+    spans = (pl.ds(0, 3), pl.ds(3, 4))
+
+    def act_local(g):
+        return pltpu.make_async_copy(
+            acts.at[x, core, spans[g]], abuf.at[spans[g], :, pl.ds(0, 128)], a_local.at[g]
+        )
+
+    def act_across(g):
+        return (
+            remote(
+                acts.at[1 - x, core, spans[g]], abuf.at[spans[g], :, pl.ds(128, 128)],
+                a_xs.at[g, 0], a_xr.at[g, 0], across,
+            ),
+            remote(
+                acts.at[1 - x, 1 - core, spans[g]], afwd.at[spans[g]],
+                a_xs.at[g, 1], a_xr.at[g, 1], across,
+            ),
+        )
+
+    def act_sibling(g):
+        return remote(
+            acts.at[x, 1 - core, spans[g]], abuf.at[spans[g], :, pl.ds(256, 128)],
+            a_cs.at[g, 0], a_cr.at[g, 0], sibling,
+        )
+
+    def act_forward(g):
+        return remote(
+            afwd.at[spans[g]], abuf.at[spans[g], :, pl.ds(384, 128)],
+            a_cs.at[g, 1], a_cr.at[g, 1], sibling,
+        )
+
+    def grad_local(i):
+        return pltpu.make_async_copy(grads.at[i], gbuf.at[i, pl.ds(0, 128)], g_local.at[i])
+
+    def grad_across(i):
+        return remote(grads.at[i], gbuf.at[i, pl.ds(128, 128)], g_xs.at[i], g_xr.at[i], across)
+
+    def grad_sibling(i):
+        return remote(grads.at[i], gbuf.at[i, pl.ds(256, 128)], g_cs.at[i], g_cr.at[i], sibling)
+
+    def grad_forward(i):
+        return remote(
+            gbuf.at[i, pl.ds(128, 128)], gbuf.at[i, pl.ds(384, 128)], g_fs.at[i], g_fr.at[i], sibling
+        )
+
+    def y_copy(t):
+        return remote(ysend.at[t], yrecv.at[t], y_s.at[t], y_r.at[t], aside)
+
+    def z_copy(t, o):
+        return remote(
+            zsend.at[t, o - 1], zrecv.at[t, 3 - o], z_s.at[t, o - 1], z_r.at[t, 3 - o], along(o)
+        )
+
+    def start_acts(g):
+        for copy in act_across(g):
+            copy.start()
+        act_sibling(g).start()
+        act_local(g).start()
+
+    def start_grad(i):
+        grad_across(i).start()
+        grad_sibling(i).start()
+        grad_local(i).start()
+
+    start_acts(0)
+    start_grad(0)
+    start_acts(1)
+    for i in range(1, AHEAD):
+        start_grad(i)
+
+    def forward_acts(g):
+        act_across(g)[1].wait_recv()
+        act_forward(g).start()
+
+    def await_acts(g):
+        act_local(g).wait()
+        act_across(g)[0].wait_recv()
+        act_sibling(g).wait_recv()
+        act_forward(g).wait_recv()
+
+    def step(s, carry):
+        t = s - 5
+
+        @pl.when(t >= 0)
+        def finish():
+            total = zown[t % 4]
+            for o in (1, 2, 3):
+                z_copy(t, o).wait_recv()
+            for o in range(3):
+                total += zrecv[t, o].astype(jnp.float32)
+            out[t] = total
+
+        u = s - 3
+
+        @pl.when((u >= 0) & (u < TILES))
+        def spread():
+            y_copy(u).wait_recv()
+
+            def part(index):
+                rows = pl.ds(pl.multiple_of(index * 32, 32), 32)
+                return own[u % 4, rows, :] + yrecv[u, rows, :].astype(jnp.float32)
+
+            for o in (2, 1, 3):
+                zsend[u, o - 1] = part((z + o) % 4).astype(jnp.bfloat16)
+                z_copy(u, o).start()
+            zown[u % 4] = part(z)
+
+        v = s - 1
+
+        @pl.when((v >= 0) & (v < TILES))
+        def compute():
+            gi = grad_index(v)
+            ai = act_index(v)
+
+            @pl.when(v == 0)
+            def first_acts():
+                await_acts(0)
+
+            @pl.when(v == 3)
+            def second_acts():
+                await_acts(1)
+
+            @pl.when(is_new(v))
+            def fresh():
+                grad_local(gi).wait()
+                grad_sibling(gi).wait_recv()
+                grad_forward(gi).wait_recv()
+
+            for half in range(2):
+                cols = pl.ds(half * 512, 512)
+                right = gbuf[gi, :, cols]
+                theirs = pl.ds(pl.multiple_of((1 - y) * 128, 128), 128)
+                mine = pl.ds(pl.multiple_of(y * 128, 128), 128)
+                ysend[v, :, cols] = jnp.dot(
+                    abuf[ai, theirs, :], right, preferred_element_type=jnp.float32
+                ).astype(jnp.bfloat16)
+                own[v % 4, :, cols] = jnp.dot(
+                    abuf[ai, mine, :], right, preferred_element_type=jnp.float32
+                )
+            y_copy(v).start()
+
+        @pl.when(is_new(s))
+        def forward():
+            i = grad_index(s)
+
+            @pl.when(s == 0)
+            def first_forward():
+                forward_acts(0)
+
+            @pl.when(s == 3)
+            def second_forward():
+                forward_acts(1)
+
+            grad_across(i).wait_recv()
+            grad_forward(i).start()
+
+            @pl.when(i + AHEAD < GRADS)
+            def more():
+                start_grad(i + AHEAD)
+
+        return carry
+
+    lax.fori_loop(0, TILES + 5, step, 0)
+
+    for g in range(2):
+        for copy in act_across(g):
+            copy.wait_send()
+        act_sibling(g).wait_send()
+        act_forward(g).wait_send()
+
+    def drain_grads(i, carry):
+        grad_across(i).wait_send()
+        grad_sibling(i).wait_send()
+        grad_forward(i).wait_send()
+        return carry
+
+    lax.fori_loop(0, GRADS, drain_grads, 0)
+
+    def drain_tiles(t, carry):
+        y_copy(t).wait_send()
+        for o in (1, 2, 3):
+            z_copy(t, o).wait_send()
+        return carry
+
+    lax.fori_loop(0, TILES, drain_tiles, 0)
+
+
+def reduce_layer(acts, grads, collective_id):
+    dma = pltpu.SemaphoreType.DMA
+    low, wide = jnp.bfloat16, jnp.float32
+    return pl.pallas_call(
+        rs_kernel,
+        out_shape=jax.ShapeDtypeStruct((TILES, 32, 1024), wide),
+        in_specs=[pl.BlockSpec(memory_space=pl.ANY)] * 2,
+        out_specs=pl.BlockSpec(memory_space=pltpu.VMEM),
+        scratch_shapes=[
+            pltpu.VMEM((7, 256, 512), low),
+            pltpu.VMEM((7, 256, 128), low),
+            pltpu.VMEM((GRADS, 512, 1024), low),
+            pltpu.VMEM((TILES, 128, 1024), low),
+            pltpu.VMEM((TILES, 128, 1024), low),
+            pltpu.VMEM((4, 128, 1024), wide),
+            pltpu.VMEM((TILES, 3, 32, 1024), low),
+            pltpu.VMEM((TILES, 3, 32, 1024), low),
+            pltpu.VMEM((4, 32, 1024), wide),
+            dma((2,)), dma((2, 2)), dma((2, 2)), dma((2, 2)), dma((2, 2)),
+            dma((GRADS,)), dma((GRADS,)), dma((GRADS,)), dma((GRADS,)), dma((GRADS,)),
+            dma((GRADS,)), dma((GRADS,)),
+            dma((TILES,)), dma((TILES,)), dma((TILES, 3)), dma((TILES, 3)),
+        ],
+        compiler_params=pltpu.CompilerParams(
+            collective_id=collective_id, has_side_effects=True, vmem_limit_bytes=48 * 2**20
+        ),
+        name="weight_gradient_reduce",
+    )(acts, grads)
+
+
+def act_blocks(values):
+    turned = values.T.reshape(4, 2, 2, 2, -1, 32, values.shape[0])
+    return turned.transpose(3, 2, 4, 1, 0, 5, 6).reshape(2, 2, -1, 256, values.shape[0])
+
+
+def grad_blocks(values):
+    return values.reshape(values.shape[0], -1, 1024).transpose(1, 0, 2)
+
+
+def side_by_side(tiles):
+    return tiles.transpose(1, 0, 2).reshape(tiles.shape[1], -1)
+
+
+def reduce_weights(acts, grads, collective_id):
+    tiles = reduce_layer(
+        jnp.concatenate([act_blocks(member) for member in acts], axis=2),
+        jnp.concatenate([grad_blocks(member) for member in grads], axis=0),
+        collective_id,
+    )
+    return (
+        side_by_side(tiles[11:13]),
+        tiles[13],
+        tiles[14],
+        tiles[3:5].reshape(64, 1024),
+        side_by_side(tiles[5:8]),
+        side_by_side(tiles[8:11]),
+        tiles[0:3].reshape(96, 1024),
+    )
 
 
 def from_partner(shard, axis, apart):
@@ -335,9 +628,6 @@
         )
         gathered, key_all, value_all, present_inputs, rest = kept
         ffn_grad_low = grad_stream.astype(jnp.bfloat16)
-        grad_down = jnp.einsum(
-            "tf,td->fd", rest["hidden_low"], ffn_grad_low, preferred_element_type=jnp.float32
-        )
         hidden_grad = jnp.einsum(
             "td,fd->tf", ffn_grad_low, gathered[6], preferred_element_type=jnp.float32
         )
@@ -347,12 +637,6 @@
             hidden_grad * rest["upward"] * sigmoid_gate * (1.0 + gate_act * (1.0 - sigmoid_gate))
         ).astype(jnp.bfloat16)
         up_grad_low = (hidden_grad * gate_act * sigmoid_gate).astype(jnp.bfloat16)
-        grad_gate = jnp.einsum(
-            "td,tf->df", rest["normed_mid_low"], gate_grad_low, preferred_element_type=jnp.float32
-        )
-        grad_up = jnp.einsum(
-            "td,tf->df", rest["normed_mid_low"], up_grad_low, preferred_element_type=jnp.float32
-        )
         normed_mid_grad = jnp.einsum(
             "tf,df->td", gate_grad_low, gathered[4], preferred_element_type=jnp.float32
         ) + jnp.einsum("tf,df->td", up_grad_low, gathered[5], preferred_element_type=jnp.float32)
@@ -361,9 +645,6 @@
         )
         middle_grad = grad_stream + mid_norm_grad
         attn_grad_low = middle_grad.astype(jnp.bfloat16)
-        grad_out = jnp.einsum(
-            "tq,td->qd", attn_low, attn_grad_low, preferred_element_type=jnp.float32
-        )
         output_gradient_lowered = jnp.einsum(
             "td,qd->tq", attn_grad_low, gathered[3], preferred_element_type=jnp.float32
         ).astype(jnp.bfloat16)
@@ -450,15 +731,6 @@
         query_grad_low = query_pre.reshape(count_rows, QUERY_HEADS * HEAD_SIZE).astype(jnp.bfloat16)
         key_grad_low = key_pre.reshape(count_rows, key_value_width).astype(jnp.bfloat16)
         normed_low = present_inputs["normed_low"]
-        grad_query = jnp.einsum(
-            "td,tq->dq", normed_low, query_grad_low, preferred_element_type=jnp.float32
-        )
-        grad_key = jnp.einsum(
-            "td,tq->dq", normed_low, key_grad_low, preferred_element_type=jnp.float32
-        )
-        grad_value = jnp.einsum(
-            "td,tq->dq", normed_low, value_grad_low, preferred_element_type=jnp.float32
-        )
         normed_grad = jnp.einsum(
             "tq,dq->td", query_grad_low, gathered[0], preferred_element_type=jnp.float32
         )
@@ -472,19 +744,47 @@
             stream_in, present_inputs["inv_attn"], gathered[7].astype(jnp.float32), normed_grad
         )
         grad_stream = middle_grad + in_norm_grad
-        layer_grads[layer_index] = (
-            lax.psum_scatter(grad_query, ("ctx", "fsdp"), scatter_dimension=0, tiled=True),
-            lax.psum_scatter(grad_key, ("ctx", "fsdp"), scatter_dimension=0, tiled=True),
-            lax.psum_scatter(grad_value, ("ctx", "fsdp"), scatter_dimension=0, tiled=True),
-            lax.psum_scatter(grad_out, ("ctx", "fsdp"), scatter_dimension=0, tiled=True),
-            lax.psum_scatter(grad_gate, ("ctx", "fsdp"), scatter_dimension=0, tiled=True),
-            lax.psum_scatter(grad_up, ("ctx", "fsdp"), scatter_dimension=0, tiled=True),
-            lax.psum_scatter(grad_down, ("ctx", "fsdp"), scatter_dimension=0, tiled=True),
-            lax.psum_scatter(attn_gain_term, ("ctx", "fsdp"), scatter_dimension=0, tiled=True),
-            lax.psum_scatter(mlp_gain_term, ("ctx", "fsdp"), scatter_dimension=0, tiled=True),
-            lax.psum_scatter(query_gain_term, ("ctx", "fsdp"), scatter_dimension=0, tiled=True),
-            lax.psum_scatter(key_gain_term, ("ctx", "fsdp"), scatter_dimension=0, tiled=True),
-        )
+        gain_sums = tuple(
+            (
+                lax.psum_scatter(term, ("ctx", "fsdp"), scatter_dimension=0, tiled=True)
+                for term in (attn_gain_term, mlp_gain_term, query_gain_term, key_gain_term)
+            )
+        )
+        if half_count == KEY_VALUE_HEADS:
+            weight_sums = reduce_weights(
+                (rest["hidden_low"], attn_low, rest["normed_mid_low"], normed_low),
+                (
+                    ffn_grad_low,
+                    attn_grad_low,
+                    gate_grad_low,
+                    up_grad_low,
+                    query_grad_low,
+                    key_grad_low,
+                    value_grad_low,
+                ),
+                layer_index + 1,
+            )
+        else:
+            weight_sums = tuple(
+                (
+                    lax.psum_scatter(
+                        jnp.einsum("td,tq->dq", left, right, preferred_element_type=jnp.float32),
+                        ("ctx", "fsdp"),
+                        scatter_dimension=0,
+                        tiled=True,
+                    )
+                    for left, right in (
+                        (normed_low, query_grad_low),
+                        (normed_low, key_grad_low),
+                        (normed_low, value_grad_low),
+                        (attn_low, attn_grad_low),
+                        (rest["normed_mid_low"], gate_grad_low),
+                        (rest["normed_mid_low"], up_grad_low),
+                        (rest["hidden_low"], ffn_grad_low),
+                    )
+                )
+            )
+        layer_grads[layer_index] = weight_sums + gain_sums
     stacked = tuple(
         (jnp.stack([layer_sums[member] for layer_sums in layer_grads]) for member in range(11))
     )

time: 3560 us -> 1740 us (0.49)
  waiting for transfers between devices: 2860 us -> 801 us
  Pallas kernels: 0 us -> 248 us
  matrix products: 231 us -> 162 us
  local copies, waits for them, and re-layouts: 219 us -> 273 us
    reduce_scatter x14 -> x0, waiting for transfers between devices: 1950 us -> none  [the longest x2 371 us: per_device(): lax.psum_scatter(grad_query, ('ctx', 'fsdp'), scatter_dimension=0, tiled=...]
    pallas_call x0 -> x2, Pallas kernels: none -> 248 us  [reduce_layer(): pl.pallas_call(rs_kernel, out_shape=jax.ShapeDtypeStruct((TILES, 32, 1024...]
    ppermute x12, waiting for transfers between devices: 337 us -> 234 us  [from_partner(): lax.ppermute(shard, axis, [(i, i ^ 1 << apart) for i in range(lax.axis_si...]
    dot_general x14 -> x0, matrix products: 71.7 us -> none  [the longest x2 14.8 us: per_device(): jnp.einsum('td,tf->df', rest['normed_mid_low'], gate_grad_low, preferred_...]
  transfers between devices with their start and end apart: 40 -> 26, of which waited for: 34 -> 20; matrix products, arithmetic and copies ran while one was open for 10% -> 18% of each run, Pallas kernels for 0% -> 8%
where the time goes in v1:
time: 1740 us; the launch traced here: 1730 us
  waiting for transfers between devices  801 us (46%)
  local copies, waits for them, and re-layouts  273 us (16%)
  Pallas kernels  248 us (14%)
  matrix products  162 us (9%)
  other arithmetic  139 us (8%)
  blocking collectives  65.7 us (4%)
  between operations  17.9 us (1%)
    pallas_call x2, Pallas kernels, reduce_layer(): pl.pallas_call(rs_kernel, out_shape=jax.ShapeDtypeStruct((TILES, 32, 1024...  248 us
    ppermute x12, waiting for transfers between devices, from_partner(): lax.ppermute(shard, axis, [(i, i ^ 1 << apart) for i in range(lax.axis_si...  234 us
    all_gather x2, waiting for transfers between devices, per_device(): lax.all_gather(w_up[layer_index], 'fsdp', axis=0, tiled=True)  157 us
    all_gather x2, waiting for transfers between devices, per_device(): lax.all_gather(w_down[layer_index], 'fsdp', axis=0, tiled=True)  152 us
    all_gather x2, waiting for transfers between devices, per_device(): lax.all_gather(w_gate[layer_index], 'fsdp', axis=0, tiled=True)  142 us
    unnamed x2, blocking collectives  46.7 us
    all_gather x2, waiting for transfers between devices, per_device(): lax.all_gather(value_projection_weight[layer_index], 'fsdp', axis=0, tile...  46.4 us
    unnamed x468, local copies, waits for them, and re-layouts  43.9 us
  transfers between devices with their start and end apart: 26, of which 20 were waited for; matrix products, arithmetic and copies ran while one was open for 18% of the time, Pallas kernels for 8%

profile of v1, /device:TPU:0, one launch (start us, length us, event | category | flops | bytes accessed | tf_op | source)
XLA Modules:
  0.0 1726.6 jit_solution(6482404634595687828)
XLA Ops:
  21.7 6.2 fusion.253
  27.9 6.0 fusion.254
  34.0 6.3 fusion.255
  64.4 16.8 all-gather.39.cloned.1.call-done
  100.9 11.1 collective-permute-done.1
  120.3 19.3 %all-gather.41.cloned.1.call-done = bf16[1,1024,2048]{2,1,0:T(8,128)(2,1)} async-done(((bf16[1,512,2048]{2,1,0:T(8,128)(2,1)}), bf16[1,1024,2048]{2,1,0:T(8,128)(2,1)}) %all-gather.41.cloned.1.call-update) | async-done | bytes 4194320 | tf_op jit(solution)/shard_map/all_gather | solution.py:580
  146.7 15.6 collective-permute-done.2
  175.1 31.2 %while.56 = (s32[]{:T(128)}, f32[8,2,128]{2,1,0:T(2,128)S(1)}, f32[8,2,128]{2,1,0:T(2,128)}, f32[8,2,128,128]{3,2,1,0:T(8,128)}, s32[2]{0:T(128)}, /*index=5*/s3...) while((s32[]{:T(128)}, f32[8,2,128]{2,1,0:T(2,128)S(1)}, ...), condition=%wide.region_6.7_spmd.clone, body=%wide.region_3.6_spmd.clone.sunk | while | flops 551561216 | bytes 40909792 | solution.py:404
  214.6 65.0 %all-gather.45.cloned.1.call-done = bf16[1,1024,3072]{2,1,0:T(8,128)(2,1)} async-done(((bf16[1,512,3072]{2,1,0:T(8,128)(2,1)}), bf16[1,1024,3072]{2,1,0:T(8,128)(2,1)}) %all-gather.45.cloned.1.call-update) | async-done | bytes 6291472 | tf_op jit(solution)/shard_map/all_gather | solution.py:584
  283.4 78.0 %all-gather.47.cloned.1.call-done = bf16[1,1024,3072]{2,1,0:T(8,128)(2,1)} async-done(((bf16[1,512,3072]{2,1,0:T(8,128)(2,1)}), bf16[1,1024,3072]{2,1,0:T(8,128)(2,1)}) %all-gather.47.cloned.1.call-update) | async-done | bytes 6291472 | tf_op jit(solution)/shard_map/all_gather | solution.py:585
  366.8 76.5 %all-gather.49.cloned.1.call-done = bf16[1,3072,1024]{2,1,0:T(8,128)(2,1)} async-done(((bf16[1,1536,1024]{2,1,0:T(8,128)(2,1)}), bf16[1,3072,1024]{2,1,0:T(8,128)(2,1)}) %all-gather.49.cloned.1.call-update) | async-done | bytes 6291472 | tf_op jit(solution)/shard_map/all_gather | solution.py:586
  448.7 29.3 %all-gather.51.cloned.1.call-done = bf16[1,1024,1024]{2,1,0:T(8,128)(2,1)} async-done(((bf16[1,512,1024]{2,1,0:T(8,128)(2,1)}), bf16[1,1024,1024]{2,1,0:T(8,128)(2,1)}) %all-gather.51.cloned.1.call-update) | async-done | bytes 2097168 | tf_op jit(solution)/shard_map/all_gather | solution.py:581
  483.1 29.6 %all-gather.53.cloned.1.call-done = bf16[1,1024,1024]{2,1,0:T(8,128)(2,1)} async-done(((bf16[1,512,1024]{2,1,0:T(8,128)(2,1)}), bf16[1,1024,1024]{2,1,0:T(8,128)(2,1)}) %all-gather.53.cloned.1.call-update) | async-done | bytes 2097168 | tf_op jit(solution)/shard_map/all_gather | solution.py:582
  519.4 22.9 %collective-permute-done.4 = bf16[256,2048]{1,0:T(8,128)(2,1)S(1)} collective-permute-done((bf16[256,2048]{1,0:T(8,128)(2,1)S(1)}, bf16[256,2048]{1,0:T(8,128)(2,1)S(1)}, u32[]{:S(2)}, u32[]{:S(2)}) %collective-permute-start.4) | collective-permute-done | bytes 1048608 | tf_op jit(solution)/shard_map/ppermute | solution.py:314
  553.2 17.7 %all-gather.55.cloned.1.call-done = bf16[1,1024,2048]{2,1,0:T(8,128)(2,1)} async-done(((bf16[1,512,2048]{2,1,0:T(8,128)(2,1)}), bf16[1,1024,2048]{2,1,0:T(8,128)(2,1)}) %all-gather.55.cloned.1.call-update) | async-done | bytes 4194320 | tf_op jit(solution)/shard_map/all_gather | solution.py:580
  577.9 75.0 %all-gather.63.cloned.1.call-done = bf16[1,3072,1024]{2,1,0:T(8,128)(2,1)} async-done(((bf16[1,1536,1024]{2,1,0:T(8,128)(2,1)}), bf16[1,3072,1024]{2,1,0:T(8,128)(2,1)}) %all-gather.63.cloned.1.call-update) | async-done | bytes 6291472 | tf_op jit(solution)/shard_map/all_gather | solution.py:586
  652.9 6.2 fusion.58
  671.4 33.3 %while.57 = (s32[]{:T(128)}, f32[8,2,128]{2,1,0:T(2,128)S(1)}, f32[8,2,128]{2,1,0:T(2,128)S(1)}, f32[8,2,128,128]{3,2,1,0:T(8,128)}, s32[2]{0:T(128)S(1)}, /*ind...) while((s32[]{:T(128)}, f32[8,2,128]{2,1,0:T(2,128)S(1)}, ...), condition=%wide.region_14.15_spmd.clone, body=%wide.region_11.14_spmd.clone.sunk | while | flops 551561216 | bytes 38681428 | solution.py:404
  714.4 78.6 %all-gather.61.cloned.1.call-done = bf16[1,1024,3072]{2,1,0:T(8,128)(2,1)} async-done(((bf16[1,512,3072]{2,1,0:T(8,128)(2,1)}), bf16[1,1024,3072]{2,1,0:T(8,128)(2,1)}) %all-gather.61.cloned.1.call-update) | async-done | bytes 6291472 | tf_op jit(solution)/shard_map/all_gather | solution.py:585
  798.1 76.7 %all-gather.59.cloned.1.call-done = bf16[1,1024,3072]{2,1,0:T(8,128)(2,1)} async-done(((bf16[1,512,3072]{2,1,0:T(8,128)(2,1)}), bf16[1,1024,3072]{2,1,0:T(8,128)(2,1)}) %all-gather.59.cloned.1.call-update) | async-done | bytes 6291472 | tf_op jit(solution)/shard_map/all_gather | solution.py:584
  874.8 6.6 multiply_convert_fusion.3
  898.8 65.6 %while.58 = (s32[]{:T(128)}, f32[128,8,2,128]{0,3,2,1:T(8,128)}, f32[2,512,2048]{2,1,0:T(8,128)}, s32[2]{0:T(128)S(1)}, bf16[1024,1024]{0,1:T(8,128)(2,1)S(1)}, ...) while((s32[]{:T(128)}, f32[128,8,2,128]{0,3,2,1:T(8,128)}, ...), condition=%wide.region_19.20_spmd.clone, body=%wide.region_18.19_spmd.clone.sunk | while | flops 1355284480 | bytes 101948424 | solution.py:706
  953.9 5.5 copy.695
  970.4 90.8 %collective-permute-done.6 = f32[512,2048]{1,0:T(8,128)S(1)} collective-permute-done((f32[512,2048]{1,0:T(8,128)S(1)}, f32[512,2048]{1,0:T(8,128)S(1)}, u32[]{:S(2)}, u32[]{:S(2)}) %collective-permute-start.6) | collective-permute-done | bytes 4194336 | tf_op jit(solution)/shard_map/ppermute | solution.py:314
  1077.1 35.4 %collective-permute-done.7 = f32[256,2048]{1,0:T(8,128)} collective-permute-done((f32[256,2048]{1,0:T(8,128)}, f32[256,2048]{1,0:T(8,128)}, u32[]{:S(2)}, u32[]{:S(2)}) %collective-permute-start.7) | collective-permute-done | bytes 2097184 | tf_op jit(solution)/shard_map/ppermute | solution.py:314
  1147.7 5.5 multiply_convert_fusion.1
  1166.5 65.8 %while.59 = (s32[]{:T(128)}, f32[128,8,2,128]{0,3,2,1:T(8,128)}, f32[2,512,2048]{2,1,0:T(8,128)}, s32[2]{0:T(128)S(1)}, bf16[1024,1024]{0,1:T(8,128)(2,1)}, /*in...) while((s32[]{:T(128)}, f32[128,8,2,128]{0,3,2,1:T(8,128)}, ...), condition=%wide.region_26.27_spmd.clone, body=%wide.region_25.26_spmd.clone.sunk | while | flops 1355284480 | bytes 83073984 | solution.py:706
  1232.4 6.7 select_bitcast_fusion
  1277.7 54.0 %collective-permute-done.9 = f32[512,2048]{1,0:T(8,128)} collective-permute-done((f32[512,2048]{1,0:T(8,128)}, f32[512,2048]{1,0:T(8,128)}, u32[]{:S(2)}, u32[]{:S(2)}) %collective-permute-start.9) | collective-permute-done | bytes 4194336 | tf_op jit(solution)/shard_map/ppermute | solution.py:314
  1347.4 131.9 %weight_gradient_reduce.3 = f32[15,32,1024]{2,1,0:T(8,128)S(1)} custom-call(bf16[2,2,7,256,128]{4,3,2,1,0:T(8,128)(2,1)S(1)} %copy-done, bf16[12,128,1024]{2,1,0:T(8,128)(2,1)} %bitcast_dynamic-update-slice_fusion.6.grads), custom_call_target="tpu_custom_call" | custom-call | tf_op jit(solution)/shard_map/weight_gradient_reduce/pallas_call | solution.py:256
  1540.8 116.2 %weight_gradient_reduce.2 = f32[15,32,1024]{2,1,0:T(8,128)S(1)} custom-call(bf16[2,2,7,256,128]{4,3,2,1,0:T(8,128)(2,1)S(1)} %pad_maximum_fusion.4.acts, bf16[12,128,1024]{2,1,0:T(8,128)(2,1)} %bitcast_dynamic-update-slice_fusion.10.grads), custom_call_target="tpu_custom_call" | custom-call | tf_op jit(solution)/shard_map/weight_gradient_reduce/pallas_call | solution.py:256
  1671.2 41.3 %all-reduce.12 = (f32[1024]{0:T(1024)S(1)}, f32[1024]{0:T(1024)S(1)}, f32[1024]{0:T(1024)S(1)}, f32[1024]{0:T(1024)S(1)}, f32[128]{0:T(128)S(1)}, /*index=5*/f32[128]{0:T(128)S(1)}, f32[128]{0:T(128)S(1)}, f32[128]{0:T(128)S(1)}) all-reduce(f32[1024]{0:T(1024)S(1)} %copy-done.190, ...), channel_id=25, replica_groups=mesh['ctx'=16,'fsdp'=2] {'ctx','fsdp'}, use_global_device_ids=true, to_apply=%region_33.34.clone | all-reduce | flops 4608 | bytes 36864
  (976 shorter events, 571.4 us)
Async XLA Ops:
  7.2 51.9 %all-gather.37.cloned.1.call-start = ((), (), s32[]{:S(2)}) async-start(), calls=%async_computation | async-start | bytes 3145728 | tf_op jit(solution)/shard_map/all_gather | solution.py:581
  10.5 70.7 %all-gather.39.cloned.1.call-start = ((), (), s32[]{:S(2)}) async-start(), calls=%async_computation.1 | async-start | bytes 3145728 | tf_op jit(solution)/shard_map/all_gather | solution.py:582
  12.0 127.5 %all-gather.41.cloned.1.call-start = ((), (), s32[]{:S(2)}) async-start(), calls=%async_computation.2 | async-start | bytes 6291456 | tf_op jit(solution)/shard_map/all_gather | solution.py:580
  16.9 193.6 %all-gather.43.cloned.1.call-start = ((), (), s32[]{:S(2)}) async-start(), calls=%async_computation.3 | async-start | bytes 6291456 | tf_op jit(solution)/shard_map/all_gather | solution.py:583
  21.7 257.9 %all-gather.45.cloned.1.call-start = ((), (), s32[]{:S(2)}) async-start(), calls=%async_computation.4 | async-start | bytes 9437184 | tf_op jit(solution)/shard_map/all_gather | solution.py:584
  27.9 333.5 %all-gather.47.cloned.1.call-start = ((), (), s32[]{:S(2)}) async-start(), calls=%async_computation.5 | async-start | bytes 9437184 | tf_op jit(solution)/shard_map/all_gather | solution.py:585
  34.0 409.4 %all-gather.49.cloned.1.call-start = ((), (), s32[]{:S(2)}) async-start(), calls=%async_computation.6 | async-start | bytes 9437184 | tf_op jit(solution)/shard_map/all_gather | solution.py:586
  40.4 437.7 %all-gather.51.cloned.1.call-start = ((), (), s32[]{:S(2)}) async-start(), calls=%async_computation.7 | async-start | bytes 3145728 | tf_op jit(solution)/shard_map/all_gather | solution.py:581
  41.1 471.6 %all-gather.53.cloned.1.call-start = ((), (), s32[]{:S(2)}) async-start(), calls=%async_computation.8 | async-start | bytes 3145728 | tf_op jit(solution)/shard_map/all_gather | solution.py:582
  41.8 529.1 %all-gather.55.cloned.1.call-start = ((), (), s32[]{:S(2)}) async-start(), calls=%async_computation.9 | async-start | bytes 6291456 | tf_op jit(solution)/shard_map/all_gather | solution.py:580
  42.5 610.4 %all-gather.63.cloned.1.call-start = ((), (), s32[]{:S(2)}) async-start(), calls=%async_computation.13 | async-start | bytes 9437184 | tf_op jit(solution)/shard_map/all_gather | solution.py:586
  43.2 667.8 %all-gather.57.cloned.1.call-start = ((), (), s32[]{:S(2)}) async-start(), calls=%async_computation.10 | async-start | bytes 6291456 | tf_op jit(solution)/shard_map/all_gather | solution.py:583
  43.8 749.2 %all-gather.61.cloned.1.call-start = ((), (), s32[]{:S(2)}) async-start(), calls=%async_computation.12 | async-start | bytes 9437184 | tf_op jit(solution)/shard_map/all_gather | solution.py:585
  58.9 516.9 %copy-start.105 = (f32[128,128]{0,1:T(8,128)}, f32[128,128]{0,1:T(8,128)S(1)}, u32[]{:S(2)}) copy-start(f32[128,128]{0,1:T(8,128)S(1)} %pad_maximum_fusion.21) | copy-start | bytes 196612
  83.3 2.0 collective-permute-start
  86.5 25.4 %collective-permute-start.1 = (bf16[256,2048]{1,0:T(8,128)(2,1)}, bf16[256,2048]{1,0:T(8,128)(2,1)S(1)}, u32[]{:S(2)}, u32[]{:S(2)}) collective-permute-start(bf16[256,2048]{1,0:T(8,128)(2,1)} %pad_maximum_fusion.6), channel_id=1, source_target_pairs={{0,4},{2,6},{4,0},{6,2},{8,12},{10,14},{12,8},{14,10},{16,20},{18,... | collective-permute-start | bytes 3145736 | tf_op jit(solution)/shard_map/ppermute | solution.py:314
  88.0 786.8 %all-gather.59.cloned.1.call-start = ((), (), s32[]{:S(2)}) async-start(), calls=%async_computation.11 | async-start | bytes 9437184 | tf_op jit(solution)/shard_map/all_gather | solution.py:584
  115.0 47.3 %collective-permute-start.2 = (bf16[512,2048]{1,0:T(8,128)(2,1)}, bf16[512,2048]{1,0:T(8,128)(2,1)}, u32[]{:S(2)}, u32[]{:S(2)}) collective-permute-start(bf16[512,2048]{1,0:T(8,128)(2,1)} %pad_maximum_fusion.2), channel_id=1, source_target_pairs={{0,8},{2,10},{4,12},{6,14},{8,0},{10,2},{12,4},{14,6},{16,24},{18,... | collective-permute-start | bytes 6291464 | tf_op jit(solution)/shard_map/ppermute | solution.py:314
  214.0 229.3 %copy-start.35 = (f32[128,1024]{1,0:T(8,128)}, f32[128,1024]{1,0:T(8,128)S(1)}, u32[]{:S(2)}) copy-start(f32[128,1024]{1,0:T(8,128)S(1)} %get-tuple-element.1174) | copy-start | bytes 1572868
  214.6 146.8 %copy-start.195 = (f32[128]{0:T(128)}, f32[128]{0:T(128)S(1)}, u32[]{:S(2)}) copy-start(f32[128]{0:T(128)S(1)} %get-tuple-element.1160) | copy-start | bytes 1540
  283.4 159.9 %copy-start.140 = (f32[128,3072]{1,0:T(8,128)}, f32[128,3072]{1,0:T(8,128)S(1)}, u32[]{:S(2)}) copy-start(f32[128,3072]{1,0:T(8,128)S(1)} %fusion.80) | copy-start | bytes 4718596
  514.8 2.0 collective-permute-start.3
  517.1 25.3 %collective-permute-start.4 = (bf16[256,2048]{1,0:T(8,128)(2,1)S(1)}, bf16[256,2048]{1,0:T(8,128)(2,1)S(1)}, u32[]{:S(2)}, u32[]{:S(2)}) collective-permute-start(bf16[256,2048]{1,0:T(8,128)(2,1)S(1)} %pad_maximum_fusion.7), channel_id=1, source_target_pairs={{0,4},{2,6},{4,0},{6,2},{8,12},{10,14},{12,8},{14,10},{16,20},{18,... | collective-permute-start | bytes 3145736 | tf_op jit(solution)/shard_map/ppermute | solution.py:314
  545.5 113.6 %collective-permute-start.5 = (bf16[512,2048]{1,0:T(8,128)(2,1)}, bf16[512,2048]{1,0:T(8,128)(2,1)}, u32[]{:S(2)}, u32[]{:S(2)}) collective-permute-start(bf16[512,2048]{1,0:T(8,128)(2,1)} %pad_maximum_fusion.3), channel_id=1, source_target_pairs={{0,8},{2,10},{4,12},{6,14},{8,0},{10,2},{12,4},{14,6},{16,24},{18,... | collective-permute-start | bytes 6291464 | tf_op jit(solution)/shard_map/ppermute | solution.py:314
  714.3 173.3 %copy-start.33 = (f32[128,1024]{1,0:T(8,128)}, f32[128,1024]{1,0:T(8,128)S(1)}, u32[]{:S(2)}) copy-start(f32[128,1024]{1,0:T(8,128)S(1)} %get-tuple-element.1178) | copy-start | bytes 1572868
  714.4 173.3 %copy-start.198 = (f32[128]{0:T(128)}, f32[128]{0:T(128)S(1)}, u32[]{:S(2)}) copy-start(f32[128]{0:T(128)S(1)} %get-tuple-element.1164) | copy-start | bytes 1540
  968.8 92.4 %collective-permute-start.6 = (f32[512,2048]{1,0:T(8,128)S(1)}, f32[512,2048]{1,0:T(8,128)S(1)}, u32[]{:S(2)}, u32[]{:S(2)}) collective-permute-start(f32[512,2048]{1,0:T(8,128)S(1)} %select_bitcast_fusion.1), channel_id=1, source_target_pairs={{0,8},{2,10},{4,12},{6,14},{8,0},{10,2},{12,4},{14,6},{16,24},{18,... | collective-permute-start | bytes 12582920 | tf_op jit(solution)/shard_map/ppermute | solution.py:314
  1065.6 46.9 %collective-permute-start.7 = (f32[256,2048]{1,0:T(8,128)}, f32[256,2048]{1,0:T(8,128)}, u32[]{:S(2)}, u32[]{:S(2)}) collective-permute-start(f32[256,2048]{1,0:T(8,128)} %slice_select_fusion.1), channel_id=1, source_target_pairs={{0,4},{2,6},{4,0},{6,2},{8,12},{10,14},{12,8},{14,10},{16,20},{18,... | collective-permute-start | bytes 6291464 | tf_op jit(solution)/shard_map/ppermute | solution.py:314
  1117.0 18.6 %collective-permute-start.8 = (f32[128,2048]{1,0:T(8,128)}, f32[128,2048]{1,0:T(8,128)}, u32[]{:S(2)}, u32[]{:S(2)}) collective-permute-start(f32[128,2048]{1,0:T(8,128)} %slice_select_fusion.3), channel_id=1, source_target_pairs={{0,2},{2,0},{4,6},{6,4},{8,10},{10,8},{12,14},{14,12},{16,18},{18,... | collective-permute-start | bytes 3145736 | tf_op jit(solution)/shard_map/ppermute | solution.py:314
  1239.1 92.6 %collective-permute-start.9 = (f32[512,2048]{1,0:T(8,128)}, f32[512,2048]{1,0:T(8,128)}, u32[]{:S(2)}, u32[]{:S(2)}) collective-permute-start(f32[512,2048]{1,0:T(8,128)} %select_bitcast_fusion), channel_id=1, source_target_pairs={{0,8},{2,10},{4,12},{6,14},{8,0},{10,2},{12,4},{14,6},{16,24},{18,... | collective-permute-start | bytes 12582920 | tf_op jit(solution)/shard_map/ppermute | solution.py:314
  1338.0 145.8 %collective-permute-start.10 = (f32[256,2048]{1,0:T(8,128)}, f32[256,2048]{1,0:T(8,128)}, u32[]{:S(2)}, u32[]{:S(2)}) collective-permute-start(f32[256,2048]{1,0:T(8,128)} %slice_select_fusion), channel_id=1, source_target_pairs={{0,4},{2,6},{4,0},{6,2},{8,12},{10,14},{12,8},{14,10},{16,20},{18,... | collective-permute-start | bytes 6291464 | tf_op jit(solution)/shard_map/ppermute | solution.py:314
  1488.8 39.5 %collective-permute-start.11 = (f32[128,2048]{1,0:T(8,128)}, f32[128,2048]{1,0:T(8,128)}, u32[]{:S(2)}, u32[]{:S(2)}) collective-permute-start(f32[128,2048]{1,0:T(8,128)} %slice_select_fusion.2), channel_id=1, source_target_pairs={{0,2},{2,0},{4,6},{6,4},{8,10},{10,8},{12,14},{14,12},{16,18},{18,... | collective-permute-start | bytes 3145736 | tf_op jit(solution)/shard_map/ppermute | solution.py:314
  (247 other events, 2319.0 us)
Sparse Core Ops, SparseCore 0:
  10.6 35.8 all-gather.36
  48.0 33.1 all-gather.38
  82.7 56.8 all-gather.40
  141.0 56.7 all-gather.42
  199.1 80.3 all-gather.44
  280.9 80.3 all-gather.46
  362.9 80.3 all-gather.48
  444.9 33.1 all-gather.50
  479.6 33.1 all-gather.52
  514.1 56.7 all-gather.54
  572.5 80.3 all-gather.62
  654.3 56.7 all-gather.56
  712.6 80.3 all-gather.60
  794.4 80.3 all-gather.58

commit v2 on v1

--- a/solution.py
+++ b/solution.py
@@ -1,3 +1,4 @@
+import functools
 import math
 
 import jax
@@ -19,6 +20,7 @@
 masked_logits = -1e30
 
 MESH = pl.DeviceIdType.MESH
+
 TILES = 15
 GRADS = 12
 AHEAD = 3
@@ -37,9 +39,9 @@
 
 
 def rs_kernel(
-    acts, grads, out, abuf, afwd, gbuf, ysend, yrecv, own, zsend, zrecv, zown,
+    acts, grads, gains, out, gain_out, abuf, afwd, gbuf, ysend, yrecv, own, zsend, zrecv, zown,
     a_local, a_xs, a_xr, a_cs, a_cr, g_local, g_xs, g_xr, g_cs, g_cr, g_fs, g_fr,
-    y_s, y_r, z_s, z_r,
+    y_s, y_r, z_s, z_r, gain_part, gain_recv, gain_s, gain_r,
 ):
     c = lax.axis_index("ctx")
     x = lax.axis_index("fsdp")
@@ -70,16 +72,15 @@
             acts.at[x, core, spans[g]], abuf.at[spans[g], :, pl.ds(0, 128)], a_local.at[g]
         )
 
-    def act_across(g):
-        return (
-            remote(
-                acts.at[1 - x, core, spans[g]], abuf.at[spans[g], :, pl.ds(128, 128)],
-                a_xs.at[g, 0], a_xr.at[g, 0], across,
-            ),
-            remote(
+    def act_across(g, other):
+        if other:
+            return remote(
                 acts.at[1 - x, 1 - core, spans[g]], afwd.at[spans[g]],
                 a_xs.at[g, 1], a_xr.at[g, 1], across,
-            ),
+            )
+        return remote(
+            acts.at[1 - x, core, spans[g]], abuf.at[spans[g], :, pl.ds(128, 128)],
+            a_xs.at[g, 0], a_xr.at[g, 0], across,
         )
 
     def act_sibling(g):
@@ -117,8 +118,8 @@
         )
 
     def start_acts(g):
-        for copy in act_across(g):
-            copy.start()
+        act_across(g, 0).start()
+        act_across(g, 1).start()
         act_sibling(g).start()
         act_local(g).start()
 
@@ -127,6 +128,21 @@
         grad_sibling(i).start()
         grad_local(i).start()
 
+    def gain_copy(i):
+        return remote(
+            gains if i == 0 else gain_part.at[i - 1],
+            gain_recv.at[i],
+            gain_s.at[i],
+            gain_r.at[i],
+            (across, sibling, aside)[i],
+        )
+
+    def gain_along(o):
+        return remote(
+            gain_part.at[2], gain_recv.at[6 - o], gain_s.at[2 + o], gain_r.at[6 - o], along(o)
+        )
+
+    gain_copy(0).start()
     start_acts(0)
     start_grad(0)
     start_acts(1)
@@ -134,16 +150,34 @@
         start_grad(i)
 
     def forward_acts(g):
-        act_across(g)[1].wait_recv()
+        act_across(g, 1).wait_recv()
         act_forward(g).start()
 
     def await_acts(g):
         act_local(g).wait()
-        act_across(g)[0].wait_recv()
+        act_across(g, 0).wait_recv()
         act_sibling(g).wait_recv()
         act_forward(g).wait_recv()
 
     def step(s, carry):
+        for i in range(3):
+
+            @pl.when(s == 2 * i + 2)
+            def gain_stage(i=i):
+                gain_copy(i).wait_recv()
+                gain_part[i] = (gains[...] if i == 0 else gain_part[i - 1]) + gain_recv[i]
+                if i < 2:
+                    gain_copy(i + 1).start()
+                else:
+                    for o in (1, 2, 3):
+                        gain_along(o).start()
+
+        @pl.when(s == 10)
+        def gain_total():
+            for o in (1, 2, 3):
+                gain_along(o).wait_recv()
+            gain_out[...] = gain_part[2] + gain_recv[3] + gain_recv[4] + gain_recv[5]
+
         t = s - 5
 
         @pl.when(t >= 0)
@@ -227,9 +261,12 @@
 
     lax.fori_loop(0, TILES + 5, step, 0)
 
+    for i in range(3):
+        gain_copy(i).wait_send()
+        gain_along(i + 1).wait_send()
     for g in range(2):
-        for copy in act_across(g):
-            copy.wait_send()
+        act_across(g, 0).wait_send()
+        act_across(g, 1).wait_send()
         act_sibling(g).wait_send()
         act_forward(g).wait_send()
 
@@ -250,14 +287,18 @@
     lax.fori_loop(0, TILES, drain_tiles, 0)
 
 
-def reduce_layer(acts, grads, collective_id):
+def reduce_layer(acts, grads, gains, collective_id):
     dma = pltpu.SemaphoreType.DMA
     low, wide = jnp.bfloat16, jnp.float32
     return pl.pallas_call(
         rs_kernel,
-        out_shape=jax.ShapeDtypeStruct((TILES, 32, 1024), wide),
-        in_specs=[pl.BlockSpec(memory_space=pl.ANY)] * 2,
-        out_specs=pl.BlockSpec(memory_space=pltpu.VMEM),
+        out_shape=[
+            jax.ShapeDtypeStruct((TILES, 32, 1024), wide),
+            jax.ShapeDtypeStruct(gains.shape, wide),
+        ],
+        in_specs=[pl.BlockSpec(memory_space=pl.ANY)] * 2
+        + [pl.BlockSpec(memory_space=pltpu.VMEM)],
+        out_specs=[pl.BlockSpec(memory_space=pltpu.VMEM)] * 2,
         scratch_shapes=[
             pltpu.VMEM((7, 256, 512), low),
             pltpu.VMEM((7, 256, 128), low),
@@ -272,42 +313,553 @@
             dma((GRADS,)), dma((GRADS,)), dma((GRADS,)), dma((GRADS,)), dma((GRADS,)),
             dma((GRADS,)), dma((GRADS,)),
             dma((TILES,)), dma((TILES,)), dma((TILES, 3)), dma((TILES, 3)),
+            pltpu.VMEM((3,) + gains.shape, wide), pltpu.VMEM((6,) + gains.shape, wide),
+            dma((6,)), dma((6,)),
         ],
         compiler_params=pltpu.CompilerParams(
             collective_id=collective_id, has_side_effects=True, vmem_limit_bytes=48 * 2**20
         ),
         name="weight_gradient_reduce",
-    )(acts, grads)
-
-
-def act_blocks(values):
-    turned = values.T.reshape(4, 2, 2, 2, -1, 32, values.shape[0])
-    return turned.transpose(3, 2, 4, 1, 0, 5, 6).reshape(2, 2, -1, 256, values.shape[0])
-
-
-def grad_blocks(values):
-    return values.reshape(values.shape[0], -1, 1024).transpose(1, 0, 2)
-
-
-def side_by_side(tiles):
-    return tiles.transpose(1, 0, 2).reshape(tiles.shape[1], -1)
-
-
-def reduce_weights(acts, grads, collective_id):
-    tiles = reduce_layer(
-        jnp.concatenate([act_blocks(member) for member in acts], axis=2),
-        jnp.concatenate([grad_blocks(member) for member in grads], axis=0),
-        collective_id,
-    )
-    return (
-        side_by_side(tiles[11:13]),
-        tiles[13],
-        tiles[14],
-        tiles[3:5].reshape(64, 1024),
-        side_by_side(tiles[5:8]),
-        side_by_side(tiles[8:11]),
-        tiles[0:3].reshape(96, 1024),
-    )
+    )(acts, grads, gains)
+
+
+GATHER_PLAN = ((0, 0, 0), (1, 0, 2048), (2, 0, 3072), (3, 1, 0), (4, 2, 0), (5, 2, 3072), (6, 3, 0))
+MEMBERS = 7
+
+
+def gather_kernel(layers, *refs):
+    sources = refs[:MEMBERS]
+    gains = refs[MEMBERS]
+    outs = refs[MEMBERS + 1 : MEMBERS + 1 + 4 * len(layers)]
+    gains_out = refs[MEMBERS + 1 + 4 * len(layers)]
+    (l_sem, l_rec, x_s, x_r, y_s, y_r, z_s, z_r, yd_s, yd_r, zd_s, zd_r, c_s, c_r, g_sem) = refs[
+        MEMBERS + 2 + 4 * len(layers) :
+    ]
+    c = lax.axis_index("ctx")
+    x = lax.axis_index("fsdp")
+    core = c % 2
+    y = c // 2 % 2
+    near = c // 4 % 2
+    sibling = (c + 1 - 2 * core, x)
+    across = (c, 1 - x)
+    aside = (c + 2 - 4 * y, x)
+    along = (c + 4 - 8 * near, x)
+
+    barrier = pltpu.get_barrier_semaphore()
+    for other in (sibling, across, aside, along):
+        pl.semaphore_signal(barrier, inc=1, device_id=other, device_id_type=MESH)
+    pl.semaphore_wait(barrier, 4)
+
+    def remote(src, dst, s, r, dev):
+        return pltpu.make_async_remote_copy(
+            src_ref=src, dst_ref=dst, send_sem=s, recv_sem=r, device_id=dev, device_id_type=MESH
+        )
+
+    here = near * 2 + y
+    by_y = near * 2 + 1 - y
+    by_z = (1 - near) * 2 + y
+    corner = (1 - near) * 2 + 1 - y
+    steps = [(n, m) for n in range(len(layers)) for m in range(MEMBERS)]
+    count = len(steps)
+
+    def geometry(i):
+        n, m = steps[i]
+        source, target, column = GATHER_PLAN[m]
+        half = sources[source].shape[1]
+        part = half // 8
+        width = sources[source].shape[2]
+        return n, sources[source], outs[4 * n + target], half, part, width, column
+
+    def window(i, owner_x, owner_core, piece, share=None):
+        n, src, out, half, part, width, column = geometry(i)
+        start = owner_x * half + (piece * 2 + owner_core) * part
+        rows = part
+        if share is not None:
+            rows = part // 2
+            start = start + share * rows
+        return out.at[pl.ds(pl.multiple_of(start, 16), rows), pl.ds(column, width)]
+
+    def local(i):
+        n, src, out, half, part, width, column = geometry(i)
+        rows = pl.ds(pl.multiple_of(x * half, 16), half)
+        return remote(
+            src.at[layers[n]], out.at[rows, pl.ds(column, width)], l_sem.at[i], l_rec.at[i], sibling
+        )
+
+    def x_copy(i):
+        n, src, out, half, part, width, column = geometry(i)
+        rows = pl.ds(pl.multiple_of((here * 2 + core) * part, 16), part)
+        return remote(
+            src.at[layers[n], rows], window(i, x, core, here), x_s.at[i], x_r.at[i], across
+        )
+
+    def same(i, piece, s, r, dev, share=None):
+        view = window(i, 1 - x, core, piece, share)
+        return remote(view, view, s, r, dev)
+
+    def y_copy(i):
+        return same(i, here, y_s.at[i], y_r.at[i], aside)
+
+    def z_copy(i):
+        return same(i, here, z_s.at[i], z_r.at[i], along)
+
+    def y_corner(i):
+        return same(i, by_z, yd_s.at[i], yd_r.at[i], aside, 1)
+
+    def z_corner(i):
+        return same(i, by_y, zd_s.at[i], zd_r.at[i], along, 0)
+
+    def core_copy(i, which):
+        piece = (here, by_y, by_z, corner)[which]
+        return same(i, piece, c_s.at[i, which], c_r.at[i, which], sibling)
+
+    gain_local = pltpu.make_async_copy(gains, gains_out.at[x], g_sem.at[0])
+    gain_remote = remote(gains, gains_out.at[x], g_sem.at[1], g_sem.at[2], across)
+    gain_local.start()
+    gain_remote.start()
+
+    ahead = 3
+    for i in range(min(ahead, count)):
+        x_copy(i).start()
+        local(i).start()
+    for s in range(count + 3):
+        if s < count:
+            x_copy(s).wait_recv()
+            y_copy(s).start()
+            z_copy(s).start()
+            core_copy(s, 0).start()
+            if s + ahead < count:
+                x_copy(s + ahead).start()
+                local(s + ahead).start()
+        i = s - 1
+        if 0 <= i < count:
+            y_copy(i).wait_recv()
+            z_corner(i).start()
+            core_copy(i, 1).start()
+            z_copy(i).wait_recv()
+            y_corner(i).start()
+            core_copy(i, 2).start()
+        i = s - 3
+        if 0 <= i < count:
+            y_corner(i).wait_recv()
+            z_corner(i).wait_recv()
+            core_copy(i, 3).start()
+    gain_local.wait()
+    gain_remote.wait()
+    for i in range(count):
+        local(i).wait()
+        for copy in (x_copy(i), y_copy(i), z_copy(i), y_corner(i), z_corner(i)):
+            copy.wait_send()
+        for which in range(4):
+            core_copy(i, which).wait()
+
+
+def gather_weights(weights, gains, layers, collective_id):
+    dma = pltpu.SemaphoreType.DMA
+    count = MEMBERS * len(layers)
+    low = jnp.bfloat16
+    shapes = [(1024, 4096), (2048, 1024), (1024, 6144), (3072, 1024)] * len(layers)
+    return pl.pallas_call(
+        functools.partial(gather_kernel, layers),
+        out_shape=[jax.ShapeDtypeStruct(s, low) for s in shapes]
+        + [jax.ShapeDtypeStruct((2,) + gains.shape, low)],
+        in_specs=[pl.BlockSpec(memory_space=pl.ANY)] * (MEMBERS + 1),
+        out_specs=[pl.BlockSpec(memory_space=pl.ANY)] * (len(shapes) + 1),
+        scratch_shapes=[dma((count,))] * 12 + [dma((count, 4))] * 2 + [dma((3,))],
+        compiler_params=pltpu.CompilerParams(collective_id=collective_id, has_side_effects=True),
+        name="weight_gather",
+    )(*weights, gains)
+
+
+PEERS = KEY_VALUE_HEADS
+SCALE = HEAD_SIZE ** (-0.5)
+NT = (((1,), (1,)), ((), ()))
+
+
+def peer_tools():
+    c = lax.axis_index("ctx")
+    x = lax.axis_index("fsdp")
+    me = c % PEERS
+
+    def peer(r):
+        return (c - me + r, x)
+
+    def remote(src, dst, s, r, dev):
+        return pltpu.make_async_remote_copy(
+            src_ref=src, dst_ref=dst, send_sem=s, recv_sem=r, device_id=dev, device_id_type=MESH
+        )
+
+    barrier = pltpu.get_barrier_semaphore()
+
+    def greet(o, carry):
+        pl.semaphore_signal(
+            barrier, inc=1, device_id=peer((me + o) % PEERS), device_id_type=MESH
+        )
+        return carry
+
+    lax.fori_loop(1, PEERS, greet, 0)
+    return me, peer, remote, barrier
+
+
+def head_columns(first, index):
+    return pl.ds(pl.multiple_of(first + index * HEAD_SIZE, HEAD_SIZE), HEAD_SIZE)
+
+
+def attend_kernel(
+    pre, cosine, sine, gains, key_place, query_cap, out, kept, kept_out, kept_log,
+    send, osend, orecv, vt, q_s, q_r, k_s, k_r, o_s, o_r,
+):
+    me, peer, remote, barrier = peer_tools()
+    cos = cosine[...]
+    sin = sine[...]
+
+    def turned(first, index, gain):
+        v = pre[:, head_columns(first, index)]
+        r = lax.rsqrt(jnp.mean(v * v, axis=-1, keepdims=True) + norm_epsilon)
+        n = v * r * gain
+        return (n * cos + pltpu.roll(n, HEAD_SIZE // 2, 1) * sin).astype(jnp.bfloat16)
+
+    def key_copy(r, slot):
+        return remote(
+            send.at[r, pl.ds(2, 2)], kept.at[slot, pl.ds(2, 2)], k_s.at[r], k_r.at[slot], peer(r)
+        )
+
+    def query_copy(r, slot):
+        return remote(
+            send.at[r, pl.ds(0, 2)], kept.at[slot, pl.ds(0, 2)], q_s.at[r], q_r.at[slot], peer(r)
+        )
+
+    def out_copy(r, slot):
+        return remote(osend.at[r], orecv.at[slot], o_s.at[r], o_r.at[slot], peer(r))
+
+    def make_keys(o, carry):
+        r = (me + o) % PEERS
+        key = turned(2048, r, gains[1:2, :])
+        value = pre[:, head_columns(3072, r)].astype(jnp.bfloat16)
+
+        @pl.when(o < PEERS)
+        def away():
+            send[r, 2] = key
+            send[r, 3] = value
+
+        @pl.when(o == PEERS)
+        def home():
+            kept[me, 2] = key
+            kept[me, 3] = value
+
+        @pl.when(o == 1)
+        def entered():
+            pl.semaphore_wait(barrier, PEERS - 1)
+
+        @pl.when(o < PEERS)
+        def push():
+            key_copy(r, me).start()
+
+        return carry
+
+    def make_queries(o, carry):
+        r = (me + o) % PEERS
+        first = turned(0, 2 * r, gains[0:1, :])
+        second = turned(0, 2 * r + 1, gains[0:1, :])
+
+        @pl.when(o < PEERS)
+        def away():
+            send[r, 0] = first
+            send[r, 1] = second
+            query_copy(r, me).start()
+
+        @pl.when(o == PEERS)
+        def home():
+            kept[me, 0] = first
+            kept[me, 1] = second
+
+        return carry
+
+    lax.fori_loop(1, PEERS + 1, make_keys, 0)
+    lax.fori_loop(1, PEERS + 1, make_queries, 0)
+
+    def await_keys(o, carry):
+        key_copy(me, (me + o) % PEERS).wait_recv()
+        return carry
+
+    lax.fori_loop(1, PEERS, await_keys, 0)
+
+    def turn_values(j, carry):
+        vt[j] = kept[j, 3].astype(jnp.float32).T.astype(jnp.bfloat16)
+        return carry
+
+    lax.fori_loop(0, PEERS, turn_values, 0)
+
+    def block(o, carry):
+        j = (me + o) % PEERS
+
+        @pl.when(o > 0)
+        def arrived():
+            query_copy(me, j).wait_recv()
+
+        queries = kept[j, 0:2].reshape(2 * 128, HEAD_SIZE)
+        keys = kept[:, 2].reshape(PEERS * 128, HEAD_SIZE)
+        scores = lax.dot_general(keys, queries, NT, preferred_element_type=jnp.float32) * SCALE
+        allowed = key_place[...] <= query_cap[j]
+        scores = jnp.where(allowed, scores, masked_logits)
+        highest = jnp.max(scores, axis=0, keepdims=True)
+        expo = jnp.exp(scores - highest)
+        total = jnp.sum(expo, axis=0, keepdims=True)
+        low = expo.astype(jnp.bfloat16)
+        turned_out = jnp.zeros((HEAD_SIZE, 256), jnp.float32)
+        for i in range(PEERS):
+            turned_out += jnp.dot(
+                vt[i], low[i * 128 : (i + 1) * 128], preferred_element_type=jnp.float32
+            )
+        turned_out = turned_out / total
+        kept_out[j] = turned_out
+        kept_log[j] = jnp.broadcast_to(highest + jnp.log(total), (8, 256))
+        attended = turned_out.T.astype(jnp.bfloat16).reshape(2, 128, HEAD_SIZE)
+
+        @pl.when(o == 0)
+        def home():
+            orecv[me] = attended
+
+        @pl.when(o > 0)
+        def away():
+            osend[j] = attended
+            out_copy(j, me).start()
+
+        return carry
+
+    lax.fori_loop(0, PEERS, block, 0)
+
+    def collect(o, carry):
+        h = (me + o) % PEERS
+
+        @pl.when(o > 0)
+        def arrived():
+            out_copy(me, h).wait_recv()
+
+        out[:, head_columns(0, 2 * h)] = orecv[h, 0]
+        out[:, head_columns(0, 2 * h + 1)] = orecv[h, 1]
+        return carry
+
+    lax.fori_loop(0, PEERS, collect, 0)
+
+    def drain(o, carry):
+        r = (me + o) % PEERS
+        key_copy(r, me).wait_send()
+        query_copy(r, me).wait_send()
+        out_copy(r, me).wait_send()
+        return carry
+
+    lax.fori_loop(1, PEERS, drain, 0)
+
+
+def attend(pre, cosine, sine, gains, key_place, query_cap, collective_id):
+    dma = pltpu.SemaphoreType.DMA
+    low, wide = jnp.bfloat16, jnp.float32
+    return pl.pallas_call(
+        attend_kernel,
+        out_shape=[
+            jax.ShapeDtypeStruct((128, 2048), low),
+            jax.ShapeDtypeStruct((PEERS, 4, 128, HEAD_SIZE), low),
+            jax.ShapeDtypeStruct((PEERS, HEAD_SIZE, 256), wide),
+            jax.ShapeDtypeStruct((PEERS, 8, 256), wide),
+        ],
+        in_specs=[pl.BlockSpec(memory_space=pltpu.VMEM)] * 6,
+        out_specs=[pl.BlockSpec(memory_space=pltpu.VMEM)] * 4,
+        scratch_shapes=[
+            pltpu.VMEM((PEERS, 4, 128, HEAD_SIZE), low),
+            pltpu.VMEM((PEERS, 2, 128, HEAD_SIZE), low),
+            pltpu.VMEM((PEERS, 2, 128, HEAD_SIZE), low),
+            pltpu.VMEM((PEERS, HEAD_SIZE, 128), low),
+        ]
+        + [dma((PEERS,))] * 6,
+        compiler_params=pltpu.CompilerParams(
+            collective_id=collective_id, has_side_effects=True, vmem_limit_bytes=40 * 2**20
+        ),
+        name="attend",
+    )(pre, cosine, sine, gains, key_place, query_cap)
+
+
+def attend_back_kernel(
+    upstream, kept, kept_out, kept_log, pre, cosine, sine, gains, key_place, query_cap,
+    out, gain_out,
+    dsend, drecv, qsend, qrecv, ksend, krecv, kt, key_sum, value_sum,
+    d_s, d_r, q_s, q_r, k_s, k_r,
+):
+    me, peer, remote, barrier = peer_tools()
+    cos = cosine[...]
+    sin = sine[...]
+
+    def grad_copy(r, slot):
+        return remote(dsend.at[r], drecv.at[slot], d_s.at[r], d_r.at[slot], peer(r))
+
+    def query_copy(r, slot):
+        return remote(qsend.at[r], qrecv.at[slot], q_s.at[r], q_r.at[slot], peer(r))
+
+    def key_copy(r, slot):
+        return remote(ksend.at[r], krecv.at[slot], k_s.at[r], k_r.at[slot], peer(r))
+
+    pl.semaphore_wait(barrier, PEERS - 1)
+
+    def push(o, carry):
+        r = (me + o) % PEERS
+        dsend[r, 0] = upstream[:, head_columns(0, 2 * r)]
+        dsend[r, 1] = upstream[:, head_columns(0, 2 * r + 1)]
+        grad_copy(r, me).start()
+        return carry
+
+    lax.fori_loop(1, PEERS, push, 0)
+    drecv[me, 0] = upstream[:, head_columns(0, 2 * me)]
+    drecv[me, 1] = upstream[:, head_columns(0, 2 * me + 1)]
+
+    def turn_keys(j, carry):
+        kt[j] = kept[j, 2].astype(jnp.float32).T.astype(jnp.bfloat16)
+        return carry
+
+    lax.fori_loop(0, PEERS, turn_keys, 0)
+    key_sum[...] = jnp.zeros_like(key_sum)
+    value_sum[...] = jnp.zeros_like(value_sum)
+
+    def block(o, carry):
+        j = (me + o) % PEERS
+
+        @pl.when(o > 0)
+        def arrived():
+            grad_copy(me, j).wait_recv()
+
+        grads = drecv[j].reshape(2 * 128, HEAD_SIZE)
+        delta = jnp.sum(grads.astype(jnp.float32).T * kept_out[j], axis=0, keepdims=True)
+        queries = kept[j, 0:2].reshape(2 * 128, HEAD_SIZE)
+        keys = kept[:, 2].reshape(PEERS * 128, HEAD_SIZE)
+        values = kept[:, 3].reshape(PEERS * 128, HEAD_SIZE)
+        scores = lax.dot_general(keys, queries, NT, preferred_element_type=jnp.float32) * SCALE
+        allowed = key_place[...] <= query_cap[j]
+        scores = jnp.where(allowed, scores, masked_logits)
+        prob = jnp.exp(scores - kept_log[j, 0:1, :])
+        dprob = lax.dot_general(values, grads, NT, preferred_element_type=jnp.float32)
+        dscore = (prob * (dprob - delta)).astype(jnp.bfloat16)
+        value_sum[...] += jnp.dot(
+            prob.astype(jnp.bfloat16), grads, preferred_element_type=jnp.float32
+        )
+        key_sum[...] += jnp.dot(dscore, queries, preferred_element_type=jnp.float32)
+        turned = jnp.zeros((HEAD_SIZE, 256), jnp.float32)
+        for i in range(PEERS):
+            turned += jnp.dot(
+                kt[i], dscore[i * 128 : (i + 1) * 128], preferred_element_type=jnp.float32
+            )
+        query_grad = (turned * SCALE).T.astype(jnp.bfloat16).reshape(2, 128, HEAD_SIZE)
+
+        @pl.when(o == 0)
+        def home():
+            qrecv[me] = query_grad
+
+        @pl.when(o > 0)
+        def away():
+            qsend[j] = query_grad
+            query_copy(j, me).start()
+
+        return carry
+
+    lax.fori_loop(0, PEERS, block, 0)
+
+    def push_keys(o, carry):
+        j = (me + o) % PEERS
+        rows = pl.ds(pl.multiple_of(j * 128, 128), 128)
+        key = (key_sum[rows, :] * SCALE).astype(jnp.bfloat16)
+        value = value_sum[rows, :].astype(jnp.bfloat16)
+
+        @pl.when(o < PEERS)
+        def away():
+            ksend[j, 0] = key
+            ksend[j, 1] = value
+            key_copy(j, me).start()
+
+        @pl.when(o == PEERS)
+        def home():
+            krecv[me, 0] = key
+            krecv[me, 1] = value
+
+        return carry
+
+    lax.fori_loop(1, PEERS + 1, push_keys, 0)
+
+    def back(grad, first, index, gain):
+        g = grad.astype(jnp.float32)
+        dy = g * cos - pltpu.roll(g, HEAD_SIZE // 2, 1) * sin
+        v = pre[:, head_columns(first, index)]
+        r = lax.rsqrt(jnp.mean(v * v, axis=-1, keepdims=True) + norm_epsilon)
+        u = dy * gain
+        result = r * u - v * (r * r * r) * jnp.mean(u * v, axis=-1, keepdims=True)
+        return result.astype(jnp.bfloat16), jnp.sum(dy * v * r, axis=0, keepdims=True)
+
+    def finish_queries(o, total):
+        h = (me + o) % PEERS
+
+        @pl.when(o > 0)
+        def arrived():
+            query_copy(me, h).wait_recv()
+
+        for i in range(2):
+            low, term = back(qrecv[h, i], 0, 2 * h + i, gains[0:1, :])
+            out[:, head_columns(0, 2 * h + i)] = low
+            total += term
+        return total
+
+    zero = jnp.zeros((1, HEAD_SIZE), jnp.float32)
+    query_total = lax.fori_loop(0, PEERS, finish_queries, zero)
+
+    def finish_keys(o, total):
+        h = (me + o) % PEERS
+
+        @pl.when(o > 0)
+        def arrived():
+            key_copy(me, h).wait_recv()
+
+        low, term = back(krecv[h, 0], 2048, h, gains[1:2, :])
+        out[:, head_columns(2048, h)] = low
+        out[:, head_columns(3072, h)] = krecv[h, 1]
+        return total + term
+
+    key_total = lax.fori_loop(0, PEERS, finish_keys, zero)
+    gain_out[...] = jnp.concatenate(
+        [query_total, key_total, jnp.zeros((6, HEAD_SIZE), jnp.float32)], axis=0
+    )
+
+    def drain(o, carry):
+        r = (me + o) % PEERS
+        grad_copy(r, me).wait_send()
+        query_copy(r, me).wait_send()
+        key_copy(r, me).wait_send()
+        return carry
+
+    lax.fori_loop(1, PEERS, drain, 0)
+
+
+def attend_back(
+    upstream, kept, kept_out, kept_log, pre, cosine, sine, gains, key_place, query_cap, collective_id
+):
+    dma = pltpu.SemaphoreType.DMA
+    low, wide = jnp.bfloat16, jnp.float32
+    pair = pltpu.VMEM((PEERS, 2, 128, HEAD_SIZE), low)
+    return pl.pallas_call(
+        attend_back_kernel,
+        out_shape=[
+            jax.ShapeDtypeStruct((128, 4096), low),
+            jax.ShapeDtypeStruct((8, HEAD_SIZE), wide),
+        ],
+        in_specs=[pl.BlockSpec(memory_space=pltpu.VMEM)] * 10,
+        out_specs=[pl.BlockSpec(memory_space=pltpu.VMEM)] * 2,
+        scratch_shapes=[pair] * 6
+        + [
+            pltpu.VMEM((PEERS, HEAD_SIZE, 128), low),
+            pltpu.VMEM((PEERS * 128, HEAD_SIZE), wide),
+            pltpu.VMEM((PEERS * 128, HEAD_SIZE), wide),
+        ]
+        + [dma((PEERS,))] * 6,
+        compiler_params=pltpu.CompilerParams(
+            collective_id=collective_id, has_side_effects=True, vmem_limit_bytes=48 * 2**20
+        ),
+        name="attend_back",
+    )(upstream, kept, kept_out, kept_log, pre, cosine, sine, gains, key_place, query_cap)
 
 
 def from_partner(shard, axis, apart):
@@ -526,7 +1078,7 @@
     }
 
 
-def per_device(
+def general_device(
     tokens,
     cotangent,
     lengths,
@@ -628,6 +1180,9 @@
         )
         gathered, key_all, value_all, present_inputs, rest = kept
         ffn_grad_low = grad_stream.astype(jnp.bfloat16)
+        grad_down = jnp.einsum(
+            "tf,td->fd", rest["hidden_low"], ffn_grad_low, preferred_element_type=jnp.float32
+        )
         hidden_grad = jnp.einsum(
             "td,fd->tf", ffn_grad_low, gathered[6], preferred_element_type=jnp.float32
         )
@@ -637,6 +1192,12 @@
             hidden_grad * rest["upward"] * sigmoid_gate * (1.0 + gate_act * (1.0 - sigmoid_gate))
         ).astype(jnp.bfloat16)
         up_grad_low = (hidden_grad * gate_act * sigmoid_gate).astype(jnp.bfloat16)
+        grad_gate = jnp.einsum(
+            "td,tf->df", rest["normed_mid_low"], gate_grad_low, preferred_element_type=jnp.float32
+        )
+        grad_up = jnp.einsum(
+            "td,tf->df", rest["normed_mid_low"], up_grad_low, preferred_element_type=jnp.float32
+        )
         normed_mid_grad = jnp.einsum(
             "tf,df->td", gate_grad_low, gathered[4], preferred_element_type=jnp.float32
         ) + jnp.einsum("tf,df->td", up_grad_low, gathered[5], preferred_element_type=jnp.float32)
@@ -645,6 +1206,9 @@
         )
         middle_grad = grad_stream + mid_norm_grad
         attn_grad_low = middle_grad.astype(jnp.bfloat16)
+        grad_out = jnp.einsum(
+            "tq,td->qd", attn_low, attn_grad_low, preferred_element_type=jnp.float32
+        )
         output_gradient_lowered = jnp.einsum(
             "td,qd->tq", attn_grad_low, gathered[3], preferred_element_type=jnp.float32
         ).astype(jnp.bfloat16)
@@ -731,6 +1295,15 @@
         query_grad_low = query_pre.reshape(count_rows, QUERY_HEADS * HEAD_SIZE).astype(jnp.bfloat16)
         key_grad_low = key_pre.reshape(count_rows, key_value_width).astype(jnp.bfloat16)
         normed_low = present_inputs["normed_low"]
+        grad_query = jnp.einsum(
+            "td,tq->dq", normed_low, query_grad_low, preferred_element_type=jnp.float32
+        )
+        grad_key = jnp.einsum(
+            "td,tq->dq", normed_low, key_grad_low, preferred_element_type=jnp.float32
+        )
+        grad_value = jnp.einsum(
+            "td,tq->dq", normed_low, value_grad_low, preferred_element_type=jnp.float32
+        )
         normed_grad = jnp.einsum(
             "tq,dq->td", query_grad_low, gathered[0], preferred_element_type=jnp.float32
         )
@@ -744,54 +1317,189 @@
             stream_in, present_inputs["inv_attn"], gathered[7].astype(jnp.float32), normed_grad
         )
         grad_stream = middle_grad + in_norm_grad
-        gain_sums = tuple(
-            (
-                lax.psum_scatter(term, ("ctx", "fsdp"), scatter_dimension=0, tiled=True)
-                for term in (attn_gain_term, mlp_gain_term, query_gain_term, key_gain_term)
-            )
-        )
-        if half_count == KEY_VALUE_HEADS:
-            weight_sums = reduce_weights(
-                (rest["hidden_low"], attn_low, rest["normed_mid_low"], normed_low),
-                (
-                    ffn_grad_low,
-                    attn_grad_low,
-                    gate_grad_low,
-                    up_grad_low,
-                    query_grad_low,
-                    key_grad_low,
-                    value_grad_low,
-                ),
-                layer_index + 1,
-            )
-        else:
-            weight_sums = tuple(
-                (
-                    lax.psum_scatter(
-                        jnp.einsum("td,tq->dq", left, right, preferred_element_type=jnp.float32),
-                        ("ctx", "fsdp"),
-                        scatter_dimension=0,
-                        tiled=True,
-                    )
-                    for left, right in (
-                        (normed_low, query_grad_low),
-                        (normed_low, key_grad_low),
-                        (normed_low, value_grad_low),
-                        (attn_low, attn_grad_low),
-                        (rest["normed_mid_low"], gate_grad_low),
-                        (rest["normed_mid_low"], up_grad_low),
-                        (rest["hidden_low"], ffn_grad_low),
-                    )
-                )
-            )
-        layer_grads[layer_index] = weight_sums + gain_sums
+        layer_grads[layer_index] = (
+            lax.psum_scatter(grad_query, ("ctx", "fsdp"), scatter_dimension=0, tiled=True),
+            lax.psum_scatter(grad_key, ("ctx", "fsdp"), scatter_dimension=0, tiled=True),
+            lax.psum_scatter(grad_value, ("ctx", "fsdp"), scatter_dimension=0, tiled=True),
+            lax.psum_scatter(grad_out, ("ctx", "fsdp"), scatter_dimension=0, tiled=True),
+            lax.psum_scatter(grad_gate, ("ctx", "fsdp"), scatter_dimension=0, tiled=True),
+            lax.psum_scatter(grad_up, ("ctx", "fsdp"), scatter_dimension=0, tiled=True),
+            lax.psum_scatter(grad_down, ("ctx", "fsdp"), scatter_dimension=0, tiled=True),
+            lax.psum_scatter(attn_gain_term, ("ctx", "fsdp"), scatter_dimension=0, tiled=True),
+            lax.psum_scatter(mlp_gain_term, ("ctx", "fsdp"), scatter_dimension=0, tiled=True),
+            lax.psum_scatter(query_gain_term, ("ctx", "fsdp"), scatter_dimension=0, tiled=True),
+            lax.psum_scatter(key_gain_term, ("ctx", "fsdp"), scatter_dimension=0, tiled=True),
+        )
     stacked = tuple(
         (jnp.stack([layer_sums[member] for layer_sums in layer_grads]) for member in range(11))
     )
     return (output_low, grad_stream) + stacked
 
 
+def act_blocks(values):
+    turned = values.T.reshape(4, 2, 2, 2, -1, 32, values.shape[0])
+    return turned.transpose(3, 2, 4, 1, 0, 5, 6).reshape(2, 2, -1, 256, values.shape[0])
+
+
+def grad_blocks(values):
+    return values.reshape(values.shape[0], -1, 1024).transpose(1, 0, 2)
+
+
+def side_by_side(tiles):
+    return tiles.transpose(1, 0, 2).reshape(tiles.shape[1], -1)
+
+
+def product(left, right):
+    return jnp.dot(left, right, preferred_element_type=jnp.float32)
+
+
+def product_turned(left, right):
+    return lax.dot_general(left, right, NT, preferred_element_type=jnp.float32)
+
+
+def fast_device(
+    tokens,
+    cotangent,
+    lengths,
+    stretch_ids,
+    w_query,
+    key_projection_weight,
+    value_projection_weight,
+    w_out,
+    w_gate,
+    w_up,
+    w_down,
+    g_attn,
+    g_mlp,
+    g_query,
+    g_key,
+):
+    count_rows, width = tokens.shape
+    ctx_index = lax.axis_index("ctx")
+    places, slot_ids, live = token_places(stretch_ids[:, 0, :], lengths[0])
+    group_rows = PEERS * count_rows
+    base_row = ctx_index // PEERS * group_rows
+    my_row = ctx_index * count_rows
+    slot_places = lax.dynamic_slice_in_dim(places, base_row, group_rows)
+    limit = lax.dynamic_slice_in_dim(lengths[0], ctx_index // PEERS, 1)
+    caps = jnp.minimum(slot_places, limit - 1).reshape(PEERS, 1, count_rows)
+    query_cap = jnp.concatenate([caps, caps], axis=2)
+    key_place = slot_places[:, None]
+    live_mine = lax.dynamic_slice_in_dim(live, my_row, count_rows).astype(jnp.float32)[:, None]
+    cosine, sine = rotary_tables(lax.dynamic_slice_in_dim(places, my_row, count_rows))
+    half = HEAD_SIZE // 2
+    sine = jnp.concatenate([-sine[:, :half], sine[:, half:]], axis=1)
+
+    packed = jnp.concatenate([member.reshape(-1) for member in (g_attn, g_mlp, g_query, g_key)])
+    packed = jnp.pad(packed, (0, 4096 - packed.shape[0])).reshape(32, 128)
+    gathered = gather_weights(
+        (w_query, key_projection_weight, value_projection_weight, w_out, w_gate, w_up, w_down),
+        packed,
+        tuple(range(DECODER_LAYERS)),
+        1,
+    )
+    flat = gathered[-1].reshape(2, -1).astype(jnp.float32)
+    gains = []
+    offset = 0
+    for member in (g_attn, g_mlp, g_query, g_key):
+        span = member.shape[1]
+        sides = flat[:, offset : offset + DECODER_LAYERS * span].reshape(2, DECODER_LAYERS, span)
+        gains.append(sides.transpose(1, 0, 2).reshape(DECODER_LAYERS, 2 * span))
+        offset += DECODER_LAYERS * span
+
+    stream = tokens.astype(jnp.float32)
+    saved = []
+    for layer in range(DECODER_LAYERS):
+        into, out_weight, wide_weight, down = gathered[4 * layer : 4 * layer + 4]
+        head_gains = jnp.concatenate([gains[2][layer : layer + 1], gains[3][layer : layer + 1]], 0)
+        normed, inv_attn = norm_forward(stream, gains[0][layer])
+        normed_low = normed.astype(jnp.bfloat16)
+        pre = product(normed_low, into)
+        attn_low, kept, kept_out, kept_log = attend(
+            pre, cosine, sine, head_gains, key_place, query_cap, 2 + layer
+        )
+        middle = stream + product(attn_low, out_weight)
+        normed_mid, inv_mid = norm_forward(middle, gains[1][layer])
+        mid_low = normed_mid.astype(jnp.bfloat16)
+        both = product(mid_low, wide_weight)
+        ff = both.shape[1] // 2
+        gate, up = both[:, :ff], both[:, ff:]
+        hidden_low = (jax.nn.silu(gate) * up).astype(jnp.bfloat16)
+        saved.append(
+            (stream, inv_attn, normed_low, pre, attn_low, kept, kept_out, kept_log,
+             middle, inv_mid, mid_low, gate, up, hidden_low, head_gains)
+        )
+        stream = middle + product(hidden_low, down)
+    output_low = (stream * live_mine).astype(jnp.bfloat16)
+
+    grad_stream = cotangent.astype(jnp.float32) * live_mine
+    layer_grads = [None] * DECODER_LAYERS
+    place = ctx_index * 2 + lax.axis_index("fsdp")
+    for layer in reversed(range(DECODER_LAYERS)):
+        into, out_weight, wide_weight, down = gathered[4 * layer : 4 * layer + 4]
+        (stream_in, inv_attn, normed_low, pre, attn_low, kept, kept_out, kept_log,
+         middle, inv_mid, mid_low, gate, up, hidden_low, head_gains) = saved[layer]
+        down_low = grad_stream.astype(jnp.bfloat16)
+        hidden_grad = product_turned(down_low, down)
+        sigmoid_gate = jax.nn.sigmoid(gate)
+        gate_low = (hidden_grad * up * sigmoid_gate * (1.0 + gate * (1.0 - sigmoid_gate))).astype(
+            jnp.bfloat16
+        )
+        up_low = (hidden_grad * gate * sigmoid_gate).astype(jnp.bfloat16)
+        both_low = jnp.concatenate([gate_low, up_low], axis=1)
+        mid_grad = product_turned(both_low, wide_weight)
+        mid_norm_grad, mlp_term = norm_backward(middle, inv_mid, gains[1][layer], mid_grad)
+        middle_grad = grad_stream + mid_norm_grad
+        out_low = middle_grad.astype(jnp.bfloat16)
+        attn_grad = product_turned(out_low, out_weight).astype(jnp.bfloat16)
+        pre_grad, head_terms = attend_back(
+            attn_grad, kept, kept_out, kept_log, pre, cosine, sine, head_gains,
+            key_place, query_cap, 2 + DECODER_LAYERS + layer,
+        )
+        normed_grad = product_turned(pre_grad, into)
+        in_norm_grad, attn_term = norm_backward(stream_in, inv_attn, gains[0][layer], normed_grad)
+        grad_stream = middle_grad + in_norm_grad
+        terms = jnp.concatenate(
+            [attn_term.reshape(-1, 128), mlp_term.reshape(-1, 128), head_terms], axis=0
+        )
+        tiles, sums = reduce_layer(
+            jnp.concatenate(
+                [act_blocks(member) for member in (hidden_low, attn_low, mid_low, normed_low)],
+                axis=2,
+            ),
+            jnp.concatenate(
+                [grad_blocks(member) for member in (down_low, out_low, both_low, pre_grad)], axis=0
+            ),
+            terms,
+            2 + 2 * DECODER_LAYERS + layer,
+        )
+
+        def share(first, rows, span):
+            flat_sum = sums[first : first + rows].reshape(-1)
+            return lax.dynamic_slice_in_dim(flat_sum, place * span, span)
+
+        layer_grads[layer] = (
+            side_by_side(tiles[11:13]),
+            tiles[13],
+            tiles[14],
+            tiles[3:5].reshape(64, 1024),
+            side_by_side(tiles[5:8]),
+            side_by_side(tiles[8:11]),
+            tiles[0:3].reshape(96, 1024),
+            share(0, 8, 32),
+            share(8, 8, 32),
+            share(16, 1, 4),
+            share(17, 1, 4),
+        )
+    stacked = tuple(
+        (jnp.stack([layer_sums[member] for layer_sums in layer_grads]) for member in range(11))
+    )
+    return (output_low, grad_stream) + stacked
+
+
 def solution(mesh):
+    plain = mesh.shape["ctx"] == 2 * KEY_VALUE_HEADS and mesh.shape["fsdp"] == 2
+    device = fast_device if plain else general_device
     in_specs = (
         P(("ctx", "fsdp"), None),
         P(("ctx", "fsdp"), None),
@@ -825,5 +1533,5 @@
         P(None, ("ctx", "fsdp")),
     )
     return jax.shard_map(
-        per_device, mesh=mesh, in_specs=in_specs, out_specs=out_specs, check_vma=False
-    )
+        device, mesh=mesh, in_specs=in_specs, out_specs=out_specs, check_vma=False
+    )

time: 1740 us -> 661 us (0.38)
  waiting for transfers between devices: 801 us -> 0 us
  Pallas kernels: 248 us -> 488 us
  local copies, waits for them, and re-layouts: 273 us -> 44.4 us
  other arithmetic: 139 us -> 32.9 us
  matrix products: 162 us -> 83.1 us
  blocking collectives: 65.7 us -> 0 us
    all_gather x14 -> x0, waiting for transfers between devices: 564 us -> none  [the longest x2 157 us: per_device(): lax.all_gather(w_up[layer_index], 'fsdp', axis=0, tiled=True)]
    pallas_call x2 -> x7, Pallas kernels: 248 us -> 488 us  [the longest x2 238 us: reduce_layer(): pl.pallas_call(rs_kernel, out_shape=[jax.ShapeDtypeStruct((TILES, 32, 102...]
    ppermute x12 -> x0, waiting for transfers between devices: 234 us -> none  [from_partner(): lax.ppermute(shard, axis, [(i, i ^ 1 << apart) for i in range(lax.axis_si...]
    dot_general x56 -> x16, matrix products: 162 us -> 83.1 us  [the longest x8 47.7 us: product_turned(): return lax.dot_general(left, right, NT, preferred_element_type=jnp.float32)]
    unnamed x2 -> x0, blocking collectives: 46.7 us -> none
    dynamic_update_slice x8 -> x0, local copies, waits for them, and re-layouts: 41.1 us -> none  [per_device(): lax.scan(backward_step, jnp.zeros((count_rows, KEY_VALUE_HEADS, group_cou...]
    slice x19 -> x17, local copies, waits for them, and re-layouts: 43.9 us -> 3.45 us  [the longest x2 1.11 us: fast_device(): tiles[3:5].reshape(64, 1024)]
    dynamic_slice x41 -> x4, local copies, waits for them, and re-layouts: 38.5 us -> 0.29 us  [share(): return lax.dynamic_slice_in_dim(flat_sum, place * span, span)]
  transfers between devices with their start and end apart: 26 -> 0, of which waited for: 20 -> 0; matrix products, arithmetic and copies ran while one was open for 18% -> 0% of each run, Pallas kernels for 8% -> 0%
where the time goes in v2:
time: 661 us; the launch traced here: 652 us
  Pallas kernels  488 us (74%)
  matrix products  83.1 us (13%)
  local copies, waits for them, and re-layouts  44.4 us (7%)
  other arithmetic  32.9 us (5%)
    pallas_call x2, Pallas kernels, reduce_layer(): pl.pallas_call(rs_kernel, out_shape=[jax.ShapeDtypeStruct((TILES, 32, 102...  238 us
    pallas_call x1, Pallas kernels, gather_weights(): pl.pallas_call(functools.partial(gather_kernel, layers), out_shape=[jax.S...  143 us
    pallas_call x2, Pallas kernels, attend_back(): pl.pallas_call(attend_back_kernel, out_shape=[jax.ShapeDtypeStruct((128,...  55.6 us
    pallas_call x2, Pallas kernels, attend(): pl.pallas_call(attend_kernel, out_shape=[jax.ShapeDtypeStruct((128, 2048)...  51.1 us
    dot_general x8, matrix products, product_turned(): return lax.dot_general(left, right, NT, preferred_element_type=jnp.float32)  47.7 us
    dot_general x8, matrix products, product(): return jnp.dot(left, right, preferred_element_type=jnp.float32)  35.4 us

profile of v2, /device:TPU:0, one launch (start us, length us, event | category | flops | bytes accessed | tf_op | source)
XLA Modules:
  0.0 651.5 jit_solution(14805032806670706047)
XLA Ops:
  9.2 143.4 %weight_gather.1 = (bf16[1024,4096]{1,0:T(8,128)(2,1)}, bf16[2048,1024]{1,0:T(8,128)(2,1)}, bf16[1024,6144]{1,0:T(8,128)(2,1)}, bf16[3072,1024]{1,0:T(8,128)(2,1...) custom-call(bf16[2,512,2048]{2,1,0:T(8,128)(2,1)} %refs_0_.1, ...), custom_call_target="tpu_custom_call" | custom-call | tf_op jit(solution)/shard_map/weight_gather/pallas_call | solution.py:462
  153.9 4.8 fusion.20.pre
  158.8 25.0 %attend.2 = (bf16[128,2048]{1,0:T(8,128)(2,1)S(1)}, bf16[8,4,128,128]{3,2,1,0:T(8,128)(2,1)S(1)}, f32[8,128,256]{2,1,0:T(8,128)S(1)}, f32[8,8,256]{2,1,0:T(8,128)S(1)}) custom-call(f32[128,4096]{1,0:T(8,128)S(1)} %fusion.20.pre, f32[128,128]{1,0:T(8,128)S(1)} %get-tuple-element.150.cosine, f32[128,128]{1,0:T(8,128)S(1)} %get-tuple-element.151.sine, ...), custom_call_target="tpu_custom_call" | custom-call | tf_op jit(solution)/shard_map/attend/pallas_call | solution.py:658
  185.4 6.6 %fusion.33 = f32[128,6144]{1,0:T(8,128)S(1)} fusion(bf16[1024,6144]{1,0:T(8,128)(2,1)} %get-tuple-element.42, f32[128,1024]{1,0:T(8,128)S(1)} %get-tuple-element.141, f32[1024]{0:T(1024)S(1)} %bitcast.188, f32[128]{0:T(128)S(1)} %get-tuple-element.130), kind=kOutput, calls=%fused_computation.144 | convolution fusion | flops 1611005952 | bytes 16257536 | tf_op jit(solution)/shard_map/dot_general | solution.py:1353
  192.0 5.2 multiply_reduce_fusion.7
  198.8 26.1 %attend.3 = (bf16[128,2048]{1,0:T(8,128)(2,1)S(1)}, bf16[8,4,128,128]{3,2,1,0:T(8,128)(2,1)S(1)}, f32[8,128,256]{2,1,0:T(8,128)S(1)}, f32[8,8,256]{2,1,0:T(8,128)S(1)}) custom-call(f32[128,4096]{1,0:T(8,128)S(1)} %fusion.35.pre, f32[128,128]{1,0:T(8,128)S(1)} %get-tuple-element.150.cosine, f32[128,128]{1,0:T(8,128)S(1)} %get-tuple-element.151.sine, ...), custom_call_target="tpu_custom_call" | custom-call | tf_op jit(solution)/shard_map/attend/pallas_call | solution.py:658
  225.0 3.7 multiply_reduce_fusion.6
  228.8 8.3 %fusion.37 = f32[128,6144]{1,0:T(8,128)} fusion(bf16[1024,6144]{1,0:T(8,128)(2,1)} %get-tuple-element.47, f32[128,1024]{1,0:T(8,128)S(1)} %get-tuple-element.145, f32[1024]{0:T(1024)S(1)} %bitcast.191, f32[128]{0:T(128)S(1)} %get-tuple-element.134), kind=kOutput, calls=%fused_computation.148 | convolution fusion | flops 1611005952 | bytes 16257536 | tf_op jit(solution)/shard_map/dot_general | solution.py:1353
  237.3 7.2 %multiply_convert_fusion.3 = (bf16[128,3072]{1,0:T(8,128)(2,1)S(1)}, bf16[128,3072]{1,0:T(8,128)(2,1)S(1)}, bf16[128,3072]{1,0:T(8,128)(2,1)}) fusion(f32[128,6144]{1,0:T(8,128)} %fusion.37, bf16[3072,1024]{1,0:T(8,128)(2,1)} %get-tuple-element.48, bf16[128,1024]{1,0:T(8,128)(2,1)S(1)} %copy-done.46, f32[128]{0:T(128)S(1)} %compare_convert_fusion), kind=kOutput, calls=%fused_computation.11 | convolution fusion | flops 811991040 | bytes 12059136 | tf_op jit(solution)/shard_map/dot_general | solution.py:1357
  244.6 9.5 %multiply_reduce_fusion = (f32[1024]{0:T(1024)S(1)}, f32[128]{0:T(128)S(1)}, f32[128,1024]{1,0:T(8,128)S(1)}) fusion(f32[128,1024]{1,0:T(8,128)S(1)} %copy-done.18, f32[128]{0:T(128)S(1)} %get-tuple-element.134, f32[1024]{0:T(1024)S(1)} %bitcast.192, bf16[1024,6144]{1,0:T(8,128)(2,1)} %get-tuple-element.47, bf16[128,3072]{1,0:T(8,128)(2,1)S(1)} %get-tuple-element.86, ...), kind=kOutput, calls=%fused_computation.41 | convolution fusion | flops 1614543744 | bytes 15213568 | tf_op jit(solution)/shard_map/dot_general | solution.py:1357
  255.2 3.8 convolution_convert_fusion.1.upstream
  259.1 27.2 %attend_back.2 = (bf16[128,4096]{1,0:T(8,128)(2,1)S(1)}, f32[8,128]{1,0:T(8,128)S(1)}) custom-call(bf16[128,2048]{1,0:T(8,128)(2,1)S(1)} %convolution_convert_fusion.1.upstream, bf16[8,4,128,128]{3,2,1,0:T(8,128)(2,1)S(1)} %copy-done.13, f32[8,128,256]{2,1,0:T(8,128)S(1)} %copy-done.15, f32[8,8,256]{2,1,0:T(8,128)S(1)} %get-tuple-element.51.kept_log, ...), custom_call_target="tpu_custom_call" | custom-call | tf_op jit(solution)/shard_map/attend_back/pallas_call | solution.py:843
  286.3 3.0 multiply_reduce_fusion.1
  290.4 6.5 multiply_convert_fusion.1
  296.9 10.0 %multiply_reduce_fusion.2 = (f32[1024]{0:T(1024)S(1)}, f32[128]{0:T(128)S(1)}, f32[128,1024]{1,0:T(8,128)}) fusion(f32[128,1024]{1,0:T(8,128)S(1)} %copy-done.26, f32[128]{0:T(128)S(1)} %get-tuple-element.130, f32[1024]{0:T(1024)S(1)} %bitcast.189, bf16[1024,6144]{1,0:T(8,128)(2,1)} %get-tuple-element.42, bf16[128,3072]{1,0:T(8,128)(2,1)} %get-tuple-element.84, ...), kind=kOutput, calls=%fused_computation.43 | convolution fusion | flops 1614543744 | bytes 15213568 | tf_op jit(solution)/shard_map/dot_general | solution.py:1357
  309.1 3.9 convolution_convert_fusion.upstream
  313.1 28.5 %attend_back.3 = (bf16[128,4096]{1,0:T(8,128)(2,1)S(1)}, f32[8,128]{1,0:T(8,128)S(1)}) custom-call(bf16[128,2048]{1,0:T(8,128)(2,1)S(1)} %convolution_convert_fusion.upstream, bf16[8,4,128,128]{3,2,1,0:T(8,128)(2,1)S(1)} %copy-done.9, f32[8,128,256]{2,1,0:T(8,128)S(1)} %copy-done.11, f32[8,8,256]{2,1,0:T(8,128)S(1)} %get-tuple-element.55.kept_log, ...), custom_call_target="tpu_custom_call" | custom-call | tf_op jit(solution)/shard_map/attend_back/pallas_call | solution.py:843
  341.6 3.7 fusion.10
  346.6 2.6 copy.50
  349.2 2.6 copy.51
  353.1 2.3 copy.53
  355.4 3.2 pad_maximum_fusion.grads
  361.1 3.2 fusion.75
  364.3 2.4 copy.42
  370.5 119.2 %weight_gradient_reduce.2 = (f32[15,32,1024]{2,1,0:T(8,128)S(1)}, f32[24,128]{1,0:T(8,128)S(1)}) custom-call(bf16[2,2,7,256,128]{4,3,2,1,0:T(8,128)(2,1)S(1)} %pad_maximum_fusion.2.acts, bf16[12,128,1024]{2,1,0:T(8,128)(2,1)} %pad_maximum_fusion.grads, f32[24,128]{1,0:T(8,128)S(1)} %pad_maximum_fusion.15.gains), custom_call_target="tpu_custom_call" | custom-call | tf_op jit(solution)/shard_map/weight_gradient_reduce/pallas_call | solution.py:293
  491.1 2.4 pad_maximum_fusion.4
  493.5 2.6 copy.63
  496.0 2.6 copy.64
  499.9 2.4 copy.66
  502.4 2.9 pad_maximum_fusion.1.grads
  507.5 119.1 %weight_gradient_reduce.3 = (f32[15,32,1024]{2,1,0:T(8,128)S(1)}, f32[24,128]{1,0:T(8,128)S(1)}) custom-call(bf16[2,2,7,256,128]{4,3,2,1,0:T(8,128)(2,1)S(1)} %pad_maximum_fusion.3.acts, bf16[12,128,1024]{2,1,0:T(8,128)(2,1)} %pad_maximum_fusion.1.grads, f32[24,128]{1,0:T(8,128)S(1)} %pad_maximum_fusion.16.gains), custom_call_target="tpu_custom_call" | custom-call | tf_op jit(solution)/shard_map/weight_gradient_reduce/pallas_call | solution.py:293
  646.6 4.5 fusion.1
  (225 shorter events, 50.5 us)
Async XLA Ops:
  9.2 144.5 %copy-start.27 = (bf16[128,1024]{1,0:T(8,128)(2,1)S(1)}, bf16[128,1024]{1,0:T(8,128)(2,1)}, u32[]{:S(2)}) copy-start(bf16[128,1024]{1,0:T(8,128)(2,1)} %param.15) | copy-start | bytes 786436
  153.9 29.9 %copy-start.16 = (bf16[2048,1024]{1,0:T(8,128)(2,1)S(1)}, bf16[2048,1024]{1,0:T(8,128)(2,1)}, u32[]{:S(2)}) copy-start(bf16[2048,1024]{1,0:T(8,128)(2,1)} %get-tuple-element.41) | copy-start | bytes 12582916
  158.8 25.9 %copy-start.1 = (f32[128,4096]{1,0:T(8,128)}, f32[128,4096]{1,0:T(8,128)S(1)}, u32[]{:S(2)}) copy-start(f32[128,4096]{1,0:T(8,128)S(1)} %fusion.20.pre) | copy-start | bytes 6291460
  185.3 6.7 %copy-start.25 = (f32[128,1024]{1,0:T(8,128)}, f32[128,1024]{1,0:T(8,128)S(1)}, u32[]{:S(2)}) copy-start(f32[128,1024]{1,0:T(8,128)S(1)} %get-tuple-element.141) | copy-start | bytes 1572868
  185.4 11.9 %slice-start.2 = ((s8[8388608]{0:T(1024)(128)(4,1)}), s8[4194304]{0:T(1024)(128)(4,1)S(1)}, s32[]{:S(2)}) async-start(s8[8388608]{0:T(1024)(128)(4,1)} %bitcast.149), calls=%async_computation.2 | async-start | bytes 8388608
  185.4 11.9 %slice-start.3 = ((s8[8388608]{0:T(1024)(128)(4,1)}), s8[4194304]{0:T(1024)(128)(4,1)S(1)}, s32[]{:S(2)}) async-start(s8[8388608]{0:T(1024)(128)(4,1)} %bitcast.149), calls=%async_computation.3 | async-start | bytes 8388608
  192.0 5.2 copy-start.20
  198.6 30.0 %copy-start = (f32[128,4096]{1,0:T(8,128)}, f32[128,4096]{1,0:T(8,128)S(1)}, u32[]{:S(2)}) copy-start(f32[128,4096]{1,0:T(8,128)S(1)} %fusion.35.pre) | copy-start | bytes 6291460
  198.8 26.1 %copy-start.23 = (f32[128,1024]{1,0:T(8,128)S(1)}, f32[128,1024]{1,0:T(8,128)}, u32[]{:S(2)}) copy-start(f32[128,1024]{1,0:T(8,128)} %copy-done.22) | copy-start | bytes 1572868
  224.9 3.8 copy-start.12
  228.7 8.3 %copy-start.17 = (f32[128,1024]{1,0:T(8,128)}, f32[128,1024]{1,0:T(8,128)S(1)}, u32[]{:S(2)}) copy-start(f32[128,1024]{1,0:T(8,128)S(1)} %get-tuple-element.145) | copy-start | bytes 1572868
  228.7 8.5 %copy-start.46 = (bf16[128,1024]{1,0:T(8,128)(2,1)S(1)}, bf16[128,1024]{1,0:T(8,128)(2,1)}, u32[]{:S(2)}) copy-start(bf16[128,1024]{1,0:T(8,128)(2,1)} %param.16) | copy-start | bytes 786436
  237.3 7.3 %copy-start.18 = (f32[128,1024]{1,0:T(8,128)S(1)}, f32[128,1024]{1,0:T(8,128)}, u32[]{:S(2)}) copy-start(f32[128,1024]{1,0:T(8,128)} %copy-done.17) | copy-start | bytes 1572868
  237.3 49.0 %slice-start.4 = ((s8[8388608]{0:T(1024)(128)(4,1)}), s8[4194304]{0:T(1024)(128)(4,1)S(1)}, s32[]{:S(2)}) async-start(s8[8388608]{0:T(1024)(128)(4,1)} %bitcast.151), calls=%async_computation.4 | async-start | bytes 8388608
  244.5 9.5 %copy-start.33 = (bf16[128,3072]{1,0:T(8,128)(2,1)}, bf16[128,3072]{1,0:T(8,128)(2,1)S(1)}, u32[]{:S(2)}) copy-start(bf16[128,3072]{1,0:T(8,128)(2,1)S(1)} %get-tuple-element.85) | copy-start | bytes 2359300
  244.5 9.5 %copy-start.35 = (bf16[128,3072]{1,0:T(8,128)(2,1)}, bf16[128,3072]{1,0:T(8,128)(2,1)S(1)}, u32[]{:S(2)}) copy-start(bf16[128,3072]{1,0:T(8,128)(2,1)S(1)} %get-tuple-element.86) | copy-start | bytes 2359300
  244.5 41.7 %slice-start.5 = ((s8[8388608]{0:T(1024)(128)(4,1)}), s8[4194304]{0:T(1024)(128)(4,1)S(1)}, s32[]{:S(2)}) async-start(s8[8388608]{0:T(1024)(128)(4,1)} %bitcast.151), calls=%async_computation.5 | async-start | bytes 8388608
  255.2 3.9 copy-start.13
  255.2 3.9 copy-start.15
  259.1 27.2 %copy-start.24 = (f32[128,1024]{1,0:T(8,128)S(1)}, f32[128,1024]{1,0:T(8,128)}, u32[]{:S(2)}) copy-start(f32[128,1024]{1,0:T(8,128)} %copy-done.22) | copy-start | bytes 1572868
  286.3 4.1 copy-start.21
  290.4 6.5 copy-start.40
  290.4 6.5 copy-start.26
  290.4 51.2 %slice-start = ((s8[8388608]{0:T(1024)(128)(4,1)}), s8[4194304]{0:T(1024)(128)(4,1)S(1)}, s32[]{:S(2)}) async-start(s8[8388608]{0:T(1024)(128)(4,1)} %bitcast.147), calls=%async_computation | async-start | bytes 8388608
  296.8 44.7 %slice-start.1 = ((s8[8388608]{0:T(1024)(128)(4,1)}), s8[4194304]{0:T(1024)(128)(4,1)S(1)}, s32[]{:S(2)}) async-start(s8[8388608]{0:T(1024)(128)(4,1)} %bitcast.147), calls=%async_computation.1 | async-start | bytes 8388608
  309.1 3.9 copy-start.31
  309.1 4.0 copy-start.9
  309.1 4.0 copy-start.11
  313.1 28.5 %copy-start.28 = (bf16[128,1024]{1,0:T(8,128)(2,1)S(1)}, bf16[128,1024]{1,0:T(8,128)(2,1)}, u32[]{:S(2)}) copy-start(bf16[128,1024]{1,0:T(8,128)(2,1)} %param.15) | copy-start | bytes 786436
  364.3 4.5 copy-start.3
  370.5 120.6 %copy-start.34 = (bf16[128,3072]{1,0:T(8,128)(2,1)S(1)}, bf16[128,3072]{1,0:T(8,128)(2,1)}, u32[]{:S(2)}) copy-start(bf16[128,3072]{1,0:T(8,128)(2,1)} %copy-done.33) | copy-start | bytes 2359300
  507.5 123.3 %copy-start.5 = (f32[15,32,1024]{2,1,0:T(8,128)S(1)}, f32[15,32,1024]{2,1,0:T(8,128)}, u32[]{:S(2)}) copy-start(f32[15,32,1024]{2,1,0:T(8,128)} %copy-done.4) | copy-start | bytes 5898244
  (21 other events, 53.2 us)

commit v3 on v2

--- a/solution.py
+++ b/solution.py
@@ -21,306 +21,447 @@
 
 MESH = pl.DeviceIdType.MESH
 
+
 TILES = 15
 GRADS = 12
+ACTS = 7
 AHEAD = 3
+ACT_SPANS = ((0, 3), (3, 1), (4, 2), (6, 1))
 
 
 def grad_index(t):
-    return jnp.maximum(t - 3, jnp.where(t < 3, 0, 1))
+    return jnp.where(t < 3, 0, jnp.where(t < 9, t - 2, jnp.where(t < 11, 7, t - 3)))
 
 
 def act_index(t):
-    return jnp.minimum(t, 5) + jnp.where(t >= 11, 1, 0)
+    return jnp.where(t < 3, t, jnp.where(t < 9, 3, jnp.where(t < 11, t - 5, 6)))
 
 
 def is_new(t):
-    return (t == 0) | (t == 3) | ((t >= 5) & (t < TILES))
-
-
-def rs_kernel(
-    acts, grads, gains, out, gain_out, abuf, afwd, gbuf, ysend, yrecv, own, zsend, zrecv, zown,
-    a_local, a_xs, a_xr, a_cs, a_cr, g_local, g_xs, g_xr, g_cs, g_cr, g_fs, g_fr,
-    y_s, y_r, z_s, z_r, gain_part, gain_recv, gain_s, gain_r,
-):
-    c = lax.axis_index("ctx")
-    x = lax.axis_index("fsdp")
-    core = c % 2
-    y = c // 2 % 2
-    z = c // 4
-    sibling = (c + 1 - 2 * core, x)
-    across = (c, 1 - x)
-    aside = (c + 2 - 4 * y, x)
-
-    def along(o):
-        return ((z + o) % 4 * 4 + c % 4, x)
-
+    return (t == 0) | ((t >= 3) & (t < 10)) | (t >= 11)
+
+
+def make_remote(src, dst, s, r, dev):
+    return pltpu.make_async_remote_copy(
+        src_ref=src, dst_ref=dst, send_sem=s, recv_sem=r, device_id=dev, device_id_type=MESH
+    )
+
+
+class Reducer:
+    def __init__(self, acts, grads, results, scratch, layers):
+        self.acts, self.grads, self.results, self.layers = acts, grads, results, layers
+        self.count = len(layers)
+        (self.gheld, self.abuf, self.afwd, self.gtile, self.ysend, self.yrecv, self.own,
+         self.zsend, self.zrecv, self.zown,
+         self.a_local, self.a_xs, self.a_xr, self.a_cs, self.a_cr,
+         self.g_local, self.g_xs, self.g_xr, self.g_cs, self.g_cr, self.g_fs, self.g_fr,
+         self.y_s, self.y_r, self.z_s, self.z_r) = scratch
+        c = lax.axis_index("ctx")
+        x = lax.axis_index("fsdp")
+        self.c, self.x = c, x
+        self.core = c % 2
+        self.y = c // 2 % 2
+        self.z = c // 4
+        self.sibling = (c + 1 - 2 * self.core, x)
+        self.across = (c, 1 - x)
+        self.aside = (c + 2 - 4 * self.y, x)
+
+    def along(self, o):
+        return ((self.z + o) % 4 * 4 + self.c % 4, self.x)
+
+    def partners(self):
+        return (self.sibling, self.across, self.aside) + tuple(self.along(o) for o in (1, 2, 3))
+
+    def act(self, n, k, what):
+        first, blocks = ACT_SPANS[k]
+        src = self.acts[n][k]
+        span = pl.ds(first, blocks)
+        x, core = self.x, self.core
+
+        def held(place):
+            return self.abuf.at[n, :, :, span, :, pl.ds(128 * place, 128)]
+
+        if what == "local":
+            return pltpu.make_async_copy(
+                src.at[:, :, core, x], held(0), self.a_local.at[n, k]
+            )
+        if what == "across":
+            return make_remote(
+                src.at[:, :, core, 1 - x], held(1), self.a_xs.at[n, k, 0], self.a_xr.at[n, k, 0],
+                self.across,
+            )
+        if what == "relay":
+            return make_remote(
+                src.at[:, :, 1 - core, 1 - x], self.afwd.at[n, :, :, span],
+                self.a_xs.at[n, k, 1], self.a_xr.at[n, k, 1], self.across,
+            )
+        if what == "sibling":
+            return make_remote(
+                src.at[:, :, 1 - core, x], held(2), self.a_cs.at[n, k, 0], self.a_cr.at[n, k, 0],
+                self.sibling,
+            )
+        return make_remote(
+            self.afwd.at[n, :, :, span], held(3), self.a_cs.at[n, k, 1], self.a_cr.at[n, k, 1],
+            self.sibling,
+        )
+
+    def start_acts(self, n, ks):
+        for what in ("across", "relay", "sibling", "local"):
+            for k in ks:
+                self.act(n, k, what).start()
+
+    def forward_acts(self, n, ks):
+        for k in ks:
+            self.act(n, k, "relay").wait_recv()
+            self.act(n, k, "forward").start()
+
+    def await_acts(self, n, ks):
+        for k in ks:
+            self.act(n, k, "local").wait()
+            for what in ("across", "sibling", "forward"):
+                self.act(n, k, what).wait_recv()
+
+    def grad_across(self, i, src=None):
+        rows = self.gheld.at[i, pl.ds(0, 128)]
+        return make_remote(
+            rows if src is None else src, rows, self.g_xs.at[i], self.g_xr.at[i], self.across
+        )
+
+    def grad_sibling(self, i, src=None):
+        rows = self.gheld.at[i, pl.ds(128, 128)]
+        return make_remote(
+            rows if src is None else src, rows, self.g_cs.at[i], self.g_cr.at[i], self.sibling
+        )
+
+    def grad_forward(self, i):
+        return make_remote(
+            self.gheld.at[i, pl.ds(0, 128)], self.gheld.at[i, pl.ds(256, 128)],
+            self.g_fs.at[i], self.g_fr.at[i], self.sibling,
+        )
+
+    def grad_own(self, i, src=None):
+        rows = self.gtile.at[pl.ds(0, 128)]
+        return pltpu.make_async_copy(rows if src is None else src, rows, self.g_local.at[0])
+
+    def grad_load(self, i):
+        return pltpu.make_async_copy(
+            self.gheld.at[i], self.gtile.at[pl.ds(128, 384)], self.g_local.at[1]
+        )
+
+    def with_source(self, i, act):
+        at = 0
+        for n in range(self.count):
+            for ref, blocks in self.grads[n]:
+                first = at
+
+                @pl.when((i >= first) & (i < first + blocks))
+                def use(ref=ref, first=first):
+                    act(ref.at[:, pl.ds(pl.multiple_of((i - first) * 1024, 1024), 1024)])
+
+                at += blocks
+
+    def start_grad(self, i):
+        def go(src):
+            self.grad_across(i, src).start()
+            self.grad_sibling(i, src).start()
+
+        self.with_source(i, go)
+
+    def y_copy(self, t):
+        return make_remote(
+            self.ysend.at[t], self.yrecv.at[t], self.y_s.at[t], self.y_r.at[t], self.aside
+        )
+
+    def z_copy(self, t, o):
+        return make_remote(
+            self.zsend.at[t, o - 1], self.zrecv.at[t, 3 - o], self.z_s.at[t, o - 1],
+            self.z_r.at[t, 3 - o], self.along(o),
+        )
+
+    def begin(self):
+        self.start_acts(0, (0,))
+        self.start_grad(0)
+        self.start_acts(0, (1, 2, 3))
+        for i in range(1, AHEAD):
+            self.start_grad(i)
+
+    def store(self, t, total):
+        n = t // TILES
+        tile = t % TILES
+        query, key, value, out, gate, up, down = self.results
+        by_rows = ((0, 3, down), (9, 2, out))
+        by_columns = ((3, 3, gate), (6, 3, up), (11, 2, query), (13, 1, key), (14, 1, value))
+        if self.count == 1:
+            layer = self.layers[0]
+        else:
+            layer = jnp.where(n == 0, self.layers[0], self.layers[1])
+        for first, blocks, ref in by_rows:
+
+            @pl.when((tile >= first) & (tile < first + blocks))
+            def rows(first=first, ref=ref):
+                ref[layer, pl.ds(pl.multiple_of((tile - first) * 32, 32), 32), :] = total
+
+        for first, blocks, ref in by_columns:
+
+            @pl.when((tile >= first) & (tile < first + blocks))
+            def columns(first=first, ref=ref):
+                ref[layer, :, pl.ds(pl.multiple_of((tile - first) * 1024, 1024), 1024)] = total
+
+    def step(self, s):
+        tiles = TILES * self.count
+        t = s - 5
+
+        @pl.when((t >= 0) & (t < tiles))
+        def finish():
+            total = self.zown[t % 4]
+            for o in (1, 2, 3):
+                self.z_copy(t, o).wait_recv()
+            for o in range(3):
+                total += self.zrecv[t, o].astype(jnp.float32)
+            self.store(t, total)
+
+        u = s - 3
+
+        @pl.when((u >= 0) & (u < tiles))
+        def spread():
+            self.y_copy(u).wait_recv()
+
+            def part(index):
+                rows = pl.ds(pl.multiple_of(index * 32, 32), 32)
+                return self.own[u % 4, rows, :] + self.yrecv[u, rows, :].astype(jnp.float32)
+
+            for o in (2, 1, 3):
+                self.zsend[u, o - 1] = part((self.z + o) % 4).astype(jnp.bfloat16)
+                self.z_copy(u, o).start()
+            self.zown[u % 4] = part(self.z)
+
+        v = s - 1
+
+        @pl.when((v >= 0) & (v < tiles))
+        def compute():
+            n = v // TILES
+            tile = v % TILES
+            gi = n * GRADS + grad_index(tile)
+            ai = act_index(tile)
+            for layer in range(self.count):
+
+                @pl.when(v == TILES * layer)
+                def first_acts(layer=layer):
+                    self.await_acts(layer, (0,))
+
+                @pl.when(v == TILES * layer + 3)
+                def second_acts(layer=layer):
+                    self.await_acts(layer, (1, 2, 3))
+
+            @pl.when(is_new(tile))
+            def fresh():
+                self.with_source(gi, lambda src: self.grad_own(gi, src).start())
+                self.grad_sibling(gi).wait_recv()
+                self.grad_forward(gi).wait_recv()
+                self.grad_load(gi).start()
+                self.grad_own(gi).wait()
+                self.grad_load(gi).wait()
+
+            for half in range(2):
+                cols = pl.ds(half * 512, 512)
+                right = self.gtile[:, cols]
+                theirs = self.abuf[n, :, 1 - self.y, ai].reshape(128, 512)
+                mine = self.abuf[n, :, self.y, ai].reshape(128, 512)
+                self.ysend[v, :, cols] = jnp.dot(
+                    theirs, right, preferred_element_type=jnp.float32
+                ).astype(jnp.bfloat16)
+                self.own[v % 4, :, cols] = jnp.dot(mine, right, preferred_element_type=jnp.float32)
+            self.y_copy(v).start()
+
+        @pl.when((s < tiles) & is_new(s % TILES))
+        def forward():
+            i = s // TILES * GRADS + grad_index(s % TILES)
+            for layer in range(self.count):
+
+                @pl.when(s == TILES * layer)
+                def first_forward(layer=layer):
+                    self.forward_acts(layer, (0,))
+
+                @pl.when(s == TILES * layer + 3)
+                def second_forward(layer=layer):
+                    self.forward_acts(layer, (1, 2, 3))
+
+            self.grad_across(i).wait_recv()
+            self.grad_forward(i).start()
+            for layer in range(1, self.count):
+
+                @pl.when(i == GRADS * layer - AHEAD)
+                def next_acts(layer=layer):
+                    self.start_acts(layer, (0,))
+
+                @pl.when(i == GRADS * layer - AHEAD + 1)
+                def other_acts(layer=layer):
+                    self.start_acts(layer, (1, 2, 3))
+
+            @pl.when(i + AHEAD < GRADS * self.count)
+            def more():
+                self.start_grad(i + AHEAD)
+
+    def steps(self):
+        return TILES * self.count + 5
+
+    def drain(self):
+        for n in range(self.count):
+            for k in range(4):
+                for what in ("across", "relay", "sibling", "forward"):
+                    self.act(n, k, what).wait_send()
+
+        def drain_grads(i, carry):
+            self.grad_across(i).wait_send()
+            self.grad_sibling(i).wait_send()
+            self.grad_forward(i).wait_send()
+            return carry
+
+        lax.fori_loop(0, GRADS * self.count, drain_grads, 0)
+
+        def drain_tiles(t, carry):
+            self.y_copy(t).wait_send()
+            for o in (1, 2, 3):
+                self.z_copy(t, o).wait_send()
+            return carry
+
+        lax.fori_loop(0, TILES * self.count, drain_tiles, 0)
+
+
+class GainSum:
+    def __init__(self, reducer, source, out, scratch):
+        self.reducer, self.source, self.out = reducer, source, out
+        self.part, self.recv, self.s, self.r = scratch
+
+    def hop(self, i):
+        red = self.reducer
+        return make_remote(
+            self.source if i == 0 else self.part.at[i - 1], self.recv.at[i], self.s.at[i],
+            self.r.at[i], (red.across, red.sibling, red.aside)[i],
+        )
+
+    def along(self, o):
+        return make_remote(
+            self.part.at[2], self.recv.at[6 - o], self.s.at[2 + o], self.r.at[6 - o],
+            self.reducer.along(o),
+        )
+
+    def step(self, s, first):
+        @pl.when(s == first)
+        def begin():
+            self.hop(0).start()
+
+        for i in range(3):
+
+            @pl.when(s == first + 1 + i)
+            def stage(i=i):
+                self.hop(i).wait_recv()
+                self.part[i] = (self.source[...] if i == 0 else self.part[i - 1]) + self.recv[i]
+                if i < 2:
+                    self.hop(i + 1).start()
+                else:
+                    for o in (1, 2, 3):
+                        self.along(o).start()
+
+        @pl.when(s == first + 5)
+        def total():
+            for o in (1, 2, 3):
+                self.along(o).wait_recv()
+            self.out[...] = self.part[2] + self.recv[3] + self.recv[4] + self.recv[5]
+
+    def drain(self):
+        for i in range(3):
+            self.hop(i).wait_send()
+            self.along(i + 1).wait_send()
+
+
+def reduce_scratch(count):
+    dma = pltpu.SemaphoreType.DMA
+    low, wide = jnp.bfloat16, jnp.float32
+    tiles, grads = TILES * count, GRADS * count
+    return [
+        pltpu.VMEM((count, 4, 2, ACTS, 32, 512), low),
+        pltpu.VMEM((count, 4, 2, ACTS, 32, 128), low),
+        pltpu.VMEM((512, 1024), low),
+        pltpu.VMEM((tiles, 128, 1024), low),
+        pltpu.VMEM((tiles, 128, 1024), low),
+        pltpu.VMEM((4, 128, 1024), wide),
+        pltpu.VMEM((tiles, 3, 32, 1024), low),
+        pltpu.VMEM((tiles, 3, 32, 1024), low),
+        pltpu.VMEM((4, 32, 1024), wide),
+        dma((count, 4)), dma((count, 4, 2)), dma((count, 4, 2)), dma((count, 4, 2)),
+        dma((count, 4, 2)),
+        dma((2,)), dma((grads,)), dma((grads,)), dma((grads,)), dma((grads,)), dma((grads,)),
+        dma((grads,)),
+        dma((tiles,)), dma((tiles,)), dma((tiles, 3)), dma((tiles, 3)),
+    ]
+
+
+def gain_scratch(rows):
+    dma = pltpu.SemaphoreType.DMA
+    return [
+        pltpu.VMEM((3, rows, 128), jnp.float32),
+        pltpu.VMEM((6, rows, 128), jnp.float32),
+        dma((6,)),
+        dma((6,)),
+    ]
+
+
+RESULTS = ((32, 2048), (32, 1024), (32, 1024), (64, 1024), (32, 3072), (32, 3072), (96, 1024))
+
+
+def reduce_kernel(layers, *refs):
+    count = len(layers)
+    acts = [refs[4 * n : 4 * n + 4] for n in range(count)]
+    refs = refs[4 * count :]
+    grads = []
+    for n in range(count):
+        down, both, out, pre = refs[4 * n : 4 * n + 4]
+        grads.append(((down, 1), (both, 6), (out, 1), (pre, 4)))
+    refs = refs[4 * count :]
+    gains = refs[0]
+    results = refs[1:8]
+    gain_out = refs[8]
+    held = refs[9]
+    sizes = len(reduce_scratch(count))
+    reducer = Reducer(acts, grads, results, (held,) + tuple(refs[10 : 10 + sizes]), layers)
+    gain_sum = GainSum(reducer, gains, gain_out, refs[10 + sizes :])
     barrier = pltpu.get_barrier_semaphore()
-    for other in (sibling, across, aside, along(1), along(2), along(3)):
+    for other in reducer.partners():
         pl.semaphore_signal(barrier, inc=1, device_id=other, device_id_type=MESH)
     pl.semaphore_wait(barrier, 6)
-
-    def remote(src, dst, s, r, dev):
-        return pltpu.make_async_remote_copy(
-            src_ref=src, dst_ref=dst, send_sem=s, recv_sem=r, device_id=dev, device_id_type=MESH
-        )
-
-    spans = (pl.ds(0, 3), pl.ds(3, 4))
-
-    def act_local(g):
-        return pltpu.make_async_copy(
-            acts.at[x, core, spans[g]], abuf.at[spans[g], :, pl.ds(0, 128)], a_local.at[g]
-        )
-
-    def act_across(g, other):
-        if other:
-            return remote(
-                acts.at[1 - x, 1 - core, spans[g]], afwd.at[spans[g]],
-                a_xs.at[g, 1], a_xr.at[g, 1], across,
-            )
-        return remote(
-            acts.at[1 - x, core, spans[g]], abuf.at[spans[g], :, pl.ds(128, 128)],
-            a_xs.at[g, 0], a_xr.at[g, 0], across,
-        )
-
-    def act_sibling(g):
-        return remote(
-            acts.at[x, 1 - core, spans[g]], abuf.at[spans[g], :, pl.ds(256, 128)],
-            a_cs.at[g, 0], a_cr.at[g, 0], sibling,
-        )
-
-    def act_forward(g):
-        return remote(
-            afwd.at[spans[g]], abuf.at[spans[g], :, pl.ds(384, 128)],
-            a_cs.at[g, 1], a_cr.at[g, 1], sibling,
-        )
-
-    def grad_local(i):
-        return pltpu.make_async_copy(grads.at[i], gbuf.at[i, pl.ds(0, 128)], g_local.at[i])
-
-    def grad_across(i):
-        return remote(grads.at[i], gbuf.at[i, pl.ds(128, 128)], g_xs.at[i], g_xr.at[i], across)
-
-    def grad_sibling(i):
-        return remote(grads.at[i], gbuf.at[i, pl.ds(256, 128)], g_cs.at[i], g_cr.at[i], sibling)
-
-    def grad_forward(i):
-        return remote(
-            gbuf.at[i, pl.ds(128, 128)], gbuf.at[i, pl.ds(384, 128)], g_fs.at[i], g_fr.at[i], sibling
-        )
-
-    def y_copy(t):
-        return remote(ysend.at[t], yrecv.at[t], y_s.at[t], y_r.at[t], aside)
-
-    def z_copy(t, o):
-        return remote(
-            zsend.at[t, o - 1], zrecv.at[t, 3 - o], z_s.at[t, o - 1], z_r.at[t, 3 - o], along(o)
-        )
-
-    def start_acts(g):
-        act_across(g, 0).start()
-        act_across(g, 1).start()
-        act_sibling(g).start()
-        act_local(g).start()
-
-    def start_grad(i):
-        grad_across(i).start()
-        grad_sibling(i).start()
-        grad_local(i).start()
-
-    def gain_copy(i):
-        return remote(
-            gains if i == 0 else gain_part.at[i - 1],
-            gain_recv.at[i],
-            gain_s.at[i],
-            gain_r.at[i],
-            (across, sibling, aside)[i],
-        )
-
-    def gain_along(o):
-        return remote(
-            gain_part.at[2], gain_recv.at[6 - o], gain_s.at[2 + o], gain_r.at[6 - o], along(o)
-        )
-
-    gain_copy(0).start()
-    start_acts(0)
-    start_grad(0)
-    start_acts(1)
-    for i in range(1, AHEAD):
-        start_grad(i)
-
-    def forward_acts(g):
-        act_across(g, 1).wait_recv()
-        act_forward(g).start()
-
-    def await_acts(g):
-        act_local(g).wait()
-        act_across(g, 0).wait_recv()
-        act_sibling(g).wait_recv()
-        act_forward(g).wait_recv()
+    reducer.begin()
 
     def step(s, carry):
-        for i in range(3):
-
-            @pl.when(s == 2 * i + 2)
-            def gain_stage(i=i):
-                gain_copy(i).wait_recv()
-                gain_part[i] = (gains[...] if i == 0 else gain_part[i - 1]) + gain_recv[i]
-                if i < 2:
-                    gain_copy(i + 1).start()
-                else:
-                    for o in (1, 2, 3):
-                        gain_along(o).start()
-
-        @pl.when(s == 10)
-        def gain_total():
-            for o in (1, 2, 3):
-                gain_along(o).wait_recv()
-            gain_out[...] = gain_part[2] + gain_recv[3] + gain_recv[4] + gain_recv[5]
-
-        t = s - 5
-
-        @pl.when(t >= 0)
-        def finish():
-            total = zown[t % 4]
-            for o in (1, 2, 3):
-                z_copy(t, o).wait_recv()
-            for o in range(3):
-                total += zrecv[t, o].astype(jnp.float32)
-            out[t] = total
-
-        u = s - 3
-
-        @pl.when((u >= 0) & (u < TILES))
-        def spread():
-            y_copy(u).wait_recv()
-
-            def part(index):
-                rows = pl.ds(pl.multiple_of(index * 32, 32), 32)
-                return own[u % 4, rows, :] + yrecv[u, rows, :].astype(jnp.float32)
-
-            for o in (2, 1, 3):
-                zsend[u, o - 1] = part((z + o) % 4).astype(jnp.bfloat16)
-                z_copy(u, o).start()
-            zown[u % 4] = part(z)
-
-        v = s - 1
-
-        @pl.when((v >= 0) & (v < TILES))
-        def compute():
-            gi = grad_index(v)
-            ai = act_index(v)
-
-            @pl.when(v == 0)
-            def first_acts():
-                await_acts(0)
-
-            @pl.when(v == 3)
-            def second_acts():
-                await_acts(1)
-
-            @pl.when(is_new(v))
-            def fresh():
-                grad_local(gi).wait()
-                grad_sibling(gi).wait_recv()
-                grad_forward(gi).wait_recv()
-
-            for half in range(2):
-                cols = pl.ds(half * 512, 512)
-                right = gbuf[gi, :, cols]
-                theirs = pl.ds(pl.multiple_of((1 - y) * 128, 128), 128)
-                mine = pl.ds(pl.multiple_of(y * 128, 128), 128)
-                ysend[v, :, cols] = jnp.dot(
-                    abuf[ai, theirs, :], right, preferred_element_type=jnp.float32
-                ).astype(jnp.bfloat16)
-                own[v % 4, :, cols] = jnp.dot(
-                    abuf[ai, mine, :], right, preferred_element_type=jnp.float32
-                )
-            y_copy(v).start()
-
-        @pl.when(is_new(s))
-        def forward():
-            i = grad_index(s)
-
-            @pl.when(s == 0)
-            def first_forward():
-                forward_acts(0)
-
-            @pl.when(s == 3)
-            def second_forward():
-                forward_acts(1)
-
-            grad_across(i).wait_recv()
-            grad_forward(i).start()
-
-            @pl.when(i + AHEAD < GRADS)
-            def more():
-                start_grad(i + AHEAD)
-
+        gain_sum.step(s, 2)
+        reducer.step(s)
         return carry
 
-    lax.fori_loop(0, TILES + 5, step, 0)
-
-    for i in range(3):
-        gain_copy(i).wait_send()
-        gain_along(i + 1).wait_send()
-    for g in range(2):
-        act_across(g, 0).wait_send()
-        act_across(g, 1).wait_send()
-        act_sibling(g).wait_send()
-        act_forward(g).wait_send()
-
-    def drain_grads(i, carry):
-        grad_across(i).wait_send()
-        grad_sibling(i).wait_send()
-        grad_forward(i).wait_send()
-        return carry
-
-    lax.fori_loop(0, GRADS, drain_grads, 0)
-
-    def drain_tiles(t, carry):
-        y_copy(t).wait_send()
-        for o in (1, 2, 3):
-            z_copy(t, o).wait_send()
-        return carry
-
-    lax.fori_loop(0, TILES, drain_tiles, 0)
-
-
-def reduce_layer(acts, grads, gains, collective_id):
-    dma = pltpu.SemaphoreType.DMA
-    low, wide = jnp.bfloat16, jnp.float32
+    lax.fori_loop(0, reducer.steps(), step, 0)
+    reducer.drain()
+    gain_sum.drain()
+
+
+def reduce_layers(acts, grads, gains, layers, collective_id):
+    count = len(layers)
+    wide = jnp.float32
     return pl.pallas_call(
-        rs_kernel,
-        out_shape=[
-            jax.ShapeDtypeStruct((TILES, 32, 1024), wide),
+        functools.partial(reduce_kernel, layers),
+        out_shape=[jax.ShapeDtypeStruct((count,) + shape, wide) for shape in RESULTS]
+        + [
             jax.ShapeDtypeStruct(gains.shape, wide),
+            jax.ShapeDtypeStruct((GRADS * count, 384, 1024), jnp.bfloat16),
         ],
-        in_specs=[pl.BlockSpec(memory_space=pl.ANY)] * 2
+        in_specs=[pl.BlockSpec(memory_space=pl.ANY)] * (8 * count)
         + [pl.BlockSpec(memory_space=pltpu.VMEM)],
-        out_specs=[pl.BlockSpec(memory_space=pltpu.VMEM)] * 2,
-        scratch_shapes=[
-            pltpu.VMEM((7, 256, 512), low),
-            pltpu.VMEM((7, 256, 128), low),
-            pltpu.VMEM((GRADS, 512, 1024), low),
-            pltpu.VMEM((TILES, 128, 1024), low),
-            pltpu.VMEM((TILES, 128, 1024), low),
-            pltpu.VMEM((4, 128, 1024), wide),
-            pltpu.VMEM((TILES, 3, 32, 1024), low),
-            pltpu.VMEM((TILES, 3, 32, 1024), low),
-            pltpu.VMEM((4, 32, 1024), wide),
-            dma((2,)), dma((2, 2)), dma((2, 2)), dma((2, 2)), dma((2, 2)),
-            dma((GRADS,)), dma((GRADS,)), dma((GRADS,)), dma((GRADS,)), dma((GRADS,)),
-            dma((GRADS,)), dma((GRADS,)),
-            dma((TILES,)), dma((TILES,)), dma((TILES, 3)), dma((TILES, 3)),
-            pltpu.VMEM((3,) + gains.shape, wide), pltpu.VMEM((6,) + gains.shape, wide),
-            dma((6,)), dma((6,)),
-        ],
+        out_specs=[pl.BlockSpec(memory_space=pltpu.VMEM)] * 8
+        + [pl.BlockSpec(memory_space=pl.ANY)],
+        scratch_shapes=reduce_scratch(count) + gain_scratch(gains.shape[0]),
         compiler_params=pltpu.CompilerParams(
-            collective_id=collective_id, has_side_effects=True, vmem_limit_bytes=48 * 2**20
+            collective_id=collective_id, has_side_effects=True, vmem_limit_bytes=56 * 2**20
         ),
         name="weight_gradient_reduce",
-    )(acts, grads, gains)
+    )(*acts, *grads, gains)
 
 
 GATHER_PLAN = ((0, 0, 0), (1, 0, 2048), (2, 0, 3072), (3, 1, 0), (4, 2, 0), (5, 2, 3072), (6, 3, 0))
@@ -1336,17 +1477,8 @@
     return (output_low, grad_stream) + stacked
 
 
-def act_blocks(values):
-    turned = values.T.reshape(4, 2, 2, 2, -1, 32, values.shape[0])
-    return turned.transpose(3, 2, 4, 1, 0, 5, 6).reshape(2, 2, -1, 256, values.shape[0])
-
-
-def grad_blocks(values):
-    return values.reshape(values.shape[0], -1, 1024).transpose(1, 0, 2)
-
-
-def side_by_side(tiles):
-    return tiles.transpose(1, 0, 2).reshape(tiles.shape[1], -1)
+def act_rows(values):
+    return values.T.reshape(4, 2, 2, 2, -1, 32, values.shape[0])
 
 
 def product(left, right):
@@ -1433,7 +1565,7 @@
     output_low = (stream * live_mine).astype(jnp.bfloat16)
 
     grad_stream = cotangent.astype(jnp.float32) * live_mine
-    layer_grads = [None] * DECODER_LAYERS
+    reduce_acts, reduce_grads, terms = [], [], [None] * DECODER_LAYERS
     place = ctx_index * 2 + lax.axis_index("fsdp")
     for layer in reversed(range(DECODER_LAYERS)):
         into, out_weight, wide_weight, down = gathered[4 * layer : 4 * layer + 4]
@@ -1459,42 +1591,26 @@
         normed_grad = product_turned(pre_grad, into)
         in_norm_grad, attn_term = norm_backward(stream_in, inv_attn, gains[0][layer], normed_grad)
         grad_stream = middle_grad + in_norm_grad
-        terms = jnp.concatenate(
+        terms[layer] = jnp.concatenate(
             [attn_term.reshape(-1, 128), mlp_term.reshape(-1, 128), head_terms], axis=0
         )
-        tiles, sums = reduce_layer(
-            jnp.concatenate(
-                [act_blocks(member) for member in (hidden_low, attn_low, mid_low, normed_low)],
-                axis=2,
-            ),
-            jnp.concatenate(
-                [grad_blocks(member) for member in (down_low, out_low, both_low, pre_grad)], axis=0
-            ),
-            terms,
-            2 + 2 * DECODER_LAYERS + layer,
-        )
-
-        def share(first, rows, span):
-            flat_sum = sums[first : first + rows].reshape(-1)
-            return lax.dynamic_slice_in_dim(flat_sum, place * span, span)
-
-        layer_grads[layer] = (
-            side_by_side(tiles[11:13]),
-            tiles[13],
-            tiles[14],
-            tiles[3:5].reshape(64, 1024),
-            side_by_side(tiles[5:8]),
-            side_by_side(tiles[8:11]),
-            tiles[0:3].reshape(96, 1024),
-            share(0, 8, 32),
-            share(8, 8, 32),
-            share(16, 1, 4),
-            share(17, 1, 4),
-        )
-    stacked = tuple(
-        (jnp.stack([layer_sums[member] for layer_sums in layer_grads]) for member in range(11))
-    )
-    return (output_low, grad_stream) + stacked
+        reduce_acts += [act_rows(member) for member in (hidden_low, mid_low, attn_low, normed_low)]
+        reduce_grads += [down_low, both_low, out_low, pre_grad]
+    *weight_sums, sums, unused = reduce_layers(
+        reduce_acts,
+        reduce_grads,
+        jnp.concatenate(terms, axis=0),
+        tuple(reversed(range(DECODER_LAYERS))),
+        2 + 2 * DECODER_LAYERS,
+    )
+    sums = sums.reshape(DECODER_LAYERS, -1)
+
+    def share(first, span):
+        return lax.dynamic_slice_in_dim(sums, first + place * span, span, axis=1)
+
+    return (output_low, grad_stream) + tuple(weight_sums) + (
+        share(0, 32), share(1024, 32), share(2048, 4), share(2176, 4)
+    )
 
 
 def solution(mesh):

time: 661 us -> 612 us (0.926)
  local copies, waits for them, and re-layouts: 44.4 us -> 23.9 us
  other arithmetic: 32.9 us -> 13.9 us
  Pallas kernels: 488 us -> 477 us
    another operation x14 -> x0, other arithmetic: 13.7 us -> none  [the longest x11 9.32 us: fast_device(): jnp.stack([layer_sums[member] for layer_sums in layer_grads])]
    pallas_call x2 -> x1, Pallas kernels: 238 us -> 227 us  [reduce_layers(): pl.pallas_call(functools.partial(reduce_kernel, layers), out_shape=[jax.S...]
    reshape x6 -> x1, local copies, waits for them, and re-layouts: 9.85 us -> 0.76 us  [fast_device(): sums = sums.reshape(DECODER_LAYERS, -1)]
    concatenate x6 -> x0, other arithmetic: 7.73 us -> none  [the longest x2 6.05 us: fast_device(): jnp.concatenate([grad_blocks(member) for member in (down_low, out_low, bo...]
where the time goes in v3:
time: 612 us; the launch traced here: 602 us
  Pallas kernels  477 us (78%)
  matrix products  85.2 us (14%)
  local copies, waits for them, and re-layouts  23.9 us (4%)
  other arithmetic  13.9 us (2%)
    pallas_call x1, Pallas kernels, reduce_layers(): pl.pallas_call(functools.partial(reduce_kernel, layers), out_shape=[jax.S...  227 us
    pallas_call x1, Pallas kernels, gather_weights(): pl.pallas_call(functools.partial(gather_kernel, layers), out_shape=[jax.S...  143 us
    pallas_call x2, Pallas kernels, attend_back(): pl.pallas_call(attend_back_kernel, out_shape=[jax.ShapeDtypeStruct((128,...  55.6 us
    pallas_call x2, Pallas kernels, attend(): pl.pallas_call(attend_kernel, out_shape=[jax.ShapeDtypeStruct((128, 2048)...  50.7 us
    dot_general x8, matrix products, product_turned(): return lax.dot_general(left, right, NT, preferred_element_type=jnp.float32)  46.1 us
    dot_general x8, matrix products, product(): return jnp.dot(left, right, preferred_element_type=jnp.float32)  39 us

profile of v3, /device:TPU:0, one launch (start us, length us, event | category | flops | bytes accessed | tf_op | source)
XLA Modules:
  0.0 602.2 jit_solution(17532871789428374831)
XLA Ops:
  0.7 1.4 fusion.40
  2.9 1.3 compare_select_fusion
  9.2 143.4 %weight_gather.1 = (bf16[1024,4096]{1,0:T(8,128)(2,1)}, bf16[2048,1024]{1,0:T(8,128)(2,1)}, bf16[1024,6144]{1,0:T(8,128)(2,1)}, bf16[3072,1024]{1,0:T(8,128)(2,1...) custom-call(bf16[2,512,2048]{2,1,0:T(8,128)(2,1)} %refs_0_.1, ...), custom_call_target="tpu_custom_call" | custom-call | tf_op jit(solution)/shard_map/weight_gather/pallas_call | solution.py:603
  153.9 4.9 fusion.13.pre
  158.8 25.0 %attend.2 = (bf16[128,2048]{1,0:T(8,128)(2,1)S(1)}, bf16[8,4,128,128]{3,2,1,0:T(8,128)(2,1)S(1)}, f32[8,128,256]{2,1,0:T(8,128)S(1)}, f32[8,8,256]{2,1,0:T(8,128)S(1)}) custom-call(f32[128,4096]{1,0:T(8,128)S(1)} %fusion.13.pre, f32[128,128]{1,0:T(8,128)S(1)} %get-tuple-element.139.cosine, f32[128,128]{1,0:T(8,128)S(1)} %get-tuple-element.140.sine, ...), custom_call_target="tpu_custom_call" | custom-call | tf_op jit(solution)/shard_map/attend/pallas_call | solution.py:799
  185.3 6.4 %fusion.26 = f32[128,6144]{1,0:T(8,128)S(1)} fusion(bf16[1024,6144]{1,0:T(8,128)(2,1)} %get-tuple-element.46, f32[128,1024]{1,0:T(8,128)S(1)} %get-tuple-element.130, f32[1024]{0:T(1024)S(1)} %bitcast.110, f32[128]{0:T(128)S(1)} %get-tuple-element.119), kind=kOutput, calls=%fused_computation.110 | convolution fusion | flops 1611005952 | bytes 16257536 | tf_op jit(solution)/shard_map/dot_general | solution.py:1485
  191.8 5.2 multiply_reduce_fusion.7
  197.1 4.9 fusion.28.pre
  202.1 25.8 %attend.3 = (bf16[128,2048]{1,0:T(8,128)(2,1)S(1)}, bf16[8,4,128,128]{3,2,1,0:T(8,128)(2,1)S(1)}, f32[8,128,256]{2,1,0:T(8,128)S(1)}, f32[8,8,256]{2,1,0:T(8,128)S(1)}) custom-call(f32[128,4096]{1,0:T(8,128)S(1)} %fusion.28.pre, f32[128,128]{1,0:T(8,128)S(1)} %get-tuple-element.139.cosine, f32[128,128]{1,0:T(8,128)S(1)} %get-tuple-element.140.sine, ...), custom_call_target="tpu_custom_call" | custom-call | tf_op jit(solution)/shard_map/attend/pallas_call | solution.py:799
  227.9 3.9 multiply_reduce_fusion.6
  231.9 8.3 %fusion.30 = f32[128,6144]{1,0:T(8,128)} fusion(bf16[1024,6144]{1,0:T(8,128)(2,1)} %get-tuple-element.51, f32[128,1024]{1,0:T(8,128)S(1)} %get-tuple-element.134, f32[1024]{0:T(1024)S(1)} %bitcast.113, f32[128]{0:T(128)S(1)} %get-tuple-element.123), kind=kOutput, calls=%fused_computation.114 | convolution fusion | flops 1611005952 | bytes 16257536 | tf_op jit(solution)/shard_map/dot_general | solution.py:1485
  240.6 7.2 %multiply_convert_fusion.3 = (bf16[128,3072]{1,0:T(8,128)(2,1)S(1)}, bf16[128,3072]{1,0:T(8,128)(2,1)S(1)}, bf16[128,3072]{1,0:T(8,128)(2,1)}) fusion(f32[128,6144]{1,0:T(8,128)} %fusion.30, bf16[128,1024]{1,0:T(8,128)(2,1)S(1)} %fusion.11.refs_8_, bf16[3072,1024]{1,0:T(8,128)(2,1)} %get-tuple-element.52), kind=kOutput, calls=%fused_computation.7 | convolution fusion | flops 811597824 | bytes 12058624 | tf_op jit(solution)/shard_map/dot_general | solution.py:1489
  247.9 9.1 %multiply_reduce_fusion = (f32[1024]{0:T(1024)S(1)}, f32[128]{0:T(128)S(1)}, f32[128,1024]{1,0:T(8,128)S(1)}) fusion(f32[128,1024]{1,0:T(8,128)S(1)} %copy-done.16, f32[128]{0:T(128)S(1)} %get-tuple-element.123, f32[1024]{0:T(1024)S(1)} %bitcast.114, bf16[1024,6144]{1,0:T(8,128)(2,1)} %get-tuple-element.51, bf16[128,3072]{1,0:T(8,128)(2,1)S(1)} %get-tuple-element.94, ...), kind=kOutput, calls=%fused_computation.32 | convolution fusion | flops 1614543744 | bytes 15213568 | tf_op jit(solution)/shard_map/dot_general | solution.py:1489
  257.0 1.1 fusion.35
  258.8 3.7 convolution_convert_fusion.1.upstream
  262.5 27.2 %attend_back.2 = (bf16[128,4096]{1,0:T(8,128)(2,1)S(1)}, f32[8,128]{1,0:T(8,128)S(1)}) custom-call(bf16[128,2048]{1,0:T(8,128)(2,1)S(1)} %convolution_convert_fusion.1.upstream, bf16[8,4,128,128]{3,2,1,0:T(8,128)(2,1)S(1)} %copy-done.11, f32[8,128,256]{2,1,0:T(8,128)S(1)} %copy-done.13, f32[8,8,256]{2,1,0:T(8,128)S(1)} %get-tuple-element.55.kept_log, ...), custom_call_target="tpu_custom_call" | custom-call | tf_op jit(solution)/shard_map/attend_back/pallas_call | solution.py:984
  289.8 3.0 multiply_reduce_fusion.1
  292.8 1.1 fusion.34
  293.9 6.7 %multiply_convert_fusion.1 = (bf16[128,3072]{1,0:T(8,128)(2,1)}, bf16[128,3072]{1,0:T(8,128)(2,1)}) fusion(f32[128,6144]{1,0:T(8,128)S(1)} %copy-done.18, bf16[128,1024]{1,0:T(8,128)(2,1)S(1)} %get-tuple-element.85.refs_12_, bf16[3072,1024]{1,0:T(8,128)(2,1)} %get-tuple-element.47), kind=kOutput, calls=%fused_computation.5 | convolution fusion | flops 810418176 | bytes 11272192 | tf_op jit(solution)/shard_map/dot_general | solution.py:1489
  300.6 9.6 %multiply_reduce_fusion.2 = (f32[1024]{0:T(1024)S(1)}, f32[128]{0:T(128)S(1)}, f32[128,1024]{1,0:T(8,128)S(1)}) fusion(f32[128,1024]{1,0:T(8,128)S(1)} %copy-done.22, f32[128]{0:T(128)S(1)} %get-tuple-element.119, f32[1024]{0:T(1024)S(1)} %bitcast.111, bf16[1024,6144]{1,0:T(8,128)(2,1)} %get-tuple-element.46, bf16[128,3072]{1,0:T(8,128)(2,1)} %get-tuple-element.92, ...), kind=kOutput, calls=%fused_computation.34 | convolution fusion | flops 1614543744 | bytes 15213568 | tf_op jit(solution)/shard_map/dot_general | solution.py:1489
  310.2 2.2 fusion.33
  312.4 3.8 convolution_convert_fusion.upstream
  316.3 28.5 %attend_back.3 = (bf16[128,4096]{1,0:T(8,128)(2,1)S(1)}, f32[8,128]{1,0:T(8,128)S(1)}) custom-call(bf16[128,2048]{1,0:T(8,128)(2,1)S(1)} %convolution_convert_fusion.upstream, bf16[8,4,128,128]{3,2,1,0:T(8,128)(2,1)S(1)} %copy-done.7, f32[8,128,256]{2,1,0:T(8,128)S(1)} %copy-done.9, f32[8,8,256]{2,1,0:T(8,128)S(1)} %get-tuple-element.59.kept_log, ...), custom_call_target="tpu_custom_call" | custom-call | tf_op jit(solution)/shard_map/attend_back/pallas_call | solution.py:984
  344.8 3.0 fusion.10
  347.9 1.2 pad_maximum_fusion.1.refs_13_
  349.2 1.2 pad_maximum_fusion.refs_9_
  352.4 1.8 copy.47
  355.9 1.2 copy.42
  358.0 2.3 fusion.67
  360.3 1.2 copy.46
  362.5 227.0 %weight_gradient_reduce.1 = (f32[2,32,2048]{2,1,0:T(8,128)}, f32[2,32,1024]{2,1,0:T(8,128)}, f32[2,32,1024]{2,1,0:T(8,128)}, f32[2,64,1024]{2,1,0:T(8,128)}, f32...) custom-call(bf16[4,2,2,2,3,32,128]{6,5,4,3,2,1,0:T(8,128)(2,1)} %bit, ...), custom_call_target="tpu_custom_call" | custom-call | tf_op jit(solution)/shard_map/weight_gradient_reduce/pallas_call | solution.py:448
  591.5 4.6 fusion.1
  (171 shorter events, 22.7 us)
Async XLA Ops:
  9.2 144.5 %copy-start.23 = (bf16[128,1024]{1,0:T(8,128)(2,1)S(1)}, bf16[128,1024]{1,0:T(8,128)(2,1)}, u32[]{:S(2)}) copy-start(bf16[128,1024]{1,0:T(8,128)(2,1)} %param.15) | copy-start | bytes 786436
  153.9 29.9 %copy-start.14 = (bf16[2048,1024]{1,0:T(8,128)(2,1)S(1)}, bf16[2048,1024]{1,0:T(8,128)(2,1)}, u32[]{:S(2)}) copy-start(bf16[2048,1024]{1,0:T(8,128)(2,1)} %get-tuple-element.45) | copy-start | bytes 12582916
  158.8 25.9 %copy-start.1 = (f32[128,4096]{1,0:T(8,128)}, f32[128,4096]{1,0:T(8,128)S(1)}, u32[]{:S(2)}) copy-start(f32[128,4096]{1,0:T(8,128)S(1)} %fusion.13.pre) | copy-start | bytes 6291460
  184.7 7.1 %copy-start.21 = (f32[128,1024]{1,0:T(8,128)}, f32[128,1024]{1,0:T(8,128)S(1)}, u32[]{:S(2)}) copy-start(f32[128,1024]{1,0:T(8,128)S(1)} %get-tuple-element.130) | copy-start | bytes 1572868
  191.8 5.2 copy-start.17
  197.0 4.9 copy-start.19
  202.0 29.9 %copy-start = (f32[128,4096]{1,0:T(8,128)}, f32[128,4096]{1,0:T(8,128)S(1)}, u32[]{:S(2)}) copy-start(f32[128,4096]{1,0:T(8,128)S(1)} %fusion.28.pre) | copy-start | bytes 6291460
  227.9 12.3 %copy-start.10 = (bf16[8,4,128,128]{3,2,1,0:T(8,128)(2,1)}, bf16[8,4,128,128]{3,2,1,0:T(8,128)(2,1)S(1)}, u32[]{:S(2)}) copy-start(bf16[8,4,128,128]{3,2,1,0:T(8,128)(2,1)S(1)} %get-tuple-element.53.kept) | copy-start | bytes 3145732
  227.9 12.3 %copy-start.12 = (f32[8,128,256]{2,1,0:T(8,128)}, f32[8,128,256]{2,1,0:T(8,128)S(1)}, u32[]{:S(2)}) copy-start(f32[8,128,256]{2,1,0:T(8,128)S(1)} %get-tuple-element.54.kept_out) | copy-start | bytes 3145732
  231.8 8.4 %copy-start.15 = (f32[128,1024]{1,0:T(8,128)}, f32[128,1024]{1,0:T(8,128)S(1)}, u32[]{:S(2)}) copy-start(f32[128,1024]{1,0:T(8,128)S(1)} %get-tuple-element.134) | copy-start | bytes 1572868
  231.9 8.6 %copy-start.34 = (bf16[128,1024]{1,0:T(8,128)(2,1)S(1)}, bf16[128,1024]{1,0:T(8,128)(2,1)}, u32[]{:S(2)}) copy-start(bf16[128,1024]{1,0:T(8,128)(2,1)} %param.16) | copy-start | bytes 786436
  240.6 7.3 %copy-start.32 = (bf16[128,1024]{1,0:T(8,128)(2,1)}, bf16[128,1024]{1,0:T(8,128)(2,1)S(1)}, u32[]{:S(2)}) copy-start(bf16[128,1024]{1,0:T(8,128)(2,1)S(1)} %fusion.11.refs_8_) | copy-start | bytes 786436
  240.6 7.3 %copy-start.16 = (f32[128,1024]{1,0:T(8,128)S(1)}, f32[128,1024]{1,0:T(8,128)}, u32[]{:S(2)}) copy-start(f32[128,1024]{1,0:T(8,128)} %copy-done.15) | copy-start | bytes 1572868
  240.6 49.1 %slice-start.2 = ((s8[8388608]{0:T(1024)(128)(4,1)}), s8[4194304]{0:T(1024)(128)(4,1)S(1)}, s32[]{:S(2)}) async-start(s8[8388608]{0:T(1024)(128)(4,1)} %bitcast.93), calls=%async_computation.2 | async-start | bytes 8388608
  247.8 9.1 %copy-start.35 = (bf16[128,1024]{1,0:T(8,128)(2,1)S(1)}, bf16[128,1024]{1,0:T(8,128)(2,1)}, u32[]{:S(2)}) copy-start(bf16[128,1024]{1,0:T(8,128)(2,1)} %param.16) | copy-start | bytes 786436
  247.8 41.9 %slice-start.3 = ((s8[8388608]{0:T(1024)(128)(4,1)}), s8[4194304]{0:T(1024)(128)(4,1)S(1)}, s32[]{:S(2)}) async-start(s8[8388608]{0:T(1024)(128)(4,1)} %bitcast.93), calls=%async_computation.3 | async-start | bytes 8388608
  256.9 5.6 copy-start.11
  257.0 5.6 copy-start.13
  262.5 27.2 %copy-start.20 = (f32[128,1024]{1,0:T(8,128)S(1)}, f32[128,1024]{1,0:T(8,128)}, u32[]{:S(2)}) copy-start(f32[128,1024]{1,0:T(8,128)} %copy-done.19) | copy-start | bytes 1572868
  293.9 6.7 %copy-start.33 = (bf16[128,1024]{1,0:T(8,128)(2,1)}, bf16[128,1024]{1,0:T(8,128)(2,1)S(1)}, u32[]{:S(2)}) copy-start(bf16[128,1024]{1,0:T(8,128)(2,1)S(1)} %get-tuple-element.85.refs_12_) | copy-start | bytes 786436
  293.9 6.7 %copy-start.22 = (f32[128,1024]{1,0:T(8,128)S(1)}, f32[128,1024]{1,0:T(8,128)}, u32[]{:S(2)}) copy-start(f32[128,1024]{1,0:T(8,128)} %copy-done.21) | copy-start | bytes 1572868
  293.9 50.8 %slice-start = ((s8[8388608]{0:T(1024)(128)(4,1)}), s8[4194304]{0:T(1024)(128)(4,1)S(1)}, s32[]{:S(2)}) async-start(s8[8388608]{0:T(1024)(128)(4,1)} %bitcast.91), calls=%async_computation | async-start | bytes 8388608
  300.6 44.2 %slice-start.1 = ((s8[8388608]{0:T(1024)(128)(4,1)}), s8[4194304]{0:T(1024)(128)(4,1)S(1)}, s32[]{:S(2)}) async-start(s8[8388608]{0:T(1024)(128)(4,1)} %bitcast.91), calls=%async_computation.1 | async-start | bytes 8388608
  316.2 28.5 %copy-start.24 = (bf16[128,1024]{1,0:T(8,128)(2,1)S(1)}, bf16[128,1024]{1,0:T(8,128)(2,1)}, u32[]{:S(2)}) copy-start(bf16[128,1024]{1,0:T(8,128)(2,1)} %param.15) | copy-start | bytes 786436
  349.2 5.9 copy-start.36
  350.4 5.4 copy-start.27
  357.0 4.5 copy-start.5
  591.5 4.6 copy-start.42
  591.5 5.4 copy-start.44
  591.5 6.1 %copy-start.43 = (f32[2,32,1024]{2,1,0:T(8,128)S(1)}, f32[2,32,1024]{2,1,0:T(8,128)}, u32[]{:S(2)}) copy-start(f32[2,32,1024]{2,1,0:T(8,128)} %get-tuple-element.160) | copy-start | bytes 786436
  591.5 6.8 %copy-start.41 = (f32[2,64,1024]{2,1,0:T(8,128)S(1)}, f32[2,64,1024]{2,1,0:T(8,128)}, u32[]{:S(2)}) copy-start(f32[2,64,1024]{2,1,0:T(8,128)} %get-tuple-element.161) | copy-start | bytes 1572868
  596.1 4.8 copy-start.38
  (18 other events, 51.2 us)

commit v4 on v3

--- a/solution.py
+++ b/solution.py
@@ -25,7 +25,8 @@
 TILES = 15
 GRADS = 12
 ACTS = 7
-AHEAD = 3
+AHEAD = 2
+SLOTS = 8
 ACT_SPANS = ((0, 3), (3, 1), (4, 2), (6, 1))
 
 
@@ -140,25 +141,25 @@
         )
 
     def grad_own(self, i, src=None):
-        rows = self.gtile.at[pl.ds(0, 128)]
-        return pltpu.make_async_copy(rows if src is None else src, rows, self.g_local.at[0])
+        rows = self.gtile.at[i % 2, pl.ds(0, 128)]
+        return pltpu.make_async_copy(rows if src is None else src, rows, self.g_local.at[i % 2, 0])
 
     def grad_load(self, i):
         return pltpu.make_async_copy(
-            self.gheld.at[i], self.gtile.at[pl.ds(128, 384)], self.g_local.at[1]
+            self.gheld.at[i], self.gtile.at[i % 2, pl.ds(128, 384)], self.g_local.at[i % 2, 1]
         )
 
     def with_source(self, i, act):
-        at = 0
-        for n in range(self.count):
-            for ref, blocks in self.grads[n]:
-                first = at
-
-                @pl.when((i >= first) & (i < first + blocks))
-                def use(ref=ref, first=first):
-                    act(ref.at[:, pl.ds(pl.multiple_of((i - first) * 1024, 1024), 1024)])
-
-                at += blocks
+        n = i // GRADS
+        g = i % GRADS
+        first = 0
+        for ref, blocks in self.grads:
+
+            @pl.when((g >= first) & (g < first + blocks))
+            def use(ref=ref, first=first):
+                act(ref.at[n, :, pl.ds(pl.multiple_of((g - first) * 1024, 1024), 1024)])
+
+            first += blocks
 
     def start_grad(self, i):
         def go(src):
@@ -169,12 +170,12 @@
 
     def y_copy(self, t):
         return make_remote(
-            self.ysend.at[t], self.yrecv.at[t], self.y_s.at[t], self.y_r.at[t], self.aside
+            self.ysend.at[t % SLOTS], self.yrecv.at[t], self.y_s.at[t], self.y_r.at[t], self.aside
         )
 
     def z_copy(self, t, o):
         return make_remote(
-            self.zsend.at[t, o - 1], self.zrecv.at[t, 3 - o], self.z_s.at[t, o - 1],
+            self.zsend.at[t % SLOTS, o - 1], self.zrecv.at[t, 3 - o], self.z_s.at[t, o - 1],
             self.z_r.at[t, 3 - o], self.along(o),
         )
 
@@ -182,6 +183,8 @@
         self.start_acts(0, (0,))
         self.start_grad(0)
         self.start_acts(0, (1, 2, 3))
+
+    def begin_more(self):
         for i in range(1, AHEAD):
             self.start_grad(i)
 
@@ -209,7 +212,7 @@
 
     def step(self, s):
         tiles = TILES * self.count
-        t = s - 5
+        t = s - 6
 
         @pl.when((t >= 0) & (t < tiles))
         def finish():
@@ -220,7 +223,7 @@
                 total += self.zrecv[t, o].astype(jnp.float32)
             self.store(t, total)
 
-        u = s - 3
+        u = s - 4
 
         @pl.when((u >= 0) & (u < tiles))
         def spread():
@@ -230,12 +233,17 @@
                 rows = pl.ds(pl.multiple_of(index * 32, 32), 32)
                 return self.own[u % 4, rows, :] + self.yrecv[u, rows, :].astype(jnp.float32)
 
+            @pl.when(u >= SLOTS)
+            def settle():
+                for o in (1, 2, 3):
+                    self.z_copy(u - SLOTS, o).wait_send()
+
             for o in (2, 1, 3):
-                self.zsend[u, o - 1] = part((self.z + o) % 4).astype(jnp.bfloat16)
+                self.zsend[u % SLOTS, o - 1] = part((self.z + o) % 4).astype(jnp.bfloat16)
                 self.z_copy(u, o).start()
             self.zown[u % 4] = part(self.z)
 
-        v = s - 1
+        v = s - 2
 
         @pl.when((v >= 0) & (v < tiles))
         def compute():
@@ -255,25 +263,38 @@
 
             @pl.when(is_new(tile))
             def fresh():
-                self.with_source(gi, lambda src: self.grad_own(gi, src).start())
-                self.grad_sibling(gi).wait_recv()
-                self.grad_forward(gi).wait_recv()
-                self.grad_load(gi).start()
                 self.grad_own(gi).wait()
                 self.grad_load(gi).wait()
 
-            for half in range(2):
-                cols = pl.ds(half * 512, 512)
-                right = self.gtile[:, cols]
-                theirs = self.abuf[n, :, 1 - self.y, ai].reshape(128, 512)
-                mine = self.abuf[n, :, self.y, ai].reshape(128, 512)
-                self.ysend[v, :, cols] = jnp.dot(
-                    theirs, right, preferred_element_type=jnp.float32
-                ).astype(jnp.bfloat16)
-                self.own[v % 4, :, cols] = jnp.dot(mine, right, preferred_element_type=jnp.float32)
+            @pl.when(v >= SLOTS)
+            def settle():
+                self.y_copy(v - SLOTS).wait_send()
+
+            left = jnp.concatenate(
+                [
+                    self.abuf[n, :, 1 - self.y, ai].reshape(128, 512),
+                    self.abuf[n, :, self.y, ai].reshape(128, 512),
+                ],
+                axis=0,
+            )
+            for part in range(4):
+                cols = pl.ds(part * 256, 256)
+                result = jnp.dot(left, self.gtile[gi % 2, :, cols], preferred_element_type=jnp.float32)
+                self.ysend[v % SLOTS, :, cols] = result[:128].astype(jnp.bfloat16)
+                self.own[v % 4, :, cols] = result[128:]
             self.y_copy(v).start()
 
-        @pl.when((s < tiles) & is_new(s % TILES))
+        w = s - 1
+
+        @pl.when((w >= 0) & (w < tiles) & is_new(w % TILES))
+        def collect():
+            gi = w // TILES * GRADS + grad_index(w % TILES)
+            self.with_source(gi, lambda src: self.grad_own(gi, src).start())
+            self.grad_sibling(gi).wait_recv()
+            self.grad_forward(gi).wait_recv()
+            self.grad_load(gi).start()
+
+        @pl.when((s >= 0) & (s < tiles) & is_new(s % TILES))
         def forward():
             i = s // TILES * GRADS + grad_index(s % TILES)
             for layer in range(self.count):
@@ -303,7 +324,7 @@
                 self.start_grad(i + AHEAD)
 
     def steps(self):
-        return TILES * self.count + 5
+        return TILES * self.count + 6
 
     def drain(self):
         for n in range(self.count):
@@ -325,7 +346,7 @@
                 self.z_copy(t, o).wait_send()
             return carry
 
-        lax.fori_loop(0, TILES * self.count, drain_tiles, 0)
+        lax.fori_loop(TILES * self.count - SLOTS, TILES * self.count, drain_tiles, 0)
 
 
 class GainSum:
@@ -382,16 +403,16 @@
     return [
         pltpu.VMEM((count, 4, 2, ACTS, 32, 512), low),
         pltpu.VMEM((count, 4, 2, ACTS, 32, 128), low),
-        pltpu.VMEM((512, 1024), low),
-        pltpu.VMEM((tiles, 128, 1024), low),
+        pltpu.VMEM((2, 512, 1024), low),
+        pltpu.VMEM((SLOTS, 128, 1024), low),
         pltpu.VMEM((tiles, 128, 1024), low),
         pltpu.VMEM((4, 128, 1024), wide),
-        pltpu.VMEM((tiles, 3, 32, 1024), low),
+        pltpu.VMEM((SLOTS, 3, 32, 1024), low),
         pltpu.VMEM((tiles, 3, 32, 1024), low),
         pltpu.VMEM((4, 32, 1024), wide),
         dma((count, 4)), dma((count, 4, 2)), dma((count, 4, 2)), dma((count, 4, 2)),
         dma((count, 4, 2)),
-        dma((2,)), dma((grads,)), dma((grads,)), dma((grads,)), dma((grads,)), dma((grads,)),
+        dma((2, 2)), dma((grads,)), dma((grads,)), dma((grads,)), dma((grads,)), dma((grads,)),
         dma((grads,)),
         dma((tiles,)), dma((tiles,)), dma((tiles, 3)), dma((tiles, 3)),
     ]
@@ -410,60 +431,6 @@
 RESULTS = ((32, 2048), (32, 1024), (32, 1024), (64, 1024), (32, 3072), (32, 3072), (96, 1024))
 
 
-def reduce_kernel(layers, *refs):
-    count = len(layers)
-    acts = [refs[4 * n : 4 * n + 4] for n in range(count)]
-    refs = refs[4 * count :]
-    grads = []
-    for n in range(count):
-        down, both, out, pre = refs[4 * n : 4 * n + 4]
-        grads.append(((down, 1), (both, 6), (out, 1), (pre, 4)))
-    refs = refs[4 * count :]
-    gains = refs[0]
-    results = refs[1:8]
-    gain_out = refs[8]
-    held = refs[9]
-    sizes = len(reduce_scratch(count))
-    reducer = Reducer(acts, grads, results, (held,) + tuple(refs[10 : 10 + sizes]), layers)
-    gain_sum = GainSum(reducer, gains, gain_out, refs[10 + sizes :])
-    barrier = pltpu.get_barrier_semaphore()
-    for other in reducer.partners():
-        pl.semaphore_signal(barrier, inc=1, device_id=other, device_id_type=MESH)
-    pl.semaphore_wait(barrier, 6)
-    reducer.begin()
-
-    def step(s, carry):
-        gain_sum.step(s, 2)
-        reducer.step(s)
-        return carry
-
-    lax.fori_loop(0, reducer.steps(), step, 0)
-    reducer.drain()
-    gain_sum.drain()
-
-
-def reduce_layers(acts, grads, gains, layers, collective_id):
-    count = len(layers)
-    wide = jnp.float32
-    return pl.pallas_call(
-        functools.partial(reduce_kernel, layers),
-        out_shape=[jax.ShapeDtypeStruct((count,) + shape, wide) for shape in RESULTS]
-        + [
-            jax.ShapeDtypeStruct(gains.shape, wide),
-            jax.ShapeDtypeStruct((GRADS * count, 384, 1024), jnp.bfloat16),
-        ],
-        in_specs=[pl.BlockSpec(memory_space=pl.ANY)] * (8 * count)
-        + [pl.BlockSpec(memory_space=pltpu.VMEM)],
-        out_specs=[pl.BlockSpec(memory_space=pltpu.VMEM)] * 8
-        + [pl.BlockSpec(memory_space=pl.ANY)],
-        scratch_shapes=reduce_scratch(count) + gain_scratch(gains.shape[0]),
-        compiler_params=pltpu.CompilerParams(
-            collective_id=collective_id, has_side_effects=True, vmem_limit_bytes=56 * 2**20
-        ),
-        name="weight_gradient_reduce",
-    )(*acts, *grads, gains)
-
-
 GATHER_PLAN = ((0, 0, 0), (1, 0, 2048), (2, 0, 3072), (3, 1, 0), (4, 2, 0), (5, 2, 3072), (6, 3, 0))
 MEMBERS = 7
 
@@ -471,10 +438,10 @@
 def gather_kernel(layers, *refs):
     sources = refs[:MEMBERS]
     gains = refs[MEMBERS]
-    outs = refs[MEMBERS + 1 : MEMBERS + 1 + 4 * len(layers)]
-    gains_out = refs[MEMBERS + 1 + 4 * len(layers)]
+    outs = refs[MEMBERS + 1 : MEMBERS + 5]
+    gains_out = refs[MEMBERS + 5]
     (l_sem, l_rec, x_s, x_r, y_s, y_r, z_s, z_r, yd_s, yd_r, zd_s, zd_r, c_s, c_r, g_sem) = refs[
-        MEMBERS + 2 + 4 * len(layers) :
+        MEMBERS + 6 :
     ]
     c = lax.axis_index("ctx")
     x = lax.axis_index("fsdp")
@@ -509,7 +476,7 @@
         half = sources[source].shape[1]
         part = half // 8
         width = sources[source].shape[2]
-        return n, sources[source], outs[4 * n + target], half, part, width, column
+        return n, sources[source], outs[target].at[n], half, part, width, column
 
     def window(i, owner_x, owner_core, piece, share=None):
         n, src, out, half, part, width, column = geometry(i)
@@ -599,10 +566,10 @@
     dma = pltpu.SemaphoreType.DMA
     count = MEMBERS * len(layers)
     low = jnp.bfloat16
-    shapes = [(1024, 4096), (2048, 1024), (1024, 6144), (3072, 1024)] * len(layers)
+    shapes = [(1024, 4096), (2048, 1024), (1024, 6144), (3072, 1024)]
     return pl.pallas_call(
         functools.partial(gather_kernel, layers),
-        out_shape=[jax.ShapeDtypeStruct(s, low) for s in shapes]
+        out_shape=[jax.ShapeDtypeStruct((len(layers),) + s, low) for s in shapes]
         + [jax.ShapeDtypeStruct((2,) + gains.shape, low)],
         in_specs=[pl.BlockSpec(memory_space=pl.ANY)] * (MEMBERS + 1),
         out_specs=[pl.BlockSpec(memory_space=pl.ANY)] * (len(shapes) + 1),
@@ -820,47 +787,240 @@
     )(pre, cosine, sine, gains, key_place, query_cap)
 
 
-def attend_back_kernel(
-    upstream, kept, kept_out, kept_log, pre, cosine, sine, gains, key_place, query_cap,
-    out, gain_out,
-    dsend, drecv, qsend, qrecv, ksend, krecv, kt, key_sum, value_sum,
-    d_s, d_r, q_s, q_r, k_s, k_r,
-):
-    me, peer, remote, barrier = peer_tools()
+WORK = 12
+
+
+def rms_back(values, gain, upstream):
+    r = lax.rsqrt(jnp.mean(values * values, axis=-1, keepdims=True) + norm_epsilon)
+    weighted = upstream * gain
+    mean = jnp.mean(weighted * values, axis=-1, keepdims=True)
+    grad = r * weighted - values * (r * r * r) * mean
+    return grad, jnp.sum(upstream * values * r, axis=0, keepdims=True)
+
+
+def stream_blocks(first, count, start, wait, body):
+    start(first, 0)
+
+    def one(i, carry):
+        slot = i % 2
+
+        @pl.when(i + 1 < count)
+        def following():
+            start(first + i + 1, 1 - slot)
+
+        wait(first + i, slot)
+        body(first + i, slot)
+        return carry
+
+    lax.fori_loop(0, count, one, 0)
+
+
+def backward_kernel(*refs):
+    count = DECODER_LAYERS
+    acts = [refs[4 * n : 4 * n + 4] for n in range(count)]
+    refs = refs[4 * count :]
+    per_layer = [refs[7 * n : 7 * n + 7] for n in range(count)]
+    refs = refs[7 * count :]
+    (into_w, out_w, wide_w, down_w) = refs[:4]
+    (upstream, cosine, sine, attn_gains, mlp_gains, head_gains, key_place, query_cap) = refs[4:12]
+    results = refs[12:19]
+    grad_stream, gain_out, held = refs[19:22]
+    refs = refs[22:]
+    sizes = len(reduce_scratch(count))
+    reduce_refs, refs = refs[:sizes], refs[sizes:]
+    gain_refs, refs = refs[:4], refs[4:]
+    (down_low, both_low, out_low, pre_low, terms,
+     gate_up, middle, entry, pre, kept, kept_out, kept_log, mid_grad, rows_w, wide_rows,
+     dsend, drecv, qsend, qrecv, ksend, krecv, kt, key_sum, value_sum,
+     load_sem, rows_sem, wide_sem, gate_sem, d_s, d_r, q_s, q_r, k_s, k_r) = refs
+    reducer = Reducer(
+        acts, ((down_low, 1), (both_low, 6), (out_low, 1), (pre_low, 4)), results,
+        (held,) + tuple(reduce_refs), tuple(reversed(range(count))),
+    )
+    gain_sum = GainSum(reducer, terms, gain_out, gain_refs)
+    c = lax.axis_index("ctx")
+    x = lax.axis_index("fsdp")
+    me = c % PEERS
+    z = c // 4
+
+    def peer(r):
+        return (c - me + r, x)
+
+    barrier = pltpu.get_barrier_semaphore()
+
+    def greet(o, carry):
+        pl.semaphore_signal(barrier, inc=1, device_id=peer((me + o) % PEERS), device_id_type=MESH)
+        return carry
+
+    lax.fori_loop(1, PEERS, greet, 0)
+    pl.semaphore_signal(barrier, inc=1, device_id=reducer.across, device_id_type=MESH)
+    for o in range(2):
+        far = ((z // 2 * 2 + 2) % 4 + o) * 4 + c % 4
+        pl.semaphore_signal(barrier, inc=1, device_id=(far, x), device_id_type=MESH)
+    pl.semaphore_wait(barrier, PEERS + 2)
+
+    grad_stream[...] = upstream[...]
+    terms[...] = jnp.zeros_like(terms)
+    reducer.start_acts(0, (0,))
+
     cos = cosine[...]
     sin = sine[...]
 
     def grad_copy(r, slot):
-        return remote(dsend.at[r], drecv.at[slot], d_s.at[r], d_r.at[slot], peer(r))
+        return make_remote(dsend.at[r], drecv.at[slot], d_s.at[r], d_r.at[slot], peer(r))
 
     def query_copy(r, slot):
-        return remote(qsend.at[r], qrecv.at[slot], q_s.at[r], q_r.at[slot], peer(r))
+        return make_remote(qsend.at[r], qrecv.at[slot], q_s.at[r], q_r.at[slot], peer(r))
 
     def key_copy(r, slot):
-        return remote(ksend.at[r], krecv.at[slot], k_s.at[r], k_r.at[slot], peer(r))
-
-    pl.semaphore_wait(barrier, PEERS - 1)
-
-    def push(o, carry):
-        r = (me + o) % PEERS
-        dsend[r, 0] = upstream[:, head_columns(0, 2 * r)]
-        dsend[r, 1] = upstream[:, head_columns(0, 2 * r + 1)]
-        grad_copy(r, me).start()
-        return carry
-
-    lax.fori_loop(1, PEERS, push, 0)
-    drecv[me, 0] = upstream[:, head_columns(0, 2 * me)]
-    drecv[me, 1] = upstream[:, head_columns(0, 2 * me + 1)]
-
-    def turn_keys(j, carry):
-        kt[j] = kept[j, 2].astype(jnp.float32).T.astype(jnp.bfloat16)
-        return carry
-
-    lax.fori_loop(0, PEERS, turn_keys, 0)
-    key_sum[...] = jnp.zeros_like(key_sum)
-    value_sum[...] = jnp.zeros_like(value_sum)
-
-    def block(o, carry):
+        return make_remote(ksend.at[r], krecv.at[slot], k_s.at[r], k_r.at[slot], peer(r))
+
+    saved = (middle, entry, pre, kept, kept_out, kept_log)
+
+    def load(n, k):
+        for layer in range(count):
+
+            @pl.when(n == layer)
+            def start(layer=layer):
+                pltpu.make_async_copy(per_layer[layer][1 + k], saved[k], load_sem.at[k]).start()
+
+    def await_load(k):
+        pltpu.make_async_copy(per_layer[0][1 + k], saved[k], load_sem.at[k]).wait()
+
+    def add_term(layer, first, term):
+        for i in range(8):
+            terms[pl.ds(layer * 24 + first + i, 1), :] = term[:, i * 128 : (i + 1) * 128]
+
+    def rows_copy(ref, layer, i, slot):
+        rows = pl.ds(pl.multiple_of(i * 512, 512), 512)
+        return pltpu.make_async_copy(ref.at[layer, rows], rows_w.at[slot], rows_sem.at[slot])
+
+    def wide_copy(ref, layer, i, slot):
+        rows = pl.ds(pl.multiple_of(i * 128, 128), 128)
+        columns = ref.shape[2]
+        return pltpu.make_async_copy(
+            ref.at[layer, rows], wide_rows.at[slot, :, pl.ds(0, columns)], wide_sem.at[slot]
+        )
+
+    def hidden_part(n, layer, part):
+        @pl.when(part == 0)
+        def opening():
+            for k in range(len(saved)):
+                load(n, k)
+            down_low[n] = grad_stream[...].astype(jnp.bfloat16)
+
+        @pl.when((n == 0) & (part == 0))
+        def first():
+            reducer.start_grad(0)
+            reducer.start_acts(0, (1, 2, 3))
+
+        def gate_copy(source, i, slot, k):
+            columns = pl.ds(pl.multiple_of(k * 3072 + i * 512, 512), 512)
+            return pltpu.make_async_copy(
+                source.at[:, columns], gate_up.at[slot, k], gate_sem.at[slot, k]
+            )
+
+        def start(i, slot):
+            rows_copy(down_w, layer, i, slot).start()
+            for place in range(count):
+
+                @pl.when(n == place)
+                def gates(place=place):
+                    for k in range(2):
+                        gate_copy(per_layer[place][0], i, slot, k).start()
+
+        def wait(i, slot):
+            rows_copy(down_w, layer, i, slot).wait()
+            for k in range(2):
+                gate_copy(per_layer[0][0], i, slot, k).wait()
+
+        def body(i, slot):
+            hidden = lax.dot_general(
+                down_low[n], rows_w[slot], NT, preferred_element_type=jnp.float32
+            )
+            gate = gate_up[slot, 0]
+            up = gate_up[slot, 1]
+            sigmoid = jax.nn.sigmoid(gate)
+            columns = pl.multiple_of(i * 512, 512)
+            both_low[n, :, pl.ds(columns, 512)] = (
+                hidden * up * sigmoid * (1.0 + gate * (1.0 - sigmoid))
+            ).astype(jnp.bfloat16)
+            both_low[n, :, pl.ds(3072 + columns, 512)] = (hidden * gate * sigmoid).astype(
+                jnp.bfloat16
+            )
+
+        stream_blocks(part * 3, 3, start, wait, body)
+
+        @pl.when((n == 0) & (part == 1))
+        def rest():
+            reducer.begin_more()
+
+    def middle_part(n, layer, part):
+        def body(i, slot):
+            mid_grad[:, pl.ds(pl.multiple_of(i * 128, 128), 128)] = lax.dot_general(
+                both_low[n], wide_rows[slot], NT, preferred_element_type=jnp.float32
+            )
+
+        stream_blocks(
+            part * 3,
+            jnp.where(part == 2, 2, 3),
+            lambda i, slot: wide_copy(wide_w, layer, i, slot).start(),
+            lambda i, slot: wide_copy(wide_w, layer, i, slot).wait(),
+            body,
+        )
+
+        @pl.when(part == 2)
+        def closing():
+            await_load(0)
+            grad, term = rms_back(middle[...], mlp_gains[layer], mid_grad[...])
+            add_term(layer, 8, term)
+            total = grad_stream[...] + grad
+            grad_stream[...] = total
+            out_low[n] = total.astype(jnp.bfloat16)
+
+    def out_part(n, layer):
+        def place(i):
+            return (i + me // 2) % 4
+
+        def body(i, slot):
+            low = lax.dot_general(
+                out_low[n], rows_w[slot], NT, preferred_element_type=jnp.float32
+            ).astype(jnp.bfloat16)
+            for k in range(2):
+                r = 2 * place(i) + k
+
+                @pl.when(r == me)
+                def home(k=k):
+                    for j in range(2):
+                        at = (2 * k + j) * HEAD_SIZE
+                        drecv[me, j] = low[:, at : at + HEAD_SIZE]
+
+                @pl.when(r != me)
+                def away(k=k, r=r):
+                    for j in range(2):
+                        at = (2 * k + j) * HEAD_SIZE
+                        dsend[r, j] = low[:, at : at + HEAD_SIZE]
+                    grad_copy(r, me).start()
+
+        stream_blocks(
+            0,
+            4,
+            lambda i, slot: rows_copy(out_w, layer, place(i), slot).start(),
+            lambda i, slot: rows_copy(out_w, layer, place(i), slot).wait(),
+            body,
+        )
+        for k in range(2, len(saved)):
+            await_load(k)
+
+        def turn_keys(j, carry):
+            kt[j] = kept[j, 2].astype(jnp.float32).T.astype(jnp.bfloat16)
+            return carry
+
+        lax.fori_loop(0, PEERS, turn_keys, 0)
+        key_sum[...] = jnp.zeros_like(key_sum)
+        value_sum[...] = jnp.zeros_like(value_sum)
+
+    def attention_block(o):
         j = (me + o) % PEERS
 
         @pl.when(o > 0)
@@ -898,9 +1058,9 @@
             qsend[j] = query_grad
             query_copy(j, me).start()
 
-        return carry
-
-    lax.fori_loop(0, PEERS, block, 0)
+        @pl.when(o == PEERS - 1)
+        def keys_done():
+            lax.fori_loop(1, PEERS + 1, push_keys, 0)
 
     def push_keys(o, carry):
         j = (me + o) % PEERS
@@ -921,86 +1081,170 @@
 
         return carry
 
-    lax.fori_loop(1, PEERS + 1, push_keys, 0)
-
-    def back(grad, first, index, gain):
-        g = grad.astype(jnp.float32)
-        dy = g * cos - pltpu.roll(g, HEAD_SIZE // 2, 1) * sin
-        v = pre[:, head_columns(first, index)]
-        r = lax.rsqrt(jnp.mean(v * v, axis=-1, keepdims=True) + norm_epsilon)
-        u = dy * gain
-        result = r * u - v * (r * r * r) * jnp.mean(u * v, axis=-1, keepdims=True)
-        return result.astype(jnp.bfloat16), jnp.sum(dy * v * r, axis=0, keepdims=True)
-
-    def finish_queries(o, total):
-        h = (me + o) % PEERS
-
-        @pl.when(o > 0)
-        def arrived():
-            query_copy(me, h).wait_recv()
-
-        for i in range(2):
-            low, term = back(qrecv[h, i], 0, 2 * h + i, gains[0:1, :])
-            out[:, head_columns(0, 2 * h + i)] = low
-            total += term
-        return total
-
-    zero = jnp.zeros((1, HEAD_SIZE), jnp.float32)
-    query_total = lax.fori_loop(0, PEERS, finish_queries, zero)
-
-    def finish_keys(o, total):
-        h = (me + o) % PEERS
-
-        @pl.when(o > 0)
-        def arrived():
-            key_copy(me, h).wait_recv()
-
-        low, term = back(krecv[h, 0], 2048, h, gains[1:2, :])
-        out[:, head_columns(2048, h)] = low
-        out[:, head_columns(3072, h)] = krecv[h, 1]
-        return total + term
-
-    key_total = lax.fori_loop(0, PEERS, finish_keys, zero)
-    gain_out[...] = jnp.concatenate(
-        [query_total, key_total, jnp.zeros((6, HEAD_SIZE), jnp.float32)], axis=0
-    )
-
-    def drain(o, carry):
-        r = (me + o) % PEERS
-        grad_copy(r, me).wait_send()
-        query_copy(r, me).wait_send()
-        key_copy(r, me).wait_send()
+    def head_part(n, layer):
+        def back(grad, first, index, gain):
+            g = grad.astype(jnp.float32)
+            dy = g * cos - pltpu.roll(g, HEAD_SIZE // 2, 1) * sin
+            low, term = rms_back(pre[:, head_columns(first, index)], gain, dy)
+            return low.astype(jnp.bfloat16), term
+
+        def finish_queries(o, total):
+            h = (me + o) % PEERS
+
+            @pl.when(o > 0)
+            def arrived():
+                query_copy(me, h).wait_recv()
+
+            for i in range(2):
+                low, term = back(qrecv[h, i], 0, 2 * h + i, head_gains[layer, 0:1, :])
+                pre_low[n, :, head_columns(0, 2 * h + i)] = low
+                total += term
+            return total
+
+        zero = jnp.zeros((1, HEAD_SIZE), jnp.float32)
+        terms[pl.ds(layer * 24 + 16, 1), :] = lax.fori_loop(0, PEERS, finish_queries, zero)
+
+        def finish_keys(o, total):
+            h = (me + o) % PEERS
+
+            @pl.when(o > 0)
+            def arrived():
+                key_copy(me, h).wait_recv()
+
+            low, term = back(krecv[h, 0], 2048, h, head_gains[layer, 1:2, :])
+            pre_low[n, :, head_columns(2048, h)] = low
+            pre_low[n, :, head_columns(3072, h)] = krecv[h, 1]
+            return total + term
+
+        terms[pl.ds(layer * 24 + 17, 1), :] = lax.fori_loop(0, PEERS, finish_keys, zero)
+
+        def settle(o, carry):
+            r = (me + o) % PEERS
+            grad_copy(r, me).wait_send()
+            query_copy(r, me).wait_send()
+            key_copy(r, me).wait_send()
+            return carry
+
+        lax.fori_loop(1, PEERS, settle, 0)
+
+    def entry_part(n, layer, part):
+        def body(i, slot):
+            mid_grad[:, pl.ds(pl.multiple_of(i * 128, 128), 128)] = lax.dot_general(
+                pre_low[n], wide_rows[slot, :, 0:4096], NT, preferred_element_type=jnp.float32
+            )
+
+        stream_blocks(
+            part * 4,
+            4,
+            lambda i, slot: wide_copy(into_w, layer, i, slot).start(),
+            lambda i, slot: wide_copy(into_w, layer, i, slot).wait(),
+            body,
+        )
+
+        @pl.when(part == 1)
+        def closing():
+            await_load(1)
+            grad, term = rms_back(entry[...], attn_gains[layer], mid_grad[...])
+            add_term(layer, 0, term)
+            grad_stream[...] += grad
+
+    def step(w, carry):
+        reducer.step(w - 2)
+        gain_sum.step(w, WORK * count)
+        n = w // WORK
+        phase = w % WORK
+        layer = count - 1 - n
+        busy = w < WORK * count
+
+        @pl.when(busy & (phase < 2))
+        def phase_hidden():
+            hidden_part(n, layer, phase)
+
+        @pl.when(busy & (phase >= 2) & (phase < 5))
+        def phase_middle():
+            middle_part(n, layer, phase - 2)
+
+        @pl.when(busy & (phase == 5))
+        def phase_out():
+            out_part(n, layer)
+
+        @pl.when(busy & (phase >= 6) & (phase < 9))
+        def phase_attention():
+            first = (phase - 6) * 3
+
+            def block(i, inner):
+                attention_block(first + i)
+                return inner
+
+            lax.fori_loop(0, jnp.minimum(3, PEERS - first), block, 0)
+
+        @pl.when(busy & (phase == 9))
+        def phase_heads():
+            head_part(n, layer)
+
+        @pl.when(busy & (phase >= 10))
+        def phase_entry():
+            entry_part(n, layer, phase - 10)
+
         return carry
 
-    lax.fori_loop(1, PEERS, drain, 0)
-
-
-def attend_back(
-    upstream, kept, kept_out, kept_log, pre, cosine, sine, gains, key_place, query_cap, collective_id
-):
+    lax.fori_loop(0, reducer.steps() + 2, step, 0)
+    reducer.drain()
+    gain_sum.drain()
+
+
+RESULTS = ((32, 2048), (32, 1024), (32, 1024), (64, 1024), (32, 3072), (32, 3072), (96, 1024))
+
+
+def backward(acts, saved, weights, upstream, cosine, sine, gains, key_place, query_cap, number):
+    count = DECODER_LAYERS
     dma = pltpu.SemaphoreType.DMA
     low, wide = jnp.bfloat16, jnp.float32
     pair = pltpu.VMEM((PEERS, 2, 128, HEAD_SIZE), low)
+    anywhere = pl.BlockSpec(memory_space=pl.ANY)
+    near = pl.BlockSpec(memory_space=pltpu.VMEM)
     return pl.pallas_call(
-        attend_back_kernel,
-        out_shape=[
-            jax.ShapeDtypeStruct((128, 4096), low),
-            jax.ShapeDtypeStruct((8, HEAD_SIZE), wide),
+        backward_kernel,
+        out_shape=[jax.ShapeDtypeStruct((count,) + shape, wide) for shape in RESULTS]
+        + [
+            jax.ShapeDtypeStruct((128, 1024), wide),
+            jax.ShapeDtypeStruct((24 * count, 128), wide),
+            jax.ShapeDtypeStruct((GRADS * count, 384, 1024), low),
         ],
-        in_specs=[pl.BlockSpec(memory_space=pltpu.VMEM)] * 10,
-        out_specs=[pl.BlockSpec(memory_space=pltpu.VMEM)] * 2,
-        scratch_shapes=[pair] * 6
+        in_specs=[anywhere] * (11 * count + 4) + [near] * 8,
+        out_specs=[near] * 9 + [anywhere],
+        scratch_shapes=reduce_scratch(count)
+        + gain_scratch(24 * count)
+        + [
+            pltpu.VMEM((count, 128, 1024), low),
+            pltpu.VMEM((count, 128, 6144), low),
+            pltpu.VMEM((count, 128, 1024), low),
+            pltpu.VMEM((count, 128, 4096), low),
+            pltpu.VMEM((24 * count, 128), wide),
+            pltpu.VMEM((2, 2, 128, 512), wide),
+            pltpu.VMEM((128, 1024), wide),
+            pltpu.VMEM((128, 1024), wide),
+            pltpu.VMEM((128, 4096), wide),
+            pltpu.VMEM((PEERS, 4, 128, HEAD_SIZE), low),
+            pltpu.VMEM((PEERS, HEAD_SIZE, 256), wide),
+            pltpu.VMEM((PEERS, 8, 256), wide),
+            pltpu.VMEM((128, 1024), wide),
+            pltpu.VMEM((2, 512, 1024), low),
+            pltpu.VMEM((2, 128, 6144), low),
+        ]
+        + [pair] * 6
         + [
             pltpu.VMEM((PEERS, HEAD_SIZE, 128), low),
             pltpu.VMEM((PEERS * 128, HEAD_SIZE), wide),
             pltpu.VMEM((PEERS * 128, HEAD_SIZE), wide),
+            dma((6,)), dma((2,)), dma((2,)), dma((2, 2)),
         ]
         + [dma((PEERS,))] * 6,
         compiler_params=pltpu.CompilerParams(
-            collective_id=collective_id, has_side_effects=True, vmem_limit_bytes=48 * 2**20
+            collective_id=number, has_side_effects=True, vmem_limit_bytes=62 * 2**20
         ),
-        name="attend_back",
-    )(upstream, kept, kept_out, kept_log, pre, cosine, sine, gains, key_place, query_cap)
+        name="backward",
+    )(*acts, *saved, *weights, upstream, cosine, sine, *gains, key_place, query_cap)
 
 
 def from_partner(shard, axis, apart):
@@ -1539,69 +1783,41 @@
         gains.append(sides.transpose(1, 0, 2).reshape(DECODER_LAYERS, 2 * span))
         offset += DECODER_LAYERS * span
 
+    attn_gains, mlp_gains = gains[0][:, None, :], gains[1][:, None, :]
+    head_gains = jnp.stack([gains[2], gains[3]], axis=1)
     stream = tokens.astype(jnp.float32)
-    saved = []
+    acts, saved = [], []
     for layer in range(DECODER_LAYERS):
-        into, out_weight, wide_weight, down = gathered[4 * layer : 4 * layer + 4]
-        head_gains = jnp.concatenate([gains[2][layer : layer + 1], gains[3][layer : layer + 1]], 0)
-        normed, inv_attn = norm_forward(stream, gains[0][layer])
+        into, out_weight, wide_weight, down = (member[layer] for member in gathered[:4])
+        normed, unused = norm_forward(stream, gains[0][layer])
         normed_low = normed.astype(jnp.bfloat16)
         pre = product(normed_low, into)
         attn_low, kept, kept_out, kept_log = attend(
-            pre, cosine, sine, head_gains, key_place, query_cap, 2 + layer
+            pre, cosine, sine, head_gains[layer], key_place, query_cap, 2 + layer
         )
         middle = stream + product(attn_low, out_weight)
-        normed_mid, inv_mid = norm_forward(middle, gains[1][layer])
+        normed_mid, unused = norm_forward(middle, gains[1][layer])
         mid_low = normed_mid.astype(jnp.bfloat16)
         both = product(mid_low, wide_weight)
         ff = both.shape[1] // 2
-        gate, up = both[:, :ff], both[:, ff:]
-        hidden_low = (jax.nn.silu(gate) * up).astype(jnp.bfloat16)
-        saved.append(
-            (stream, inv_attn, normed_low, pre, attn_low, kept, kept_out, kept_log,
-             middle, inv_mid, mid_low, gate, up, hidden_low, head_gains)
-        )
+        hidden_low = (jax.nn.silu(both[:, :ff]) * both[:, ff:]).astype(jnp.bfloat16)
+        acts = [act_rows(member) for member in (hidden_low, mid_low, attn_low, normed_low)] + acts
+        saved = [both, middle, stream, pre, kept, kept_out, kept_log] + saved
         stream = middle + product(hidden_low, down)
     output_low = (stream * live_mine).astype(jnp.bfloat16)
 
-    grad_stream = cotangent.astype(jnp.float32) * live_mine
-    reduce_acts, reduce_grads, terms = [], [], [None] * DECODER_LAYERS
     place = ctx_index * 2 + lax.axis_index("fsdp")
-    for layer in reversed(range(DECODER_LAYERS)):
-        into, out_weight, wide_weight, down = gathered[4 * layer : 4 * layer + 4]
-        (stream_in, inv_attn, normed_low, pre, attn_low, kept, kept_out, kept_log,
-         middle, inv_mid, mid_low, gate, up, hidden_low, head_gains) = saved[layer]
-        down_low = grad_stream.astype(jnp.bfloat16)
-        hidden_grad = product_turned(down_low, down)
-        sigmoid_gate = jax.nn.sigmoid(gate)
-        gate_low = (hidden_grad * up * sigmoid_gate * (1.0 + gate * (1.0 - sigmoid_gate))).astype(
-            jnp.bfloat16
-        )
-        up_low = (hidden_grad * gate * sigmoid_gate).astype(jnp.bfloat16)
-        both_low = jnp.concatenate([gate_low, up_low], axis=1)
-        mid_grad = product_turned(both_low, wide_weight)
-        mid_norm_grad, mlp_term = norm_backward(middle, inv_mid, gains[1][layer], mid_grad)
-        middle_grad = grad_stream + mid_norm_grad
-        out_low = middle_grad.astype(jnp.bfloat16)
-        attn_grad = product_turned(out_low, out_weight).astype(jnp.bfloat16)
-        pre_grad, head_terms = attend_back(
-            attn_grad, kept, kept_out, kept_log, pre, cosine, sine, head_gains,
-            key_place, query_cap, 2 + DECODER_LAYERS + layer,
-        )
-        normed_grad = product_turned(pre_grad, into)
-        in_norm_grad, attn_term = norm_backward(stream_in, inv_attn, gains[0][layer], normed_grad)
-        grad_stream = middle_grad + in_norm_grad
-        terms[layer] = jnp.concatenate(
-            [attn_term.reshape(-1, 128), mlp_term.reshape(-1, 128), head_terms], axis=0
-        )
-        reduce_acts += [act_rows(member) for member in (hidden_low, mid_low, attn_low, normed_low)]
-        reduce_grads += [down_low, both_low, out_low, pre_grad]
-    *weight_sums, sums, unused = reduce_layers(
-        reduce_acts,
-        reduce_grads,
-        jnp.concatenate(terms, axis=0),
-        tuple(reversed(range(DECODER_LAYERS))),
-        2 + 2 * DECODER_LAYERS,
+    *weight_sums, grad_stream, sums, unused = backward(
+        acts,
+        saved,
+        gathered[:4],
+        cotangent.astype(jnp.float32) * live_mine,
+        cosine,
+        sine,
+        (attn_gains, mlp_gains, head_gains),
+        key_place,
+        query_cap,
+        2 + DECODER_LAYERS,
     )
     sums = sums.reshape(DECODER_LAYERS, -1)
 

time: 612 us -> 524 us (0.86); the launches traced: 602 us -> 523 us
  matrix products: 85.2 us -> 40.5 us
  Pallas kernels: 477 us -> 445 us
    dot_general x8 -> x0, matrix products: 46.1 us -> none  [product_turned(): return lax.dot_general(left, right, NT, preferred_element_type=jnp.float32)]
    pallas_call x3 -> x1, Pallas kernels: 283 us -> 251 us  [backward(): pl.pallas_call(backward_kernel, out_shape=[jax.ShapeDtypeStruct((count,)...]
where the time goes in v4:
time: 524 us; the launch traced here: 523 us
  Pallas kernels  445 us (85%)
  matrix products  40.5 us (8%)
  local copies, waits for them, and re-layouts  26.7 us (5%)
  other arithmetic  9.03 us (2%)
    pallas_call x1, Pallas kernels, backward(): pl.pallas_call(backward_kernel, out_shape=[jax.ShapeDtypeStruct((count,)...  251 us
    pallas_call x1, Pallas kernels, gather_weights(): pl.pallas_call(functools.partial(gather_kernel, layers), out_shape=[jax.S...  143 us
    pallas_call x2, Pallas kernels, attend(): pl.pallas_call(attend_kernel, out_shape=[jax.ShapeDtypeStruct((128, 2048)...  50.5 us
    dot_general x8, matrix products, product(): return jnp.dot(left, right, preferred_element_type=jnp.float32)  40.5 us
    unnamed x74, local copies, waits for them, and re-layouts  12 us

profile of v4, /device:TPU:0, one launch (start us, length us, event | category | flops | bytes accessed | tf_op | source)
XLA Modules:
  0.0 522.6 jit_solution(16754938282353330045)
XLA Ops:
  0.7 1.4 fusion.64
  2.9 1.3 compare_select_fusion
  9.3 143.4 %weight_gather.1 = (bf16[2,1024,4096]{2,1,0:T(8,128)(2,1)}, bf16[2,2048,1024]{2,1,0:T(8,128)(2,1)}, bf16[2,1024,6144]{2,1,0:T(8,128)(2,1)}, bf16[2,3072,1024]{2,1,0:T(8,128)(2,1)}, bf16[2,32,128]{2,1,0:T(8,128)(2,1)}) custom-call(bf16[2,512,2048]{2,1,0:T(8,128)(2,1)} %refs_0_.1, bf16[2,512,1024]{2,1,0:T(8,128)(2,1)} %refs_1_.1, ...), custom_call_target="tpu_custom_call" | custom-call | tf_op jit(solution)/shard_map/weight_gather/pallas_call | solution.py:570
  153.6 6.1 %fusion.8.pre.refs_18_ = f32[128,4096]{1,0:T(8,128)} fusion(bf16[2,1024,4096]{2,1,0:T(8,128)(2,1)} %get-tuple-element.36.refs_22_, bf16[128,1024]{1,0:T(8,128)(2,1)S(1)} %copy-done.14, f32[1024]{0:T(1024)S(1)} %bitcast.134, f32[128]{0:T(128)S(1)} %add_rsqrt_fusion.3), kind=kOutput, calls=%fused_computation.8 | convolution fusion | flops 1074266112 | bytes 10752512 | tf_op jit(solution)/shard_map/dot_general | solution.py:1729
  160.1 1.6 copy-done.1
  161.6 24.9 %attend.2 = (bf16[128,2048]{1,0:T(8,128)(2,1)S(1)}, bf16[8,4,128,128]{3,2,1,0:T(8,128)(2,1)S(1)}, f32[8,128,256]{2,1,0:T(8,128)S(1)}, f32[8,8,256]{2,1,0:T(8,128)S(1)}) custom-call(f32[128,4096]{1,0:T(8,128)S(1)} %copy-done.1, f32[128,128]{1,0:T(8,128)S(1)} %get-tuple-element.87.cosine.refs_27_, f32[128,128]{1,0:T(8,128)S(1)} %get-tuple-element.88.sine.refs_28_, ...), custom_call_target="tpu_custom_call" | custom-call | tf_op jit(solution)/shard_map/attend/pallas_call | solution.py:766
  186.6 3.8 multiply_reduce_fusion.2
  190.6 0.8 copy.49
  191.5 5.7 %fusion.2.refs_15_ = f32[128,6144]{1,0:T(8,128)S(1)} fusion(bf16[2,1024,6144]{2,1,0:T(8,128)(2,1)} %get-tuple-element.39.refs_24_, f32[128,1024]{1,0:T(8,128)S(1)} %get-tuple-element.82.refs_16_, f32[1024]{0:T(1024)S(1)} %bitcast.137, f32[128]{0:T(128)S(1)} %add_rsqrt_fusion.2), kind=kOutput, calls=%fused_computation.2 | convolution fusion | flops 1611005952 | bytes 16257536 | tf_op jit(solution)/shard_map/dot_general | solution.py:1729
  197.2 5.1 multiply_reduce_fusion.1
  202.4 0.8 copy.47
  203.3 4.7 fusion.6.pre.refs_11_
  208.0 25.5 %attend.3 = (bf16[128,2048]{1,0:T(8,128)(2,1)S(1)}, bf16[8,4,128,128]{3,2,1,0:T(8,128)(2,1)S(1)}, f32[8,128,256]{2,1,0:T(8,128)S(1)}, f32[8,8,256]{2,1,0:T(8,128)S(1)}) custom-call(f32[128,4096]{1,0:T(8,128)S(1)} %fusion.6.pre.refs_11_, f32[128,128]{1,0:T(8,128)S(1)} %get-tuple-element.87.cosine.refs_27_, f32[128,128]{1,0:T(8,128)S(1)} %get-tuple-element.88.sine.refs_28_, ...), custom_call_target="tpu_custom_call" | custom-call | tf_op jit(solution)/shard_map/attend/pallas_call | solution.py:766
  233.6 3.8 multiply_reduce_fusion
  237.6 0.8 copy.45
  238.5 5.7 %fusion.refs_8_ = f32[128,6144]{1,0:T(8,128)S(1)} fusion(bf16[2,1024,6144]{2,1,0:T(8,128)(2,1)} %get-tuple-element.39.refs_24_, f32[128,1024]{1,0:T(8,128)S(1)} %get-tuple-element.86.refs_9_, f32[1024]{0:T(1024)S(1)} %bitcast.141, f32[128]{0:T(128)S(1)} %add_rsqrt_fusion), kind=kOutput, calls=%fused_computation | convolution fusion | flops 1611005952 | bytes 16257536 | tf_op jit(solution)/shard_map/dot_general | solution.py:1729
  244.2 1.7 copy-done.12
  246.3 1.2 copy.44
  247.4 1.0 copy.46
  248.4 2.4 fusion.69
  250.8 1.2 copy.48
  252.0 1.0 copy.50
  253.2 0.9 convert_multiply_fusion.refs_26_
  254.8 0.9 copy.51
  256.9 0.8 convert_element_type.48.refs_17_
  257.7 250.7 %backward.1 = (f32[2,32,2048]{2,1,0:T(8,128)}, f32[2,32,1024]{2,1,0:T(8,128)}, f32[2,32,1024]{2,1,0:T(8,128)}, f32[2,64,1024]{2,1,0:T(8,128)}, f32[2,32,3072]{2,...) custom-call(bf16[4,2,2,2,3,32,128]{6,5,4,3,2,1,0:T(8,128)(2,1)} %bit, ...), custom_call_target="tpu_custom_call" | custom-call | tf_op jit(solution)/shard_map/backward/pallas_call | solution.py:1206
  510.5 5.7 %fusion.41 = bf16[128,1024]{1,0:T(8,128)(2,1)} fusion(f32[128,1024]{1,0:T(8,128)S(1)} %copy-done.16, bf16[2,3072,1024]{2,1,0:T(8,128)(2,1)} %get-tuple-element.40.refs_25_, f32[128]{0:T(128)S(1)} %compare_convert_fusion, f32[128,6144]{1,0:T(8,128)} %copy-done.12), kind=kOutput, calls=%fused_computation.33 | convolution fusion | flops 808058880 | bytes 10224128 | tf_op jit(solution)/shard_map/dot_general | solution.py:1729
  516.2 0.8 copy.74
  517.0 0.8 copy.75
  520.0 0.9 copy.79
  520.8 0.9 copy.80
  521.7 0.9 copy.81
  (109 shorter events, 13.8 us)
Async XLA Ops:
  4.8 203.2 %copy-start.7 = (f32[128,128]{1,0:T(8,128)}, f32[128,128]{1,0:T(8,128)S(1)}, u32[]{:S(2)}) copy-start(f32[128,128]{1,0:T(8,128)S(1)} %get-tuple-element.87.cosine.refs_27_) | copy-start | bytes 196612
  4.8 203.2 %copy-start.8 = (f32[128,128]{1,0:T(8,128)}, f32[128,128]{1,0:T(8,128)S(1)}, u32[]{:S(2)}) copy-start(f32[128,128]{1,0:T(8,128)S(1)} %get-tuple-element.88.sine.refs_28_) | copy-start | bytes 196612
  5.8 202.2 %copy-start = (s32[1024,1]{1,0:T(8,128)}, s32[1024,1]{1,0:T(8,128)S(1)}, u32[]{:S(2)}) copy-start(s32[1024,1]{1,0:T(8,128)S(1)} %copy.41.key_place.refs_32_) | copy-start | bytes 12292
  5.8 202.2 %copy-start.9 = (s32[8,1,256]{2,1,0:T(1,128)}, s32[8,1,256]{2,1,0:T(1,128)S(1)}, u32[]{:S(2)}) copy-start(s32[8,1,256]{2,1,0:T(1,128)S(1)} %pad_add_fusion.query_cap.refs_33_) | copy-start | bytes 24580
  9.3 144.2 %copy-start.14 = (bf16[128,1024]{1,0:T(8,128)(2,1)S(1)}, bf16[128,1024]{1,0:T(8,128)(2,1)}, u32[]{:S(2)}) copy-start(bf16[128,1024]{1,0:T(8,128)(2,1)} %param.15) | copy-start | bytes 786436
  160.1 1.6 copy-start.1
  186.6 3.8 copy-start.3
  186.6 3.8 copy-start.4
  186.6 3.8 copy-start.10
  190.4 6.7 %copy-start.17 = (f32[128,1024]{1,0:T(8,128)}, f32[128,1024]{1,0:T(8,128)S(1)}, u32[]{:S(2)}) copy-start(f32[128,1024]{1,0:T(8,128)S(1)} %get-tuple-element.82.refs_16_) | copy-start | bytes 1572868
  197.1 5.1 copy-start.13
  202.3 31.3 %copy-start.18 = (f32[128,1024]{1,0:T(8,128)}, f32[128,1024]{1,0:T(8,128)S(1)}, u32[]{:S(2)}) copy-start(f32[128,1024]{1,0:T(8,128)S(1)} %get-tuple-element.84.refs_10_) | copy-start | bytes 1572868
  208.0 29.4 %copy-start.2 = (f32[128,4096]{1,0:T(8,128)}, f32[128,4096]{1,0:T(8,128)S(1)}, u32[]{:S(2)}) copy-start(f32[128,4096]{1,0:T(8,128)S(1)} %fusion.6.pre.refs_11_) | copy-start | bytes 6291460
  233.6 3.9 copy-start.5
  233.6 3.9 copy-start.6
  233.6 3.9 copy-start.11
  237.5 6.7 %copy-start.15 = (f32[128,1024]{1,0:T(8,128)}, f32[128,1024]{1,0:T(8,128)S(1)}, u32[]{:S(2)}) copy-start(f32[128,1024]{1,0:T(8,128)S(1)} %get-tuple-element.86.refs_9_) | copy-start | bytes 1572868
  244.2 1.7 copy-start.12
  248.4 4.7 copy-start.27
  257.7 252.7 %copy-start.16 = (f32[128,1024]{1,0:T(8,128)S(1)}, f32[128,1024]{1,0:T(8,128)}, u32[]{:S(2)}) copy-start(f32[128,1024]{1,0:T(8,128)} %copy-done.15) | copy-start | bytes 1572868
  510.5 5.7 %copy-start.24 = (f32[128,1024]{1,0:T(8,128)S(1)}, f32[128,1024]{1,0:T(8,128)}, u32[]{:S(2)}) copy-start(f32[128,1024]{1,0:T(8,128)} %get-tuple-element.103) | copy-start | bytes 1572868
  510.5 6.5 %copy-start.23 = (f32[2,32,2048]{2,1,0:T(8,128)S(1)}, f32[2,32,2048]{2,1,0:T(8,128)}, u32[]{:S(2)}) copy-start(f32[2,32,2048]{2,1,0:T(8,128)} %get-tuple-element.104) | copy-start | bytes 1572868
  510.5 7.3 %copy-start.26 = (f32[2,32,1024]{2,1,0:T(8,128)S(1)}, f32[2,32,1024]{2,1,0:T(8,128)}, u32[]{:S(2)}) copy-start(f32[2,32,1024]{2,1,0:T(8,128)} %get-tuple-element.105) | copy-start | bytes 786436
  510.5 8.0 %copy-start.25 = (f32[2,32,1024]{2,1,0:T(8,128)S(1)}, f32[2,32,1024]{2,1,0:T(8,128)}, u32[]{:S(2)}) copy-start(f32[2,32,1024]{2,1,0:T(8,128)} %get-tuple-element.106) | copy-start | bytes 786436
  516.1 3.0 copy-start.22
  516.1 3.8 copy-start.21
  516.2 4.7 copy-start.20
  517.0 4.8 copy-start.19

commit v5 on v4

--- a/solution.py
+++ b/solution.py
@@ -75,7 +75,7 @@
 
     def act(self, n, k, what):
         first, blocks = ACT_SPANS[k]
-        src = self.acts[n][k]
+        src = self.acts[k].at[self.layers[n]]
         span = pl.ds(first, blocks)
         x, core = self.x, self.core
 
@@ -431,360 +431,623 @@
 RESULTS = ((32, 2048), (32, 1024), (32, 1024), (64, 1024), (32, 3072), (32, 3072), (96, 1024))
 
 
-GATHER_PLAN = ((0, 0, 0), (1, 0, 2048), (2, 0, 3072), (3, 1, 0), (4, 2, 0), (5, 2, 3072), (6, 3, 0))
-MEMBERS = 7
-
-
-def gather_kernel(layers, *refs):
-    sources = refs[:MEMBERS]
-    gains = refs[MEMBERS]
-    outs = refs[MEMBERS + 1 : MEMBERS + 5]
-    gains_out = refs[MEMBERS + 5]
-    (l_sem, l_rec, x_s, x_r, y_s, y_r, z_s, z_r, yd_s, yd_r, zd_s, zd_r, c_s, c_r, g_sem) = refs[
-        MEMBERS + 6 :
-    ]
-    c = lax.axis_index("ctx")
-    x = lax.axis_index("fsdp")
-    core = c % 2
-    y = c // 2 % 2
-    near = c // 4 % 2
-    sibling = (c + 1 - 2 * core, x)
-    across = (c, 1 - x)
-    aside = (c + 2 - 4 * y, x)
-    along = (c + 4 - 8 * near, x)
-
-    barrier = pltpu.get_barrier_semaphore()
-    for other in (sibling, across, aside, along):
-        pl.semaphore_signal(barrier, inc=1, device_id=other, device_id_type=MESH)
-    pl.semaphore_wait(barrier, 4)
-
-    def remote(src, dst, s, r, dev):
-        return pltpu.make_async_remote_copy(
-            src_ref=src, dst_ref=dst, send_sem=s, recv_sem=r, device_id=dev, device_id_type=MESH
-        )
-
-    here = near * 2 + y
-    by_y = near * 2 + 1 - y
-    by_z = (1 - near) * 2 + y
-    corner = (1 - near) * 2 + 1 - y
-    steps = [(n, m) for n in range(len(layers)) for m in range(MEMBERS)]
-    count = len(steps)
-
-    def geometry(i):
-        n, m = steps[i]
-        source, target, column = GATHER_PLAN[m]
-        half = sources[source].shape[1]
-        part = half // 8
-        width = sources[source].shape[2]
-        return n, sources[source], outs[target].at[n], half, part, width, column
-
-    def window(i, owner_x, owner_core, piece, share=None):
-        n, src, out, half, part, width, column = geometry(i)
-        start = owner_x * half + (piece * 2 + owner_core) * part
-        rows = part
-        if share is not None:
-            rows = part // 2
-            start = start + share * rows
-        return out.at[pl.ds(pl.multiple_of(start, 16), rows), pl.ds(column, width)]
-
-    def local(i):
-        n, src, out, half, part, width, column = geometry(i)
-        rows = pl.ds(pl.multiple_of(x * half, 16), half)
-        return remote(
-            src.at[layers[n]], out.at[rows, pl.ds(column, width)], l_sem.at[i], l_rec.at[i], sibling
-        )
-
-    def x_copy(i):
-        n, src, out, half, part, width, column = geometry(i)
-        rows = pl.ds(pl.multiple_of((here * 2 + core) * part, 16), part)
-        return remote(
-            src.at[layers[n], rows], window(i, x, core, here), x_s.at[i], x_r.at[i], across
-        )
-
-    def same(i, piece, s, r, dev, share=None):
-        view = window(i, 1 - x, core, piece, share)
-        return remote(view, view, s, r, dev)
-
-    def y_copy(i):
-        return same(i, here, y_s.at[i], y_r.at[i], aside)
-
-    def z_copy(i):
-        return same(i, here, z_s.at[i], z_r.at[i], along)
-
-    def y_corner(i):
-        return same(i, by_z, yd_s.at[i], yd_r.at[i], aside, 1)
-
-    def z_corner(i):
-        return same(i, by_y, zd_s.at[i], zd_r.at[i], along, 0)
-
-    def core_copy(i, which):
-        piece = (here, by_y, by_z, corner)[which]
-        return same(i, piece, c_s.at[i, which], c_r.at[i, which], sibling)
-
-    gain_local = pltpu.make_async_copy(gains, gains_out.at[x], g_sem.at[0])
-    gain_remote = remote(gains, gains_out.at[x], g_sem.at[1], g_sem.at[2], across)
-    gain_local.start()
-    gain_remote.start()
-
-    ahead = 3
-    for i in range(min(ahead, count)):
-        x_copy(i).start()
-        local(i).start()
-    for s in range(count + 3):
-        if s < count:
-            x_copy(s).wait_recv()
-            y_copy(s).start()
-            z_copy(s).start()
-            core_copy(s, 0).start()
-            if s + ahead < count:
-                x_copy(s + ahead).start()
-                local(s + ahead).start()
-        i = s - 1
-        if 0 <= i < count:
-            y_copy(i).wait_recv()
-            z_corner(i).start()
-            core_copy(i, 1).start()
-            z_copy(i).wait_recv()
-            y_corner(i).start()
-            core_copy(i, 2).start()
-        i = s - 3
-        if 0 <= i < count:
-            y_corner(i).wait_recv()
-            z_corner(i).wait_recv()
-            core_copy(i, 3).start()
-    gain_local.wait()
-    gain_remote.wait()
-    for i in range(count):
-        local(i).wait()
-        for copy in (x_copy(i), y_copy(i), z_copy(i), y_corner(i), z_corner(i)):
-            copy.wait_send()
-        for which in range(4):
-            core_copy(i, which).wait()
-
-
-def gather_weights(weights, gains, layers, collective_id):
-    dma = pltpu.SemaphoreType.DMA
-    count = MEMBERS * len(layers)
-    low = jnp.bfloat16
-    shapes = [(1024, 4096), (2048, 1024), (1024, 6144), (3072, 1024)]
-    return pl.pallas_call(
-        functools.partial(gather_kernel, layers),
-        out_shape=[jax.ShapeDtypeStruct((len(layers),) + s, low) for s in shapes]
-        + [jax.ShapeDtypeStruct((2,) + gains.shape, low)],
-        in_specs=[pl.BlockSpec(memory_space=pl.ANY)] * (MEMBERS + 1),
-        out_specs=[pl.BlockSpec(memory_space=pl.ANY)] * (len(shapes) + 1),
-        scratch_shapes=[dma((count,))] * 12 + [dma((count, 4))] * 2 + [dma((3,))],
-        compiler_params=pltpu.CompilerParams(collective_id=collective_id, has_side_effects=True),
-        name="weight_gather",
-    )(*weights, gains)
-
-
 PEERS = KEY_VALUE_HEADS
 SCALE = HEAD_SIZE ** (-0.5)
 NT = (((1,), (1,)), ((), ()))
 
 
-def peer_tools():
+GATHER_PLAN = ((0, 2048), (0, 3072), (0, 0), (1, 0), (2, 0), (2, 3072), (3, 0))
+MEMBERS = len(GATHER_PLAN)
+LEAD = 3
+
+
+class Gatherer:
+    def __init__(self, sources, outs, sems, count):
+        self.sources, self.outs, self.count = sources, outs, count * MEMBERS
+        (self.l_s, self.l_r, self.x_s, self.x_r, self.y_s, self.y_r, self.z_s, self.z_r,
+         self.yc_s, self.yc_r, self.zc_s, self.zc_r, self.c_s, self.c_r) = sems
+        c = lax.axis_index("ctx")
+        x = lax.axis_index("fsdp")
+        self.x = x
+        self.core = c % 2
+        y = c // 2 % 2
+        near = c // 4 % 2
+        self.sibling = (c + 1 - 2 * self.core, x)
+        self.across = (c, 1 - x)
+        self.aside = (c + 2 - 4 * y, x)
+        self.along = (c + 4 - 8 * near, x)
+        self.here = near * 2 + y
+        self.by_y = near * 2 + 1 - y
+        self.by_z = (1 - near) * 2 + y
+        self.corner = (1 - near) * 2 + 1 - y
+
+    def partners(self):
+        return (self.sibling, self.across, self.aside, self.along)
+
+    def window(self, i, m, owner_x, piece, share=None):
+        target, column = GATHER_PLAN[m]
+        half, width = self.sources[m].shape[1], self.sources[m].shape[2]
+        rows = half // 8
+        start = owner_x * half + (piece * 2 + self.core) * rows
+        if share is not None:
+            rows = rows // 2
+            start = start + share * rows
+        return self.outs[target].at[
+            i // MEMBERS, pl.ds(pl.multiple_of(start, 16), rows), pl.ds(column, width)
+        ]
+
+    def direct(self, i, m, owner_x):
+        target, column = GATHER_PLAN[m]
+        half, width = self.sources[m].shape[1], self.sources[m].shape[2]
+        start = owner_x * half + self.core * (half // 2)
+        return self.outs[target].at[
+            i // MEMBERS, pl.ds(pl.multiple_of(start, 16), half // 2), pl.ds(column, width)
+        ]
+
+    def local(self, i, m):
+        target, column = GATHER_PLAN[m]
+        half, width = self.sources[m].shape[1], self.sources[m].shape[2]
+        rows = pl.ds(pl.multiple_of(self.x * half, 16), half)
+        return make_remote(
+            self.sources[m].at[i // MEMBERS],
+            self.outs[target].at[i // MEMBERS, rows, pl.ds(column, width)],
+            self.l_s.at[i], self.l_r.at[i], self.sibling,
+        )
+
+    def x_copy(self, i, m):
+        half = self.sources[m].shape[1]
+        if m == MEMBERS - 1:
+            rows = pl.ds(pl.multiple_of(self.core * (half // 2), 16), half // 2)
+            view = self.direct(i, m, self.x)
+        else:
+            rows = pl.ds(pl.multiple_of((self.here * 2 + self.core) * (half // 8), 16), half // 8)
+            view = self.window(i, m, self.x, self.here)
+        return make_remote(
+            self.sources[m].at[i // MEMBERS, rows], view, self.x_s.at[i], self.x_r.at[i],
+            self.across,
+        )
+
+    def y_copy(self, i, m):
+        view = self.window(i, m, 1 - self.x, self.here)
+        return make_remote(view, view, self.y_s.at[i], self.y_r.at[i], self.aside)
+
+    def z_copy(self, i, m):
+        view = self.window(i, m, 1 - self.x, self.here)
+        return make_remote(view, view, self.z_s.at[i], self.z_r.at[i], self.along)
+
+    def y_corner(self, i, m):
+        view = self.window(i, m, 1 - self.x, self.by_z, 1)
+        return make_remote(view, view, self.yc_s.at[i], self.yc_r.at[i], self.aside)
+
+    def z_corner(self, i, m):
+        view = self.window(i, m, 1 - self.x, self.by_y, 0)
+        return make_remote(view, view, self.zc_s.at[i], self.zc_r.at[i], self.along)
+
+    def core_copy(self, i, m, which):
+        if m == MEMBERS - 1:
+            view = self.direct(i, m, 1 - self.x)
+        else:
+            piece = (self.here, self.by_y, self.by_z, self.corner)[which]
+            view = self.window(i, m, 1 - self.x, piece)
+        return make_remote(
+            view, view, self.c_s.at[i, which], self.c_r.at[i, which], self.sibling
+        )
+
+    def each(self, i, act, members=range(MEMBERS)):
+        for m in members:
+
+            @pl.when((i >= 0) & (i < self.count) & (i % MEMBERS == m))
+            def member(m=m):
+                act(m)
+
+    def send(self, i):
+        def go(m):
+            self.x_copy(i, m).start()
+            self.local(i, m).start()
+
+        self.each(i, go)
+
+    def step(self, s):
+        shared = range(MEMBERS - 1)
+
+        def spread(m):
+            self.x_copy(s, m).wait_recv()
+            if m < MEMBERS - 1:
+                self.y_copy(s, m).start()
+                self.z_copy(s, m).start()
+            self.core_copy(s, m, 0).start()
+
+        self.each(s, spread)
+        self.send(s + LEAD)
+        i = s - 1
+
+        def corners(m):
+            self.y_copy(i, m).wait_recv()
+            self.z_corner(i, m).start()
+            self.core_copy(i, m, 1).start()
+            self.z_copy(i, m).wait_recv()
+            self.y_corner(i, m).start()
+            self.core_copy(i, m, 2).start()
+
+        self.each(i, corners, shared)
+        j = s - 2
+
+        def last(m):
+            self.y_corner(j, m).wait_recv()
+            self.z_corner(j, m).wait_recv()
+            self.core_copy(j, m, 3).start()
+
+        self.each(j, last, shared)
+
+    def steps(self):
+        return self.count + 2
+
+    def ready(self, n, m):
+        i = n * MEMBERS + m
+        self.local(i, m).wait_recv()
+        for which in range(1 if m == MEMBERS - 1 else 4):
+            self.core_copy(i, m, which).wait_recv()
+
+    def drain(self):
+        def one(i, carry):
+            def go(m):
+                self.local(i, m).wait_send()
+                self.x_copy(i, m).wait_send()
+                if m < MEMBERS - 1:
+                    for copy in (self.y_copy, self.z_copy, self.y_corner, self.z_corner):
+                        copy(i, m).wait_send()
+                for which in range(1 if m == MEMBERS - 1 else 4):
+                    self.core_copy(i, m, which).wait_send()
+
+            self.each(i, go)
+            return carry
+
+        lax.fori_loop(0, self.count, one, 0)
+
+
+def gather_scratch(count):
+    dma = pltpu.SemaphoreType.DMA
+    return [dma((count * MEMBERS,))] * 12 + [dma((count * MEMBERS, 4))] * 2
+
+
+def head_columns(first, index):
+    return pl.ds(pl.multiple_of(first + index * HEAD_SIZE, HEAD_SIZE), HEAD_SIZE)
+
+
+def stream_blocks(first, count, start, wait, body):
+    start(first, 0)
+
+    def one(i, carry):
+        slot = i % 2
+
+        @pl.when(i + 1 < count)
+        def following():
+            start(first + i + 1, 1 - slot)
+
+        wait(first + i, slot)
+        body(first + i, slot)
+        return carry
+
+    lax.fori_loop(0, count, one, 0)
+
+
+def rms(values, gain):
+    r = lax.rsqrt(jnp.mean(values * values, axis=-1, keepdims=True) + norm_epsilon)
+    return values * r * gain
+
+
+FIRST_WORK = 4
+NEXT_WORK = 7
+
+
+def forward_kernel(*refs):
+    count = DECODER_LAYERS
+    sources, refs = refs[:MEMBERS], refs[MEMBERS:]
+    (packed, tokens, live, cosine, sine, key_place, query_cap), refs = refs[:7], refs[7:]
+    weights, refs = refs[:4], refs[4:]
+    into_w, out_w, wide_w, down_w = weights
+    (both_out, middle_out, entry_out, pre_out, kept_hbm, kept_out_hbm, kept_log_hbm), refs = (
+        refs[:7], refs[7:]
+    )
+    (hidden_t, mid_t, attn_t, normed_t, attn_gains, mlp_gains, head_gains, output), refs = (
+        refs[:8], refs[8:]
+    )
+    sizes = len(gather_scratch(count))
+    gather = Gatherer(sources, weights, refs[:sizes], count)
+    (packs, stream, middle, pre, low, attn_low, hidden_low, gate_up, cols_w, rows_w,
+     kept, kept_out, kept_log, send, osend, orecv, vt,
+     pack_sem, cols_sem, rows_sem, gate_sem, save_sem,
+     q_s, q_r, k_s, k_r, o_s, o_r) = refs[sizes:]
     c = lax.axis_index("ctx")
     x = lax.axis_index("fsdp")
     me = c % PEERS
+    z = c // 4
 
     def peer(r):
         return (c - me + r, x)
 
-    def remote(src, dst, s, r, dev):
-        return pltpu.make_async_remote_copy(
-            src_ref=src, dst_ref=dst, send_sem=s, recv_sem=r, device_id=dev, device_id_type=MESH
-        )
-
     barrier = pltpu.get_barrier_semaphore()
 
     def greet(o, carry):
-        pl.semaphore_signal(
-            barrier, inc=1, device_id=peer((me + o) % PEERS), device_id_type=MESH
-        )
+        pl.semaphore_signal(barrier, inc=1, device_id=peer((me + o) % PEERS), device_id_type=MESH)
         return carry
 
     lax.fori_loop(1, PEERS, greet, 0)
-    return me, peer, remote, barrier
-
-
-def head_columns(first, index):
-    return pl.ds(pl.multiple_of(first + index * HEAD_SIZE, HEAD_SIZE), HEAD_SIZE)
-
-
-def attend_kernel(
-    pre, cosine, sine, gains, key_place, query_cap, out, kept, kept_out, kept_log,
-    send, osend, orecv, vt, q_s, q_r, k_s, k_r, o_s, o_r,
-):
-    me, peer, remote, barrier = peer_tools()
+    pl.semaphore_signal(barrier, inc=1, device_id=gather.across, device_id_type=MESH)
+    pl.semaphore_wait(barrier, PEERS)
+
+    pack_copy = make_remote(packed, packs, pack_sem.at[0], pack_sem.at[1], gather.across)
+    pack_copy.start()
+    for i in range(LEAD):
+        gather.send(i)
+    stream[...] = tokens[...].astype(jnp.float32)
+    pack_copy.wait_recv()
+
+    def gain_rows(first):
+        mine = [packed[first + i : first + i + 1, :] for i in range(4)]
+        other = [packs[first + i : first + i + 1, :] for i in range(4)]
+        a = jnp.concatenate(mine, axis=1)
+        b = jnp.concatenate(other, axis=1)
+        low_side = jnp.where(x == 0, a, b)
+        high_side = jnp.where(x == 0, b, a)
+        return jnp.concatenate([low_side, high_side], axis=1)
+
+    for n in range(count):
+        attn_gains[n] = gain_rows(4 * n)
+        mlp_gains[n] = gain_rows(8 + 4 * n)
+        for k in range(2):
+            row = 16 + 2 * k + n
+            head_gains[n, k : k + 1, :] = packed[row : row + 1, :] + packs[row : row + 1, :]
+
     cos = cosine[...]
     sin = sine[...]
 
-    def turned(first, index, gain):
-        v = pre[:, head_columns(first, index)]
-        r = lax.rsqrt(jnp.mean(v * v, axis=-1, keepdims=True) + norm_epsilon)
-        n = v * r * gain
-        return (n * cos + pltpu.roll(n, HEAD_SIZE // 2, 1) * sin).astype(jnp.bfloat16)
-
-    def key_copy(r, slot):
-        return remote(
-            send.at[r, pl.ds(2, 2)], kept.at[slot, pl.ds(2, 2)], k_s.at[r], k_r.at[slot], peer(r)
-        )
-
-    def query_copy(r, slot):
-        return remote(
-            send.at[r, pl.ds(0, 2)], kept.at[slot, pl.ds(0, 2)], q_s.at[r], q_r.at[slot], peer(r)
+    def cols_copy(ref, n, column, slot):
+        return pltpu.make_async_copy(
+            ref.at[n, :, pl.ds(pl.multiple_of(column, 512), 512)], cols_w.at[slot],
+            cols_sem.at[slot],
+        )
+
+    def rows_copy(ref, n, i, slot):
+        rows = pl.ds(pl.multiple_of(i * 512, 512), 512)
+        return pltpu.make_async_copy(ref.at[n, rows], rows_w.at[slot], rows_sem.at[slot])
+
+    saves = (
+        (stream, entry_out), (pre, pre_out), (middle, middle_out), (kept_out, kept_out_hbm),
+        (kept_log, kept_log_hbm),
+    )
+
+    def save(n, k):
+        return pltpu.make_async_copy(saves[k][0], saves[k][1].at[n], save_sem.at[k])
+
+    def save_kept(n):
+        return pltpu.make_async_copy(kept.at[n], kept_hbm.at[n], save_sem.at[5])
+
+    def turn(source, target, n, blocks):
+        def one(j, carry):
+            columns = pl.ds(pl.multiple_of(j * 128, 128), 128)
+            target[n, columns, :] = source[:, columns].astype(jnp.float32).T.astype(jnp.bfloat16)
+            return carry
+
+        lax.fori_loop(0, blocks, one, 0)
+
+    def key_copy(n, r, slot):
+        return make_remote(
+            send.at[r, pl.ds(2, 2)], kept.at[n, slot, pl.ds(2, 2)], k_s.at[r], k_r.at[slot], peer(r)
+        )
+
+    def query_copy(n, r, slot):
+        return make_remote(
+            send.at[r, pl.ds(0, 2)], kept.at[n, slot, pl.ds(0, 2)], q_s.at[r], q_r.at[slot], peer(r)
         )
 
     def out_copy(r, slot):
-        return remote(osend.at[r], orecv.at[slot], o_s.at[r], o_r.at[slot], peer(r))
-
-    def make_keys(o, carry):
-        r = (me + o) % PEERS
-        key = turned(2048, r, gains[1:2, :])
-        value = pre[:, head_columns(3072, r)].astype(jnp.bfloat16)
-
-        @pl.when(o < PEERS)
-        def away():
-            send[r, 2] = key
-            send[r, 3] = value
-
-        @pl.when(o == PEERS)
-        def home():
-            kept[me, 2] = key
-            kept[me, 3] = value
-
-        @pl.when(o == 1)
-        def entered():
-            pl.semaphore_wait(barrier, PEERS - 1)
-
-        @pl.when(o < PEERS)
-        def push():
-            key_copy(r, me).start()
+        return make_remote(osend.at[r], orecv.at[slot], o_s.at[r], o_r.at[slot], peer(r))
+
+    def project(n):
+        save(n, 0).start()
+        low[...] = rms(stream[...], attn_gains[n]).astype(jnp.bfloat16)
+        turn(low, normed_t, n, 8)
+        for m in range(3):
+            gather.ready(n, m)
+
+        def column(i):
+            return (i + 4) % 8 * 512
+
+        def body(i, slot):
+            pre[:, pl.ds(pl.multiple_of(column(i), 512), 512)] = jnp.dot(
+                low[...], cols_w[slot], preferred_element_type=jnp.float32
+            )
+
+        stream_blocks(
+            0,
+            8,
+            lambda i, slot: cols_copy(into_w, n, column(i), slot).start(),
+            lambda i, slot: cols_copy(into_w, n, column(i), slot).wait(),
+            body,
+        )
+        save(n, 1).start()
+
+        def turned(first, index, gain):
+            v = rms(pre[:, head_columns(first, index)], gain)
+            return (v * cos + pltpu.roll(v, HEAD_SIZE // 2, 1) * sin).astype(jnp.bfloat16)
+
+        def make_keys(o, carry):
+            r = (me + o) % PEERS
+            key = turned(2048, r, head_gains[n, 1:2, :])
+            value = pre[:, head_columns(3072, r)].astype(jnp.bfloat16)
+
+            @pl.when(o < PEERS)
+            def away():
+                send[r, 2] = key
+                send[r, 3] = value
+                key_copy(n, r, me).start()
+
+            @pl.when(o == PEERS)
+            def home():
+                kept[n, me, 2] = key
+                kept[n, me, 3] = value
+
+            return carry
+
+        def make_queries(o, carry):
+            r = (me + o) % PEERS
+            first = turned(0, 2 * r, head_gains[n, 0:1, :])
+            second = turned(0, 2 * r + 1, head_gains[n, 0:1, :])
+
+            @pl.when(o < PEERS)
+            def away():
+                send[r, 0] = first
+                send[r, 1] = second
+                query_copy(n, r, me).start()
+
+            @pl.when(o == PEERS)
+            def home():
+                kept[n, me, 0] = first
+                kept[n, me, 1] = second
+
+            return carry
+
+        lax.fori_loop(1, PEERS + 1, make_keys, 0)
+        lax.fori_loop(1, PEERS + 1, make_queries, 0)
+
+    def attention(n):
+        def await_keys(o, carry):
+            key_copy(n, me, (me + o) % PEERS).wait_recv()
+            return carry
+
+        lax.fori_loop(1, PEERS, await_keys, 0)
+
+        def turn_values(j, carry):
+            vt[j] = kept[n, j, 3].astype(jnp.float32).T.astype(jnp.bfloat16)
+            return carry
+
+        lax.fori_loop(0, PEERS, turn_values, 0)
+
+        def block(o, carry):
+            j = (me + o) % PEERS
+
+            @pl.when(o > 0)
+            def arrived():
+                query_copy(n, me, j).wait_recv()
+
+            queries = kept[n, j, 0:2].reshape(2 * 128, HEAD_SIZE)
+            keys = kept[n, :, 2].reshape(PEERS * 128, HEAD_SIZE)
+            scores = lax.dot_general(keys, queries, NT, preferred_element_type=jnp.float32) * SCALE
+            allowed = key_place[...] <= query_cap[j]
+            scores = jnp.where(allowed, scores, masked_logits)
+            highest = jnp.max(scores, axis=0, keepdims=True)
+            expo = jnp.exp(scores - highest)
+            total = jnp.sum(expo, axis=0, keepdims=True)
+            expo_low = expo.astype(jnp.bfloat16)
+            turned_out = jnp.zeros((HEAD_SIZE, 256), jnp.float32)
+            for i in range(PEERS):
+                turned_out += jnp.dot(
+                    vt[i], expo_low[i * 128 : (i + 1) * 128], preferred_element_type=jnp.float32
+                )
+            turned_out = turned_out / total
+            kept_out[j] = turned_out
+            kept_log[j] = jnp.broadcast_to(highest + jnp.log(total), (8, 256))
+            attended = turned_out.T.astype(jnp.bfloat16).reshape(2, 128, HEAD_SIZE)
+
+            @pl.when(o == 0)
+            def home():
+                orecv[me] = attended
+
+            @pl.when(o > 0)
+            def away():
+                osend[j] = attended
+                out_copy(j, me).start()
+
+            return carry
+
+        lax.fori_loop(0, PEERS, block, 0)
+        save(n, 3).start()
+        save(n, 4).start()
+        save_kept(n).start()
+
+    def close_attention(n):
+        def collect(o, carry):
+            h = (me + o) % PEERS
+
+            @pl.when(o > 0)
+            def arrived():
+                out_copy(me, h).wait_recv()
+
+            attn_low[:, head_columns(0, 2 * h)] = orecv[h, 0]
+            attn_low[:, head_columns(0, 2 * h + 1)] = orecv[h, 1]
+            return carry
+
+        lax.fori_loop(0, PEERS, collect, 0)
+        save(n, 0).wait()
+        middle[...] = stream[...]
+        gather.ready(n, 3)
+
+        def body(i, slot):
+            columns = pl.ds(pl.multiple_of(i * 512, 512), 512)
+            middle[...] += jnp.dot(
+                attn_low[:, columns], rows_w[slot], preferred_element_type=jnp.float32
+            )
+
+        stream_blocks(
+            0,
+            4,
+            lambda i, slot: rows_copy(out_w, n, i, slot).start(),
+            lambda i, slot: rows_copy(out_w, n, i, slot).wait(),
+            body,
+        )
+        save(n, 2).start()
+        turn(attn_low, attn_t, n, 16)
+        low[...] = rms(middle[...], mlp_gains[n]).astype(jnp.bfloat16)
+        turn(low, mid_t, n, 8)
+
+        def settle(o, carry):
+            r = (me + o) % PEERS
+            key_copy(n, r, me).wait_send()
+            query_copy(n, r, me).wait_send()
+            out_copy(r, me).wait_send()
+            return carry
+
+        lax.fori_loop(1, PEERS, settle, 0)
+
+    def gate_copy(n, i, slot, k):
+        columns = pl.ds(pl.multiple_of(k * 3072 + i * 512, 512), 512)
+        return pltpu.make_async_copy(
+            gate_up.at[slot, k], both_out.at[n, :, columns], gate_sem.at[slot, k]
+        )
+
+    def widen(n):
+        gather.ready(n, 4)
+        gather.ready(n, 5)
+
+        def column(i):
+            return i % 2 * 3072 + i // 2 * 512
+
+        def body(i, slot):
+            k = i % 2
+            at = i // 2
+            held = at % 2
+
+            @pl.when(i >= 4)
+            def settle():
+                gate_copy(n, at - 2, held, k).wait()
+
+            gate_up[held, k] = jnp.dot(
+                low[...], cols_w[slot], preferred_element_type=jnp.float32
+            )
+            gate_copy(n, at, held, k).start()
+
+            @pl.when(k == 1)
+            def finish():
+                gate = gate_up[held, 0]
+                columns = pl.ds(pl.multiple_of(at * 512, 512), 512)
+                hidden_low[:, columns] = (
+                    gate * jax.nn.sigmoid(gate) * gate_up[held, 1]
+                ).astype(jnp.bfloat16)
+
+        stream_blocks(
+            0,
+            12,
+            lambda i, slot: cols_copy(wide_w, n, column(i), slot).start(),
+            lambda i, slot: cols_copy(wide_w, n, column(i), slot).wait(),
+            body,
+        )
+        for at in (4, 5):
+            for k in range(2):
+                gate_copy(n, at, at % 2, k).wait()
+
+    def narrow(n):
+        turn(hidden_low, hidden_t, n, 24)
+        gather.ready(n, 6)
+        stream[...] = middle[...]
+
+        def body(i, slot):
+            columns = pl.ds(pl.multiple_of(i * 512, 512), 512)
+            stream[...] += jnp.dot(
+                hidden_low[:, columns], rows_w[slot], preferred_element_type=jnp.float32
+            )
+
+        stream_blocks(
+            0,
+            6,
+            lambda i, slot: rows_copy(down_w, n, i, slot).start(),
+            lambda i, slot: rows_copy(down_w, n, i, slot).wait(),
+            body,
+        )
+        for k in range(1, 5):
+            save(n, k).wait()
+        save_kept(n).wait()
+
+    def step(w, carry):
+        gather.step(w)
+        n = jnp.where(w >= FIRST_WORK + NEXT_WORK, 1, 0)
+        phase = w - FIRST_WORK - n * NEXT_WORK
+        for at, work in enumerate((project, attention, close_attention, widen, narrow)):
+
+            @pl.when(phase == at)
+            def piece(work=work):
+                work(n)
 
         return carry
 
-    def make_queries(o, carry):
-        r = (me + o) % PEERS
-        first = turned(0, 2 * r, gains[0:1, :])
-        second = turned(0, 2 * r + 1, gains[0:1, :])
-
-        @pl.when(o < PEERS)
-        def away():
-            send[r, 0] = first
-            send[r, 1] = second
-            query_copy(r, me).start()
-
-        @pl.when(o == PEERS)
-        def home():
-            kept[me, 0] = first
-            kept[me, 1] = second
-
-        return carry
-
-    lax.fori_loop(1, PEERS + 1, make_keys, 0)
-    lax.fori_loop(1, PEERS + 1, make_queries, 0)
-
-    def await_keys(o, carry):
-        key_copy(me, (me + o) % PEERS).wait_recv()
-        return carry
-
-    lax.fori_loop(1, PEERS, await_keys, 0)
-
-    def turn_values(j, carry):
-        vt[j] = kept[j, 3].astype(jnp.float32).T.astype(jnp.bfloat16)
-        return carry
-
-    lax.fori_loop(0, PEERS, turn_values, 0)
-
-    def block(o, carry):
-        j = (me + o) % PEERS
-
-        @pl.when(o > 0)
-        def arrived():
-            query_copy(me, j).wait_recv()
-
-        queries = kept[j, 0:2].reshape(2 * 128, HEAD_SIZE)
-        keys = kept[:, 2].reshape(PEERS * 128, HEAD_SIZE)
-        scores = lax.dot_general(keys, queries, NT, preferred_element_type=jnp.float32) * SCALE
-        allowed = key_place[...] <= query_cap[j]
-        scores = jnp.where(allowed, scores, masked_logits)
-        highest = jnp.max(scores, axis=0, keepdims=True)
-        expo = jnp.exp(scores - highest)
-        total = jnp.sum(expo, axis=0, keepdims=True)
-        low = expo.astype(jnp.bfloat16)
-        turned_out = jnp.zeros((HEAD_SIZE, 256), jnp.float32)
-        for i in range(PEERS):
-            turned_out += jnp.dot(
-                vt[i], low[i * 128 : (i + 1) * 128], preferred_element_type=jnp.float32
-            )
-        turned_out = turned_out / total
-        kept_out[j] = turned_out
-        kept_log[j] = jnp.broadcast_to(highest + jnp.log(total), (8, 256))
-        attended = turned_out.T.astype(jnp.bfloat16).reshape(2, 128, HEAD_SIZE)
-
-        @pl.when(o == 0)
-        def home():
-            orecv[me] = attended
-
-        @pl.when(o > 0)
-        def away():
-            osend[j] = attended
-            out_copy(j, me).start()
-
-        return carry
-
-    lax.fori_loop(0, PEERS, block, 0)
-
-    def collect(o, carry):
-        h = (me + o) % PEERS
-
-        @pl.when(o > 0)
-        def arrived():
-            out_copy(me, h).wait_recv()
-
-        out[:, head_columns(0, 2 * h)] = orecv[h, 0]
-        out[:, head_columns(0, 2 * h + 1)] = orecv[h, 1]
-        return carry
-
-    lax.fori_loop(0, PEERS, collect, 0)
-
-    def drain(o, carry):
-        r = (me + o) % PEERS
-        key_copy(r, me).wait_send()
-        query_copy(r, me).wait_send()
-        out_copy(r, me).wait_send()
-        return carry
-
-    lax.fori_loop(1, PEERS, drain, 0)
-
-
-def attend(pre, cosine, sine, gains, key_place, query_cap, collective_id):
+    lax.fori_loop(0, FIRST_WORK + NEXT_WORK + 5, step, 0)
+    output[...] = (stream[...] * live[...]).astype(jnp.bfloat16)
+    gather.drain()
+    pack_copy.wait_send()
+
+
+def forward(weights, packed, tokens, live, cosine, sine, key_place, query_cap, number):
+    count = DECODER_LAYERS
     dma = pltpu.SemaphoreType.DMA
     low, wide = jnp.bfloat16, jnp.float32
+    pair = pltpu.VMEM((PEERS, 2, 128, HEAD_SIZE), low)
+    anywhere = pl.BlockSpec(memory_space=pl.ANY)
+    near = pl.BlockSpec(memory_space=pltpu.VMEM)
+    gathered = [(1024, 4096), (2048, 1024), (1024, 6144), (3072, 1024)]
+    saved = [
+        ((128, 6144), wide), ((128, 1024), wide), ((128, 1024), wide), ((128, 4096), wide),
+        ((PEERS, 4, 128, HEAD_SIZE), low), ((PEERS, HEAD_SIZE, 256), wide), ((PEERS, 8, 256), wide),
+    ]
+    turned = [(3072, 128), (1024, 128), (2048, 128), (1024, 128)]
+    results = (
+        [((count,) + s, low) for s in gathered]
+        + [((count,) + s, d) for s, d in saved]
+        + [((count,) + s, low) for s in turned]
+        + [((count, 1, 1024), wide)] * 2
+        + [((count, 2, HEAD_SIZE), wide), ((128, 1024), low)]
+    )
     return pl.pallas_call(
-        attend_kernel,
-        out_shape=[
-            jax.ShapeDtypeStruct((128, 2048), low),
-            jax.ShapeDtypeStruct((PEERS, 4, 128, HEAD_SIZE), low),
-            jax.ShapeDtypeStruct((PEERS, HEAD_SIZE, 256), wide),
-            jax.ShapeDtypeStruct((PEERS, 8, 256), wide),
-        ],
-        in_specs=[pl.BlockSpec(memory_space=pltpu.VMEM)] * 6,
-        out_specs=[pl.BlockSpec(memory_space=pltpu.VMEM)] * 4,
-        scratch_shapes=[
+        forward_kernel,
+        out_shape=[jax.ShapeDtypeStruct(s, d) for s, d in results],
+        in_specs=[anywhere] * MEMBERS + [near] * 7,
+        out_specs=[anywhere] * 11 + [near] * 8,
+        scratch_shapes=gather_scratch(count)
+        + [
+            pltpu.VMEM(packed.shape, wide),
+            pltpu.VMEM((128, 1024), wide),
+            pltpu.VMEM((128, 1024), wide),
+            pltpu.VMEM((128, 4096), wide),
+            pltpu.VMEM((128, 1024), low),
+            pltpu.VMEM((128, 2048), low),
+            pltpu.VMEM((128, 3072), low),
+            pltpu.VMEM((2, 2, 128, 512), wide),
+            pltpu.VMEM((2, 1024, 512), low),
+            pltpu.VMEM((2, 512, 1024), low),
+            pltpu.VMEM((count, PEERS, 4, 128, HEAD_SIZE), low),
+            pltpu.VMEM((PEERS, HEAD_SIZE, 256), wide),
+            pltpu.VMEM((PEERS, 8, 256), wide),
             pltpu.VMEM((PEERS, 4, 128, HEAD_SIZE), low),
-            pltpu.VMEM((PEERS, 2, 128, HEAD_SIZE), low),
-            pltpu.VMEM((PEERS, 2, 128, HEAD_SIZE), low),
+            pair,
+            pair,
             pltpu.VMEM((PEERS, HEAD_SIZE, 128), low),
+            dma((2,)), dma((2,)), dma((2,)), dma((2, 2)), dma((6,)),
         ]
         + [dma((PEERS,))] * 6,
         compiler_params=pltpu.CompilerParams(
-            collective_id=collective_id, has_side_effects=True, vmem_limit_bytes=40 * 2**20
+            collective_id=number, has_side_effects=True, vmem_limit_bytes=56 * 2**20
         ),
-        name="attend",
-    )(pre, cosine, sine, gains, key_place, query_cap)
+        name="forward",
+    )(*weights, packed, tokens, live, cosine, sine, key_place, query_cap)
 
 
 WORK = 12
@@ -798,29 +1061,9 @@
     return grad, jnp.sum(upstream * values * r, axis=0, keepdims=True)
 
 
-def stream_blocks(first, count, start, wait, body):
-    start(first, 0)
-
-    def one(i, carry):
-        slot = i % 2
-
-        @pl.when(i + 1 < count)
-        def following():
-            start(first + i + 1, 1 - slot)
-
-        wait(first + i, slot)
-        body(first + i, slot)
-        return carry
-
-    lax.fori_loop(0, count, one, 0)
-
-
 def backward_kernel(*refs):
     count = DECODER_LAYERS
-    acts = [refs[4 * n : 4 * n + 4] for n in range(count)]
-    refs = refs[4 * count :]
-    per_layer = [refs[7 * n : 7 * n + 7] for n in range(count)]
-    refs = refs[7 * count :]
+    acts, stored, refs = refs[:4], refs[4:11], refs[11:]
     (into_w, out_w, wide_w, down_w) = refs[:4]
     (upstream, cosine, sine, attn_gains, mlp_gains, head_gains, key_place, query_cap) = refs[4:12]
     results = refs[12:19]
@@ -877,15 +1120,11 @@
 
     saved = (middle, entry, pre, kept, kept_out, kept_log)
 
-    def load(n, k):
-        for layer in range(count):
-
-            @pl.when(n == layer)
-            def start(layer=layer):
-                pltpu.make_async_copy(per_layer[layer][1 + k], saved[k], load_sem.at[k]).start()
+    def load(layer, k):
+        return pltpu.make_async_copy(stored[1 + k].at[layer], saved[k], load_sem.at[k])
 
     def await_load(k):
-        pltpu.make_async_copy(per_layer[0][1 + k], saved[k], load_sem.at[k]).wait()
+        load(0, k).wait()
 
     def add_term(layer, first, term):
         for i in range(8):
@@ -906,7 +1145,7 @@
         @pl.when(part == 0)
         def opening():
             for k in range(len(saved)):
-                load(n, k)
+                load(layer, k).start()
             down_low[n] = grad_stream[...].astype(jnp.bfloat16)
 
         @pl.when((n == 0) & (part == 0))
@@ -914,25 +1153,21 @@
             reducer.start_grad(0)
             reducer.start_acts(0, (1, 2, 3))
 
-        def gate_copy(source, i, slot, k):
+        def gate_copy(i, slot, k):
             columns = pl.ds(pl.multiple_of(k * 3072 + i * 512, 512), 512)
             return pltpu.make_async_copy(
-                source.at[:, columns], gate_up.at[slot, k], gate_sem.at[slot, k]
+                stored[0].at[layer, :, columns], gate_up.at[slot, k], gate_sem.at[slot, k]
             )
 
         def start(i, slot):
             rows_copy(down_w, layer, i, slot).start()
-            for place in range(count):
-
-                @pl.when(n == place)
-                def gates(place=place):
-                    for k in range(2):
-                        gate_copy(per_layer[place][0], i, slot, k).start()
+            for k in range(2):
+                gate_copy(i, slot, k).start()
 
         def wait(i, slot):
             rows_copy(down_w, layer, i, slot).wait()
             for k in range(2):
-                gate_copy(per_layer[0][0], i, slot, k).wait()
+                gate_copy(i, slot, k).wait()
 
         def body(i, slot):
             hidden = lax.dot_general(
@@ -1211,7 +1446,7 @@
             jax.ShapeDtypeStruct((24 * count, 128), wide),
             jax.ShapeDtypeStruct((GRADS * count, 384, 1024), low),
         ],
-        in_specs=[anywhere] * (11 * count + 4) + [near] * 8,
+        in_specs=[anywhere] * 15 + [near] * 8,
         out_specs=[near] * 9 + [anywhere],
         scratch_shapes=reduce_scratch(count)
         + gain_scratch(24 * count)
@@ -1721,18 +1956,6 @@
     return (output_low, grad_stream) + stacked
 
 
-def act_rows(values):
-    return values.T.reshape(4, 2, 2, 2, -1, 32, values.shape[0])
-
-
-def product(left, right):
-    return jnp.dot(left, right, preferred_element_type=jnp.float32)
-
-
-def product_turned(left, right):
-    return lax.dot_general(left, right, NT, preferred_element_type=jnp.float32)
-
-
 def fast_device(
     tokens,
     cotangent,
@@ -1766,58 +1989,46 @@
     half = HEAD_SIZE // 2
     sine = jnp.concatenate([-sine[:, :half], sine[:, half:]], axis=1)
 
-    packed = jnp.concatenate([member.reshape(-1) for member in (g_attn, g_mlp, g_query, g_key)])
-    packed = jnp.pad(packed, (0, 4096 - packed.shape[0])).reshape(32, 128)
-    gathered = gather_weights(
-        (w_query, key_projection_weight, value_projection_weight, w_out, w_gate, w_up, w_down),
+    mesh_x = lax.axis_index("fsdp")
+    rows = [member.reshape(-1, 128) for member in (g_attn, g_mlp)]
+    for member in (g_query, g_key):
+        zero = jnp.zeros_like(member)
+        rows.append(
+            jnp.concatenate(
+                [jnp.where(mesh_x == 0, member, zero), jnp.where(mesh_x == 0, zero, member)], axis=1
+            )
+        )
+    packed = jnp.pad(jnp.concatenate(rows, axis=0).astype(jnp.float32), ((0, 4), (0, 0)))
+    results = forward(
+        (key_projection_weight, value_projection_weight, w_query, w_out, w_gate, w_up, w_down),
         packed,
-        tuple(range(DECODER_LAYERS)),
+        tokens,
+        live_mine,
+        cosine,
+        sine,
+        key_place,
+        query_cap,
         1,
     )
-    flat = gathered[-1].reshape(2, -1).astype(jnp.float32)
-    gains = []
-    offset = 0
-    for member in (g_attn, g_mlp, g_query, g_key):
-        span = member.shape[1]
-        sides = flat[:, offset : offset + DECODER_LAYERS * span].reshape(2, DECODER_LAYERS, span)
-        gains.append(sides.transpose(1, 0, 2).reshape(DECODER_LAYERS, 2 * span))
-        offset += DECODER_LAYERS * span
-
-    attn_gains, mlp_gains = gains[0][:, None, :], gains[1][:, None, :]
-    head_gains = jnp.stack([gains[2], gains[3]], axis=1)
-    stream = tokens.astype(jnp.float32)
-    acts, saved = [], []
-    for layer in range(DECODER_LAYERS):
-        into, out_weight, wide_weight, down = (member[layer] for member in gathered[:4])
-        normed, unused = norm_forward(stream, gains[0][layer])
-        normed_low = normed.astype(jnp.bfloat16)
-        pre = product(normed_low, into)
-        attn_low, kept, kept_out, kept_log = attend(
-            pre, cosine, sine, head_gains[layer], key_place, query_cap, 2 + layer
-        )
-        middle = stream + product(attn_low, out_weight)
-        normed_mid, unused = norm_forward(middle, gains[1][layer])
-        mid_low = normed_mid.astype(jnp.bfloat16)
-        both = product(mid_low, wide_weight)
-        ff = both.shape[1] // 2
-        hidden_low = (jax.nn.silu(both[:, :ff]) * both[:, ff:]).astype(jnp.bfloat16)
-        acts = [act_rows(member) for member in (hidden_low, mid_low, attn_low, normed_low)] + acts
-        saved = [both, middle, stream, pre, kept, kept_out, kept_log] + saved
-        stream = middle + product(hidden_low, down)
-    output_low = (stream * live_mine).astype(jnp.bfloat16)
-
-    place = ctx_index * 2 + lax.axis_index("fsdp")
+    gathered, saved, turned, gains, output_low = (
+        results[:4], results[4:11], results[11:15], results[15:18], results[18]
+    )
+    acts = [
+        member.reshape(DECODER_LAYERS, 4, 2, 2, 2, -1, 32, count_rows) for member in turned
+    ]
+
+    place = ctx_index * 2 + mesh_x
     *weight_sums, grad_stream, sums, unused = backward(
         acts,
         saved,
-        gathered[:4],
+        gathered,
         cotangent.astype(jnp.float32) * live_mine,
         cosine,
         sine,
-        (attn_gains, mlp_gains, head_gains),
+        gains,
         key_place,
         query_cap,
-        2 + DECODER_LAYERS,
+        2,
     )
     sums = sums.reshape(DECODER_LAYERS, -1)
 

time: 524 us -> 483 us (0.922)
  matrix products: 40.5 us -> 0 us
  Pallas kernels: 445 us -> 453 us
  local copies, waits for them, and re-layouts: 26.7 us -> 21.3 us
    dot_general x8 -> x0, matrix products: 40.5 us -> none  [product(): return jnp.dot(left, right, preferred_element_type=jnp.float32)]
    pallas_call x3 -> x1, Pallas kernels: 194 us -> 202 us  [forward(): pl.pallas_call(forward_kernel, out_shape=[jax.ShapeDtypeStruct(s, d) for...]
    transpose x10 -> x0, local copies, waits for them, and re-layouts: 7.7 us -> none  [the longest x8 7.69 us: act_rows(): return values.T.reshape(4, 2, 2, 2, -1, 32, values.shape[0])]
    unnamed x74 -> x18, local copies, waits for them, and re-layouts: 12 us -> 14.3 us
where the time goes in v5:
time: 483 us; the launch traced here: 481 us
  Pallas kernels  453 us (94%)
  local copies, waits for them, and re-layouts  21.3 us (4%)
  other arithmetic  5.47 us (1%)
    pallas_call x1, Pallas kernels, backward(): pl.pallas_call(backward_kernel, out_shape=[jax.ShapeDtypeStruct((count,)...  251 us
    pallas_call x1, Pallas kernels, forward(): pl.pallas_call(forward_kernel, out_shape=[jax.ShapeDtypeStruct(s, d) for...  202 us
    unnamed x18, local copies, waits for them, and re-layouts  14.3 us

profile of v5, /device:TPU:0, one launch (start us, length us, event | category | flops | bytes accessed | tf_op | source)
XLA Modules:
  0.0 480.9 jit_solution(14229415171931802355)
XLA Ops:
  0.7 0.7 broadcast_select_fusion.1
  1.3 0.7 reshape.127
  2.0 0.7 reshape.126
  2.7 0.7 fusion.10.refs_7_
  3.4 0.8 copy.30
  4.1 0.1 reshape_squeeze.3
  4.3 1.4 constant_dynamic-slice_fusion.4
  5.6 1.3 fusion.13
  7.0 0.1 select_n.83
  7.1 0.1 add.78
  7.2 0.1 compare_convert_fusion
  7.3 0.8 copy.31.refs_9_
  8.0 0.1 dynamic-slice_convert_fusion
  8.1 0.3 fusion
  8.4 0.8 pad_maximum_fusion
  9.9 1.0 copy.32.refs_12_.refs_21_
  10.9 0.6 pad_add_fusion.refs_13_.refs_22_
  11.5 202.1 %forward.1 = (bf16[2,1024,4096]{2,1,0:T(8,128)(2,1)}, bf16[2,2048,1024]{2,1,0:T(8,128)(2,1)}, bf16[2,1024,6144]{2,1,0:T(8,128)(2,1)}, bf16[2,3072,1024]{2,1,0:T(...) custom-call(bf16[2,512,1024]{2,1,0:T(8,128)(2,1)} %refs_0_.1, ...), custom_call_target="tpu_custom_call" | custom-call | tf_op jit(solution)/shard_map/forward/pallas_call | solution.py:1019
  213.6 0.9 convert_multiply_fusion.refs_15_
  214.5 250.7 %backward.1 = (f32[2,32,2048]{2,1,0:T(8,128)}, f32[2,32,1024]{2,1,0:T(8,128)}, f32[2,32,1024]{2,1,0:T(8,128)}, f32[2,64,1024]{2,1,0:T(8,128)}, f32[2,32,3072]{2,...) custom-call(bf16[2,4,2,2,2,3,32,128]{7,6,5,4,3,2,1,0:T(8,128)(2,1)} , ...), custom_call_target="tpu_custom_call" | custom-call | tf_op jit(solution)/shard_map/backward/pallas_call | solution.py:1441
  465.2 0.9 reshape.133
  466.1 0.6 constant_dynamic-slice_fusion.2
  466.8 0.6 constant_dynamic-slice_fusion
  467.4 0.7 copy.43
  468.1 1.9 copy.44
  470.0 1.9 copy.45
  471.9 1.7 copy.46
  473.5 1.7 copy.47
  475.2 1.9 copy.48
  477.1 2.1 copy.49
  479.2 0.9 copy.50
  480.0 0.9 copy.51
  (12 shorter events, 0.2 us)
Async XLA Ops:
  11.5 202.1 %copy-start.3 = (bf16[128,1024]{1,0:T(8,128)(2,1)S(1)}, bf16[128,1024]{1,0:T(8,128)(2,1)}, u32[]{:S(2)}) copy-start(bf16[128,1024]{1,0:T(8,128)(2,1)} %param.16) | copy-start | bytes 786436
  214.5 252.9 %copy-start.2 = (bf16[128,1024]{1,0:T(8,128)(2,1)S(1)}, bf16[128,1024]{1,0:T(8,128)(2,1)}, u32[]{:S(2)}) copy-start(bf16[128,1024]{1,0:T(8,128)(2,1)} %get-tuple-element.104) | copy-start | bytes 786436
  465.2 13.9 %copy-start.1 = (f32[2,32,3072]{2,1,0:T(8,128)S(1)}, f32[2,32,3072]{2,1,0:T(8,128)}, u32[]{:S(2)}) copy-start(f32[2,32,3072]{2,1,0:T(8,128)} %get-tuple-element.111) | copy-start | bytes 2359300
  465.2 14.8 %copy-start = (f32[2,96,1024]{2,1,0:T(8,128)S(1)}, f32[2,96,1024]{2,1,0:T(8,128)}, u32[]{:S(2)}) copy-start(f32[2,96,1024]{2,1,0:T(8,128)} %get-tuple-element.112) | copy-start | bytes 2359300

commit v6 on v5

--- a/solution.py
+++ b/solution.py
@@ -547,40 +547,49 @@
 
         self.each(i, go)
 
-    def step(self, s):
-        shared = range(MEMBERS - 1)
-
-        def spread(m):
-            self.x_copy(s, m).wait_recv()
-            if m < MEMBERS - 1:
-                self.y_copy(s, m).start()
-                self.z_copy(s, m).start()
-            self.core_copy(s, m, 0).start()
-
-        self.each(s, spread)
-        self.send(s + LEAD)
-        i = s - 1
-
-        def corners(m):
-            self.y_copy(i, m).wait_recv()
-            self.z_corner(i, m).start()
-            self.core_copy(i, m, 1).start()
-            self.z_copy(i, m).wait_recv()
-            self.y_corner(i, m).start()
-            self.core_copy(i, m, 2).start()
-
-        self.each(i, corners, shared)
-        j = s - 2
-
-        def last(m):
-            self.y_corner(j, m).wait_recv()
-            self.z_corner(j, m).wait_recv()
-            self.core_copy(j, m, 3).start()
-
-        self.each(j, last, shared)
+    def step(self, u):
+        s = u // 3
+        stage = u % 3
+
+        @pl.when(stage == 0)
+        def first():
+            def spread(m):
+                self.x_copy(s, m).wait_recv()
+                if m < MEMBERS - 1:
+                    self.y_copy(s, m).start()
+                    self.z_copy(s, m).start()
+                self.core_copy(s, m, 0).start()
+
+            self.each(s, spread)
+            self.send(s + LEAD)
+
+        @pl.when(stage == 1)
+        def second():
+            i = s - 1
+
+            def corners(m):
+                self.y_copy(i, m).wait_recv()
+                self.z_corner(i, m).start()
+                self.core_copy(i, m, 1).start()
+                self.z_copy(i, m).wait_recv()
+                self.y_corner(i, m).start()
+                self.core_copy(i, m, 2).start()
+
+            self.each(i, corners, range(MEMBERS - 1))
+
+        @pl.when(stage == 2)
+        def third():
+            j = s - 2
+
+            def last(m):
+                self.y_corner(j, m).wait_recv()
+                self.z_corner(j, m).wait_recv()
+                self.core_copy(j, m, 3).start()
+
+            self.each(j, last, range(MEMBERS - 1))
 
     def steps(self):
-        return self.count + 2
+        return 3 * (self.count + 2)
 
     def ready(self, n, m):
         i = n * MEMBERS + m
@@ -614,15 +623,19 @@
     return pl.ds(pl.multiple_of(first + index * HEAD_SIZE, HEAD_SIZE), HEAD_SIZE)
 
 
-def stream_blocks(first, count, start, wait, body):
-    start(first, 0)
+def stream_blocks(first, count, slots, start, wait, body):
+    def fill(i, carry):
+        start(first + i, i)
+        return carry
+
+    lax.fori_loop(0, jnp.minimum(slots - 1, count), fill, 0)
 
     def one(i, carry):
-        slot = i % 2
-
-        @pl.when(i + 1 < count)
+        slot = i % slots
+
+        @pl.when(i + slots - 1 < count)
         def following():
-            start(first + i + 1, 1 - slot)
+            start(first + i + slots - 1, (i + slots - 1) % slots)
 
         wait(first + i, slot)
         body(first + i, slot)
@@ -636,25 +649,29 @@
     return values * r * gain
 
 
-FIRST_WORK = 4
-NEXT_WORK = 7
+BUFFERS = 4
+SCHEDULE = (
+    (9, 12, 15, 16, 18, 19, 20, 21, 23, 24, 25, 26, 27, 28, 29),
+    (30, 33, 36, 37, 39, 40, 41, 42, 43, 44, 45, 46, 47, 47, 48),
+)
 
 
 def forward_kernel(*refs):
     count = DECODER_LAYERS
     sources, refs = refs[:MEMBERS], refs[MEMBERS:]
-    (packed, tokens, live, cosine, sine, key_place, query_cap), refs = refs[:7], refs[7:]
+    (g_attn, g_mlp, g_query, g_key, tokens, stretch_ids, lengths), refs = refs[:7], refs[7:]
     weights, refs = refs[:4], refs[4:]
     into_w, out_w, wide_w, down_w = weights
     (both_out, middle_out, entry_out, pre_out, kept_hbm, kept_out_hbm, kept_log_hbm), refs = (
         refs[:7], refs[7:]
     )
-    (hidden_t, mid_t, attn_t, normed_t, attn_gains, mlp_gains, head_gains, output), refs = (
-        refs[:8], refs[8:]
-    )
+    (hidden_t, mid_t, attn_t, normed_t, attn_gains, mlp_gains, head_gains), refs = (
+        refs[:7], refs[7:]
+    )
+    (output, live, cosine, sine, key_place, query_cap), refs = refs[:6], refs[6:]
     sizes = len(gather_scratch(count))
     gather = Gatherer(sources, weights, refs[:sizes], count)
-    (packs, stream, middle, pre, low, attn_low, hidden_low, gate_up, cols_w, rows_w,
+    (wide_mine, wide_other, head_mine, head_other, stream, middle, pre, low, attn_low, hidden_low, gate_up, cols_w, rows_w,
      kept, kept_out, kept_log, send, osend, orecv, vt,
      pack_sem, cols_sem, rows_sem, gate_sem, save_sem,
      q_s, q_r, k_s, k_r, o_s, o_r) = refs[sizes:]
@@ -676,28 +693,59 @@
     pl.semaphore_signal(barrier, inc=1, device_id=gather.across, device_id_type=MESH)
     pl.semaphore_wait(barrier, PEERS)
 
-    pack_copy = make_remote(packed, packs, pack_sem.at[0], pack_sem.at[1], gather.across)
-    pack_copy.start()
+    for k, member in enumerate((g_attn, g_mlp)):
+        wide_mine[k] = member[...].astype(jnp.float32)
+    for k, member in enumerate((g_query, g_key)):
+        head_mine[k] = member[...].astype(jnp.float32)
+    gain_copies = (
+        make_remote(wide_mine, wide_other, pack_sem.at[0], pack_sem.at[1], gather.across),
+        make_remote(head_mine, head_other, pack_sem.at[2], pack_sem.at[3], gather.across),
+    )
+    for copy in gain_copies:
+        copy.start()
     for i in range(LEAD):
         gather.send(i)
     stream[...] = tokens[...].astype(jnp.float32)
-    pack_copy.wait_recv()
-
-    def gain_rows(first):
-        mine = [packed[first + i : first + i + 1, :] for i in range(4)]
-        other = [packs[first + i : first + i + 1, :] for i in range(4)]
-        a = jnp.concatenate(mine, axis=1)
-        b = jnp.concatenate(other, axis=1)
-        low_side = jnp.where(x == 0, a, b)
-        high_side = jnp.where(x == 0, b, a)
-        return jnp.concatenate([low_side, high_side], axis=1)
-
-    for n in range(count):
-        attn_gains[n] = gain_rows(4 * n)
-        mlp_gains[n] = gain_rows(8 + 4 * n)
-        for k in range(2):
-            row = 16 + 2 * k + n
-            head_gains[n, k : k + 1, :] = packed[row : row + 1, :] + packs[row : row + 1, :]
+
+    slot = c // PEERS
+    limit = lengths[0, slot]
+    stretches = 2 * PEERS
+    lane = lax.broadcasted_iota(jnp.int32, (1, 256), 1) % 128
+    row = lax.broadcasted_iota(jnp.int32, (128, 1), 0)
+
+    def spots(r, along):
+        first = stretch_ids[slot * PEERS + r, 0, 0] % stretches * STRETCH
+        second = stretch_ids[slot * PEERS + r, 0, 1] % stretches * STRETCH
+        return jnp.where(along < STRETCH, first, second - STRETCH) + along
+
+    for r in range(PEERS):
+        key_place[r * 128 : (r + 1) * 128, :] = spots(r, row)
+        query_cap[r] = jnp.minimum(spots(r, lane), limit - 1)
+    mine = spots(me, row)
+    live[...] = jnp.where(mine < limit, 1.0, 0.0)
+    half = HEAD_SIZE // 2
+    column = lax.broadcasted_iota(jnp.int32, (1, HEAD_SIZE), 1)
+    spread = (column % half).astype(jnp.float32) * (2.0 / HEAD_SIZE)
+    angles = mine.astype(jnp.float32) * jnp.exp(spread * -math.log(rope_base))
+    cosine[...] = jnp.cos(angles)
+    sine[...] = jnp.where(column < half, -jnp.sin(angles), jnp.sin(angles))
+
+    for copy in gain_copies:
+        copy.wait_recv()
+    low_side = jnp.where(x == 0, 0, 1)
+
+    def pick(first, second, flip):
+        return jnp.where(low_side == flip, first, second)
+
+    for k, target in enumerate((attn_gains, mlp_gains)):
+        sides = [pick(wide_mine[k], wide_other[k], flip) for flip in range(2)]
+        for n in range(count):
+            target[n] = jnp.concatenate([side[n : n + 1] for side in sides], axis=1)
+    for k in range(2):
+        for flip in range(2):
+            side = pick(head_mine[k], head_other[k], flip)
+            for n in range(count):
+                head_gains[n, k : k + 1, flip * half : (flip + 1) * half] = side[n : n + 1]
 
     cos = cosine[...]
     sin = sine[...]
@@ -744,37 +792,39 @@
     def out_copy(r, slot):
         return make_remote(osend.at[r], orecv.at[slot], o_s.at[r], o_r.at[slot], peer(r))
 
-    def project(n):
+    def project(n, first, blocks):
+        def body(i, slot):
+            pre[:, pl.ds(pl.multiple_of(i * 512, 512), 512)] = jnp.dot(
+                low[...], cols_w[slot], preferred_element_type=jnp.float32
+            )
+
+        stream_blocks(
+            first,
+            blocks,
+            BUFFERS,
+            lambda i, slot: cols_copy(into_w, n, i * 512, slot).start(),
+            lambda i, slot: cols_copy(into_w, n, i * 512, slot).wait(),
+            body,
+        )
+
+    def turned(n, first, index, k):
+        v = rms(pre[:, head_columns(first, index)], head_gains[n, k : k + 1, :])
+        return (v * cos + pltpu.roll(v, HEAD_SIZE // 2, 1) * sin).astype(jnp.bfloat16)
+
+    def keys_part(n):
         save(n, 0).start()
         low[...] = rms(stream[...], attn_gains[n]).astype(jnp.bfloat16)
         turn(low, normed_t, n, 8)
-        for m in range(3):
-            gather.ready(n, m)
-
-        def column(i):
-            return (i + 4) % 8 * 512
-
-        def body(i, slot):
-            pre[:, pl.ds(pl.multiple_of(column(i), 512), 512)] = jnp.dot(
-                low[...], cols_w[slot], preferred_element_type=jnp.float32
-            )
-
-        stream_blocks(
-            0,
-            8,
-            lambda i, slot: cols_copy(into_w, n, column(i), slot).start(),
-            lambda i, slot: cols_copy(into_w, n, column(i), slot).wait(),
-            body,
-        )
-        save(n, 1).start()
-
-        def turned(first, index, gain):
-            v = rms(pre[:, head_columns(first, index)], gain)
-            return (v * cos + pltpu.roll(v, HEAD_SIZE // 2, 1) * sin).astype(jnp.bfloat16)
+        gather.ready(n, 0)
+        project(n, 4, 2)
+
+    def values_part(n):
+        gather.ready(n, 1)
+        project(n, 6, 2)
 
         def make_keys(o, carry):
             r = (me + o) % PEERS
-            key = turned(2048, r, head_gains[n, 1:2, :])
+            key = turned(n, 2048, r, 1)
             value = pre[:, head_columns(3072, r)].astype(jnp.bfloat16)
 
             @pl.when(o < PEERS)
@@ -790,10 +840,18 @@
 
             return carry
 
+        lax.fori_loop(1, PEERS + 1, make_keys, 0)
+
+    def queries_part(n):
+        gather.ready(n, 2)
+        project(n, 0, 4)
+        save(n, 1).start()
+
+    def spread_queries(n):
         def make_queries(o, carry):
             r = (me + o) % PEERS
-            first = turned(0, 2 * r, head_gains[n, 0:1, :])
-            second = turned(0, 2 * r + 1, head_gains[n, 0:1, :])
+            first = turned(n, 0, 2 * r, 0)
+            second = turned(n, 0, 2 * r + 1, 0)
 
             @pl.when(o < PEERS)
             def away():
@@ -808,21 +866,21 @@
 
             return carry
 
-        lax.fori_loop(1, PEERS + 1, make_keys, 0)
         lax.fori_loop(1, PEERS + 1, make_queries, 0)
 
-    def attention(n):
+    def attention(n, part):
         def await_keys(o, carry):
             key_copy(n, me, (me + o) % PEERS).wait_recv()
             return carry
 
-        lax.fori_loop(1, PEERS, await_keys, 0)
-
         def turn_values(j, carry):
             vt[j] = kept[n, j, 3].astype(jnp.float32).T.astype(jnp.bfloat16)
             return carry
 
-        lax.fori_loop(0, PEERS, turn_values, 0)
+        @pl.when(part == 0)
+        def opening():
+            lax.fori_loop(1, PEERS, await_keys, 0)
+            lax.fori_loop(0, PEERS, turn_values, 0)
 
         def block(o, carry):
             j = (me + o) % PEERS
@@ -861,10 +919,13 @@
 
             return carry
 
-        lax.fori_loop(0, PEERS, block, 0)
-        save(n, 3).start()
-        save(n, 4).start()
-        save_kept(n).start()
+        lax.fori_loop(2 * part, 2 * part + 2, block, 0)
+
+        @pl.when(part == 3)
+        def closing():
+            save(n, 3).start()
+            save(n, 4).start()
+            save_kept(n).start()
 
     def close_attention(n):
         def collect(o, carry):
@@ -892,11 +953,14 @@
         stream_blocks(
             0,
             4,
+            BUFFERS,
             lambda i, slot: rows_copy(out_w, n, i, slot).start(),
             lambda i, slot: rows_copy(out_w, n, i, slot).wait(),
             body,
         )
         save(n, 2).start()
+
+    def middle_norm(n):
         turn(attn_low, attn_t, n, 16)
         low[...] = rms(middle[...], mlp_gains[n]).astype(jnp.bfloat16)
         turn(low, mid_t, n, 8)
@@ -916,9 +980,11 @@
             gate_up.at[slot, k], both_out.at[n, :, columns], gate_sem.at[slot, k]
         )
 
-    def widen(n):
-        gather.ready(n, 4)
-        gather.ready(n, 5)
+    def widen(n, part):
+        @pl.when(part == 0)
+        def opening():
+            gather.ready(n, 4)
+            gather.ready(n, 5)
 
         def column(i):
             return i % 2 * 3072 + i // 2 * 512
@@ -946,18 +1012,23 @@
                 ).astype(jnp.bfloat16)
 
         stream_blocks(
-            0,
-            12,
+            4 * part,
+            4,
+            BUFFERS,
             lambda i, slot: cols_copy(wide_w, n, column(i), slot).start(),
             lambda i, slot: cols_copy(wide_w, n, column(i), slot).wait(),
             body,
         )
-        for at in (4, 5):
-            for k in range(2):
-                gate_copy(n, at, at % 2, k).wait()
+        @pl.when(part == 2)
+        def closing():
+            for at in (4, 5):
+                for k in range(2):
+                    gate_copy(n, at, at % 2, k).wait()
+
+    def turn_hidden(n):
+        turn(hidden_low, hidden_t, n, 24)
 
     def narrow(n):
-        turn(hidden_low, hidden_t, n, 24)
         gather.ready(n, 6)
         stream[...] = middle[...]
 
@@ -970,6 +1041,7 @@
         stream_blocks(
             0,
             6,
+            BUFFERS,
             lambda i, slot: rows_copy(down_w, n, i, slot).start(),
             lambda i, slot: rows_copy(down_w, n, i, slot).wait(),
             body,
@@ -978,25 +1050,46 @@
             save(n, k).wait()
         save_kept(n).wait()
 
-    def step(w, carry):
-        gather.step(w)
-        n = jnp.where(w >= FIRST_WORK + NEXT_WORK, 1, 0)
-        phase = w - FIRST_WORK - n * NEXT_WORK
-        for at, work in enumerate((project, attention, close_attention, widen, narrow)):
-
-            @pl.when(phase == at)
-            def piece(work=work):
-                work(n)
-
+    def when_at(u, index):
+        return (u == SCHEDULE[0][index]) | (u == SCHEDULE[1][index])
+
+    def at_among(u, first, blocks):
+        part = jnp.zeros((), jnp.int32)
+        for k in range(blocks):
+            part = jnp.where(when_at(u, first + k), k, part)
+        chosen = functools.reduce(jnp.logical_or, [when_at(u, first + k) for k in range(blocks)])
+        return chosen, part
+
+    def step(u, carry):
+        gather.step(u)
+        n = jnp.where(u >= SCHEDULE[1][0], 1, 0)
+        pieces = (
+            (1, keys_part), (1, values_part), (1, queries_part), (1, spread_queries),
+            (4, attention), (1, close_attention), (1, middle_norm), (3, widen), (1, turn_hidden),
+            (1, narrow),
+        )
+        index = 0
+        for blocks, work in pieces:
+            chosen, part = at_among(u, index, blocks)
+
+            @pl.when(chosen)
+            def piece(blocks=blocks, work=work, part=part):
+                if blocks == 1:
+                    work(n)
+                else:
+                    work(n, part)
+
+            index += blocks
         return carry
 
-    lax.fori_loop(0, FIRST_WORK + NEXT_WORK + 5, step, 0)
+    lax.fori_loop(0, SCHEDULE[1][-1] + 1, step, 0)
     output[...] = (stream[...] * live[...]).astype(jnp.bfloat16)
     gather.drain()
-    pack_copy.wait_send()
-
-
-def forward(weights, packed, tokens, live, cosine, sine, key_place, query_cap, number):
+    for copy in gain_copies:
+        copy.wait_send()
+
+
+def forward(weights, gains, tokens, stretch_ids, lengths, number):
     count = DECODER_LAYERS
     dma = pltpu.SemaphoreType.DMA
     low, wide = jnp.bfloat16, jnp.float32
@@ -1014,16 +1107,21 @@
         + [((count,) + s, d) for s, d in saved]
         + [((count,) + s, low) for s in turned]
         + [((count, 1, 1024), wide)] * 2
-        + [((count, 2, HEAD_SIZE), wide), ((128, 1024), low)]
+        + [((count, 2, HEAD_SIZE), wide), ((128, 1024), low), ((128, 1), wide)]
+        + [((128, HEAD_SIZE), wide)] * 2
+        + [((PEERS * 128, 1), jnp.int32), ((PEERS, 1, 256), jnp.int32)]
     )
     return pl.pallas_call(
         forward_kernel,
         out_shape=[jax.ShapeDtypeStruct(s, d) for s, d in results],
-        in_specs=[anywhere] * MEMBERS + [near] * 7,
-        out_specs=[anywhere] * 11 + [near] * 8,
+        in_specs=[anywhere] * MEMBERS + [near] * 5 + [pl.BlockSpec(memory_space=pltpu.SMEM)] * 2,
+        out_specs=[anywhere] * 11 + [near] * 13,
         scratch_shapes=gather_scratch(count)
         + [
-            pltpu.VMEM(packed.shape, wide),
+            pltpu.VMEM((2, count, 512), wide),
+            pltpu.VMEM((2, count, 512), wide),
+            pltpu.VMEM((2, count, 64), wide),
+            pltpu.VMEM((2, count, 64), wide),
             pltpu.VMEM((128, 1024), wide),
             pltpu.VMEM((128, 1024), wide),
             pltpu.VMEM((128, 4096), wide),
@@ -1031,8 +1129,8 @@
             pltpu.VMEM((128, 2048), low),
             pltpu.VMEM((128, 3072), low),
             pltpu.VMEM((2, 2, 128, 512), wide),
-            pltpu.VMEM((2, 1024, 512), low),
-            pltpu.VMEM((2, 512, 1024), low),
+            pltpu.VMEM((BUFFERS, 1024, 512), low),
+            pltpu.VMEM((BUFFERS, 512, 1024), low),
             pltpu.VMEM((count, PEERS, 4, 128, HEAD_SIZE), low),
             pltpu.VMEM((PEERS, HEAD_SIZE, 256), wide),
             pltpu.VMEM((PEERS, 8, 256), wide),
@@ -1040,14 +1138,14 @@
             pair,
             pair,
             pltpu.VMEM((PEERS, HEAD_SIZE, 128), low),
-            dma((2,)), dma((2,)), dma((2,)), dma((2, 2)), dma((6,)),
+            dma((4,)), dma((BUFFERS,)), dma((BUFFERS,)), dma((2, 2)), dma((6,)),
         ]
         + [dma((PEERS,))] * 6,
         compiler_params=pltpu.CompilerParams(
             collective_id=number, has_side_effects=True, vmem_limit_bytes=56 * 2**20
         ),
         name="forward",
-    )(*weights, packed, tokens, live, cosine, sine, key_place, query_cap)
+    )(*weights, *gains, tokens, stretch_ids, lengths)
 
 
 WORK = 12
@@ -1065,10 +1163,12 @@
     count = DECODER_LAYERS
     acts, stored, refs = refs[:4], refs[4:11], refs[11:]
     (into_w, out_w, wide_w, down_w) = refs[:4]
-    (upstream, cosine, sine, attn_gains, mlp_gains, head_gains, key_place, query_cap) = refs[4:12]
-    results = refs[12:19]
-    grad_stream, gain_out, held = refs[19:22]
-    refs = refs[22:]
+    (cotangent, attn_gains, mlp_gains, head_gains, live, cosine, sine, key_place, query_cap) = (
+        refs[4:13]
+    )
+    results = refs[13:20]
+    grad_stream, gain_out, held = refs[20:23]
+    refs = refs[23:]
     sizes = len(reduce_scratch(count))
     reduce_refs, refs = refs[:sizes], refs[sizes:]
     gain_refs, refs = refs[:4], refs[4:]
@@ -1102,7 +1202,7 @@
         pl.semaphore_signal(barrier, inc=1, device_id=(far, x), device_id_type=MESH)
     pl.semaphore_wait(barrier, PEERS + 2)
 
-    grad_stream[...] = upstream[...]
+    grad_stream[...] = cotangent[...].astype(jnp.float32) * live[...]
     terms[...] = jnp.zeros_like(terms)
     reducer.start_acts(0, (0,))
 
@@ -1184,7 +1284,7 @@
                 jnp.bfloat16
             )
 
-        stream_blocks(part * 3, 3, start, wait, body)
+        stream_blocks(part * 3, 3, 2, start, wait, body)
 
         @pl.when((n == 0) & (part == 1))
         def rest():
@@ -1199,6 +1299,7 @@
         stream_blocks(
             part * 3,
             jnp.where(part == 2, 2, 3),
+            2,
             lambda i, slot: wide_copy(wide_w, layer, i, slot).start(),
             lambda i, slot: wide_copy(wide_w, layer, i, slot).wait(),
             body,
@@ -1240,6 +1341,7 @@
         stream_blocks(
             0,
             4,
+            2,
             lambda i, slot: rows_copy(out_w, layer, place(i), slot).start(),
             lambda i, slot: rows_copy(out_w, layer, place(i), slot).wait(),
             body,
@@ -1371,6 +1473,7 @@
         stream_blocks(
             part * 4,
             4,
+            2,
             lambda i, slot: wide_copy(into_w, layer, i, slot).start(),
             lambda i, slot: wide_copy(into_w, layer, i, slot).wait(),
             body,
@@ -1431,7 +1534,7 @@
 RESULTS = ((32, 2048), (32, 1024), (32, 1024), (64, 1024), (32, 3072), (32, 3072), (96, 1024))
 
 
-def backward(acts, saved, weights, upstream, cosine, sine, gains, key_place, query_cap, number):
+def backward(acts, saved, weights, cotangent, gains, tables, number):
     count = DECODER_LAYERS
     dma = pltpu.SemaphoreType.DMA
     low, wide = jnp.bfloat16, jnp.float32
@@ -1446,7 +1549,7 @@
             jax.ShapeDtypeStruct((24 * count, 128), wide),
             jax.ShapeDtypeStruct((GRADS * count, 384, 1024), low),
         ],
-        in_specs=[anywhere] * 15 + [near] * 8,
+        in_specs=[anywhere] * 15 + [near] * 9,
         out_specs=[near] * 9 + [anywhere],
         scratch_shapes=reduce_scratch(count)
         + gain_scratch(24 * count)
@@ -1479,7 +1582,56 @@
             collective_id=number, has_side_effects=True, vmem_limit_bytes=62 * 2**20
         ),
         name="backward",
-    )(*acts, *saved, *weights, upstream, cosine, sine, *gains, key_place, query_cap)
+    )(*acts, *saved, *weights, cotangent, *gains, *tables)
+
+
+def finish_kernel(*refs):
+    count = DECODER_LAYERS
+    moved, sums = refs[:9], refs[9]
+    outs, gain_outs = refs[10:19], refs[19:23]
+    held, sems = refs[23:32], refs[32]
+
+    def into(k):
+        return pltpu.make_async_copy(moved[k], held[k], sems.at[0, k])
+
+    def onward(k):
+        return pltpu.make_async_copy(held[k], outs[k], sems.at[1, k])
+
+    for k in range(9):
+        into(k).start()
+    for k in range(9):
+        into(k).wait()
+        onward(k).start()
+    place = lax.axis_index("ctx") * 2 + lax.axis_index("fsdp")
+
+    def cut(row, offset, span):
+        values = sums[pl.ds(row, 1), :]
+        return pltpu.roll(values, (128 - offset) % 128, 1)[:, :span]
+
+    for n in range(count):
+        first = 24 * n
+        for k in range(2):
+            gain_outs[k][n : n + 1, :] = cut(first + 8 * k + place // 4, place % 4 * 32, 32)
+            gain_outs[2 + k][n : n + 1, :] = cut(first + 16 + k, place * 4, 4)
+    for k in range(9):
+        onward(k).wait()
+
+
+def finish(moved, sums):
+    count = DECODER_LAYERS
+    anywhere = pl.BlockSpec(memory_space=pl.ANY)
+    near = pl.BlockSpec(memory_space=pltpu.VMEM)
+    return pl.pallas_call(
+        finish_kernel,
+        out_shape=[jax.ShapeDtypeStruct(member.shape, member.dtype) for member in moved]
+        + [jax.ShapeDtypeStruct((count, span), jnp.float32) for span in (32, 32, 4, 4)],
+        in_specs=[anywhere] * 9 + [near],
+        out_specs=[anywhere] * 9 + [near] * 4,
+        scratch_shapes=[pltpu.VMEM(member.shape, member.dtype) for member in moved]
+        + [pltpu.SemaphoreType.DMA((2, 9))],
+        compiler_params=pltpu.CompilerParams(vmem_limit_bytes=60 * 2**20),
+        name="finish",
+    )(*moved, sums)
 
 
 def from_partner(shard, axis, apart):
@@ -1973,71 +2125,24 @@
     g_query,
     g_key,
 ):
-    count_rows, width = tokens.shape
-    ctx_index = lax.axis_index("ctx")
-    places, slot_ids, live = token_places(stretch_ids[:, 0, :], lengths[0])
-    group_rows = PEERS * count_rows
-    base_row = ctx_index // PEERS * group_rows
-    my_row = ctx_index * count_rows
-    slot_places = lax.dynamic_slice_in_dim(places, base_row, group_rows)
-    limit = lax.dynamic_slice_in_dim(lengths[0], ctx_index // PEERS, 1)
-    caps = jnp.minimum(slot_places, limit - 1).reshape(PEERS, 1, count_rows)
-    query_cap = jnp.concatenate([caps, caps], axis=2)
-    key_place = slot_places[:, None]
-    live_mine = lax.dynamic_slice_in_dim(live, my_row, count_rows).astype(jnp.float32)[:, None]
-    cosine, sine = rotary_tables(lax.dynamic_slice_in_dim(places, my_row, count_rows))
-    half = HEAD_SIZE // 2
-    sine = jnp.concatenate([-sine[:, :half], sine[:, half:]], axis=1)
-
-    mesh_x = lax.axis_index("fsdp")
-    rows = [member.reshape(-1, 128) for member in (g_attn, g_mlp)]
-    for member in (g_query, g_key):
-        zero = jnp.zeros_like(member)
-        rows.append(
-            jnp.concatenate(
-                [jnp.where(mesh_x == 0, member, zero), jnp.where(mesh_x == 0, zero, member)], axis=1
-            )
-        )
-    packed = jnp.pad(jnp.concatenate(rows, axis=0).astype(jnp.float32), ((0, 4), (0, 0)))
     results = forward(
         (key_projection_weight, value_projection_weight, w_query, w_out, w_gate, w_up, w_down),
-        packed,
+        (g_attn, g_mlp, g_query, g_key),
         tokens,
-        live_mine,
-        cosine,
-        sine,
-        key_place,
-        query_cap,
+        stretch_ids,
+        lengths,
         1,
     )
-    gathered, saved, turned, gains, output_low = (
-        results[:4], results[4:11], results[11:15], results[15:18], results[18]
+    gathered, saved, turned, gains, output_low, tables = (
+        results[:4], results[4:11], results[11:15], results[15:18], results[18], results[19:]
     )
     acts = [
-        member.reshape(DECODER_LAYERS, 4, 2, 2, 2, -1, 32, count_rows) for member in turned
+        member.reshape(DECODER_LAYERS, 4, 2, 2, 2, -1, 32, tokens.shape[0]) for member in turned
     ]
-
-    place = ctx_index * 2 + mesh_x
     *weight_sums, grad_stream, sums, unused = backward(
-        acts,
-        saved,
-        gathered,
-        cotangent.astype(jnp.float32) * live_mine,
-        cosine,
-        sine,
-        gains,
-        key_place,
-        query_cap,
-        2,
-    )
-    sums = sums.reshape(DECODER_LAYERS, -1)
-
-    def share(first, span):
-        return lax.dynamic_slice_in_dim(sums, first + place * span, span, axis=1)
-
-    return (output_low, grad_stream) + tuple(weight_sums) + (
-        share(0, 32), share(1024, 32), share(2048, 4), share(2176, 4)
-    )
+        acts, saved, gathered, cotangent, gains, tables, 2
+    )
+    return tuple(finish((output_low, grad_stream, *weight_sums), sums))
 
 
 def solution(mesh):

time: 483 us -> 460 us (0.952)
  local copies, waits for them, and re-layouts: 21.3 us -> 1.35 us
  other arithmetic: 5.47 us -> 0 us
    unnamed x18 -> x1, local copies, waits for them, and re-layouts: 14.3 us -> 1.35 us
    pallas_call x0 -> x1, Pallas kernels: none -> 5.7 us  [finish(): pl.pallas_call(finish_kernel, out_shape=[jax.ShapeDtypeStruct(member.shap...]
where the time goes in v6:
time: 460 us; the launch traced here: 459 us
  Pallas kernels  457 us (99%)
    pallas_call x1, Pallas kernels, backward(): pl.pallas_call(backward_kernel, out_shape=[jax.ShapeDtypeStruct((count,)...  253 us
    pallas_call x1, Pallas kernels, forward(): pl.pallas_call(forward_kernel, out_shape=[jax.ShapeDtypeStruct(s, d) for...  198 us

profile of v6, /device:TPU:0, one launch (start us, length us, event | category | flops | bytes accessed | tf_op | source)
XLA Modules:
  0.0 458.8 jit_solution(12745137447560113182)
XLA Ops:
  0.6 1.4 copy.28.refs_12_
  2.0 198.0 %forward.1 = (bf16[2,1024,4096]{2,1,0:T(8,128)(2,1)}, bf16[2,2048,1024]{2,1,0:T(8,128)(2,1)}, bf16[2,1024,6144]{2,1,0:T(8,128)(2,1)}, bf16[2,3072,1024]{2,1,0:T(...) custom-call(bf16[2,512,1024]{2,1,0:T(8,128)(2,1)} %refs_0_.1, ...), custom_call_target="tpu_custom_call" | custom-call | tf_op jit(solution)/shard_map/forward/pallas_call | solution.py:1114
  200.0 253.1 %backward.1 = (f32[2,32,2048]{2,1,0:T(8,128)}, f32[2,32,1024]{2,1,0:T(8,128)}, f32[2,32,1024]{2,1,0:T(8,128)}, f32[2,64,1024]{2,1,0:T(8,128)}, f32[2,32,3072]{2,...) custom-call(bf16[2,4,2,2,2,3,32,128]{7,6,5,4,3,2,1,0:T(8,128)(2,1)} , ...), custom_call_target="tpu_custom_call" | custom-call | tf_op jit(solution)/shard_map/backward/pallas_call | solution.py:1544
  453.1 5.7 %finish.1 = (bf16[128,1024]{1,0:T(8,128)(2,1)}, f32[128,1024]{1,0:T(8,128)}, f32[2,32,2048]{2,1,0:T(8,128)}, f32[2,32,1024]{2,1,0:T(8,128)}, f32[2,32,1024]{2,1,...) custom-call(bf16[128,1024]{1,0:T(8,128)(2,1)} %get-tuple-element.46., ...), custom_call_target="tpu_custom_call" | custom-call | tf_op jit(solution)/shard_map/finish/pallas_call | solution.py:1624

commit v7 on v6

--- a/solution.py
+++ b/solution.py
@@ -438,12 +438,14 @@
 
 GATHER_PLAN = ((0, 2048), (0, 3072), (0, 0), (1, 0), (2, 0), (2, 3072), (3, 0))
 MEMBERS = len(GATHER_PLAN)
-LEAD = 3
+ORDER = tuple((n, m) for n in range(2) for m in range(MEMBERS))
+ALONE = tuple(i for i, member in enumerate(ORDER) if member[1] == MEMBERS - 1)
+LEAD = 4
 
 
 class Gatherer:
-    def __init__(self, sources, outs, sems, count):
-        self.sources, self.outs, self.count = sources, outs, count * MEMBERS
+    def __init__(self, sources, outs, sems):
+        self.sources, self.outs = sources, outs
         (self.l_s, self.l_r, self.x_s, self.x_r, self.y_s, self.y_r, self.z_s, self.z_r,
          self.yc_s, self.yc_r, self.zc_s, self.zc_r, self.c_s, self.c_r) = sems
         c = lax.axis_index("ctx")
@@ -461,91 +463,83 @@
         self.by_z = (1 - near) * 2 + y
         self.corner = (1 - near) * 2 + 1 - y
 
-    def partners(self):
-        return (self.sibling, self.across, self.aside, self.along)
-
-    def window(self, i, m, owner_x, piece, share=None):
+    def rows(self, i, owner_x, start, rows):
+        n, m = ORDER[i]
         target, column = GATHER_PLAN[m]
         half, width = self.sources[m].shape[1], self.sources[m].shape[2]
+        return self.outs[target].at[
+            n, pl.ds(pl.multiple_of(owner_x * half + start, 16), rows), pl.ds(column, width)
+        ]
+
+    def window(self, i, owner_x, piece, share=None):
+        half = self.sources[ORDER[i][1]].shape[1]
+        if i in ALONE:
+            return self.rows(i, owner_x, self.core * (half // 2), half // 2)
         rows = half // 8
-        start = owner_x * half + (piece * 2 + self.core) * rows
+        start = (piece * 2 + self.core) * rows
         if share is not None:
             rows = rows // 2
             start = start + share * rows
-        return self.outs[target].at[
-            i // MEMBERS, pl.ds(pl.multiple_of(start, 16), rows), pl.ds(column, width)
-        ]
-
-    def direct(self, i, m, owner_x):
-        target, column = GATHER_PLAN[m]
-        half, width = self.sources[m].shape[1], self.sources[m].shape[2]
-        start = owner_x * half + self.core * (half // 2)
-        return self.outs[target].at[
-            i // MEMBERS, pl.ds(pl.multiple_of(start, 16), half // 2), pl.ds(column, width)
-        ]
-
-    def local(self, i, m):
-        target, column = GATHER_PLAN[m]
-        half, width = self.sources[m].shape[1], self.sources[m].shape[2]
-        rows = pl.ds(pl.multiple_of(self.x * half, 16), half)
+        return self.rows(i, owner_x, start, rows)
+
+    def local(self, i):
+        n, m = ORDER[i]
+        half = self.sources[m].shape[1]
         return make_remote(
-            self.sources[m].at[i // MEMBERS],
-            self.outs[target].at[i // MEMBERS, rows, pl.ds(column, width)],
-            self.l_s.at[i], self.l_r.at[i], self.sibling,
-        )
-
-    def x_copy(self, i, m):
+            self.sources[m].at[n], self.rows(i, self.x, 0, half), self.l_s.at[i], self.l_r.at[i],
+            self.sibling,
+        )
+
+    def x_copy(self, i):
+        n, m = ORDER[i]
         half = self.sources[m].shape[1]
-        if m == MEMBERS - 1:
+        if i in ALONE:
             rows = pl.ds(pl.multiple_of(self.core * (half // 2), 16), half // 2)
-            view = self.direct(i, m, self.x)
         else:
             rows = pl.ds(pl.multiple_of((self.here * 2 + self.core) * (half // 8), 16), half // 8)
-            view = self.window(i, m, self.x, self.here)
         return make_remote(
-            self.sources[m].at[i // MEMBERS, rows], view, self.x_s.at[i], self.x_r.at[i],
-            self.across,
-        )
-
-    def y_copy(self, i, m):
-        view = self.window(i, m, 1 - self.x, self.here)
+            self.sources[m].at[n, rows], self.window(i, self.x, self.here), self.x_s.at[i],
+            self.x_r.at[i], self.across,
+        )
+
+    def y_copy(self, i):
+        view = self.window(i, 1 - self.x, self.here)
         return make_remote(view, view, self.y_s.at[i], self.y_r.at[i], self.aside)
 
-    def z_copy(self, i, m):
-        view = self.window(i, m, 1 - self.x, self.here)
+    def z_copy(self, i):
+        view = self.window(i, 1 - self.x, self.here)
         return make_remote(view, view, self.z_s.at[i], self.z_r.at[i], self.along)
 
-    def y_corner(self, i, m):
-        view = self.window(i, m, 1 - self.x, self.by_z, 1)
+    def y_corner(self, i):
+        view = self.window(i, 1 - self.x, self.by_z, 1)
         return make_remote(view, view, self.yc_s.at[i], self.yc_r.at[i], self.aside)
 
-    def z_corner(self, i, m):
-        view = self.window(i, m, 1 - self.x, self.by_y, 0)
+    def z_corner(self, i):
+        view = self.window(i, 1 - self.x, self.by_y, 0)
         return make_remote(view, view, self.zc_s.at[i], self.zc_r.at[i], self.along)
 
-    def core_copy(self, i, m, which):
-        if m == MEMBERS - 1:
-            view = self.direct(i, m, 1 - self.x)
-        else:
-            piece = (self.here, self.by_y, self.by_z, self.corner)[which]
-            view = self.window(i, m, 1 - self.x, piece)
+    def core_copy(self, i, which):
+        piece = (self.here, self.by_y, self.by_z, self.corner)[which]
+        view = self.window(i, 1 - self.x, piece)
         return make_remote(
             view, view, self.c_s.at[i, which], self.c_r.at[i, which], self.sibling
         )
 
-    def each(self, i, act, members=range(MEMBERS)):
-        for m in members:
-
-            @pl.when((i >= 0) & (i < self.count) & (i % MEMBERS == m))
-            def member(m=m):
-                act(m)
+    def each(self, i, act, alone=False):
+        for place in range(len(ORDER)):
+            if place in ALONE and not alone:
+                continue
+
+            @pl.when(i == place)
+            def member(place=place):
+                act(place)
 
     def send(self, i):
-        def go(m):
-            self.x_copy(i, m).start()
-            self.local(i, m).start()
-
-        self.each(i, go)
+        def go(i):
+            self.x_copy(i).start()
+            self.local(i).start()
+
+        self.each(i, go, True)
 
     def step(self, u):
         s = u // 3
@@ -553,70 +547,69 @@
 
         @pl.when(stage == 0)
         def first():
-            def spread(m):
-                self.x_copy(s, m).wait_recv()
-                if m < MEMBERS - 1:
-                    self.y_copy(s, m).start()
-                    self.z_copy(s, m).start()
-                self.core_copy(s, m, 0).start()
+            def spread(i):
+                self.x_copy(i).wait_recv()
+                self.y_copy(i).start()
+                self.z_copy(i).start()
+                self.core_copy(i, 0).start()
 
             self.each(s, spread)
             self.send(s + LEAD)
 
         @pl.when(stage == 1)
         def second():
-            i = s - 1
-
-            def corners(m):
-                self.y_copy(i, m).wait_recv()
-                self.z_corner(i, m).start()
-                self.core_copy(i, m, 1).start()
-                self.z_copy(i, m).wait_recv()
-                self.y_corner(i, m).start()
-                self.core_copy(i, m, 2).start()
-
-            self.each(i, corners, range(MEMBERS - 1))
+            def corners(i):
+                self.y_copy(i).wait_recv()
+                self.z_corner(i).start()
+                self.core_copy(i, 1).start()
+                self.z_copy(i).wait_recv()
+                self.y_corner(i).start()
+                self.core_copy(i, 2).start()
+
+            self.each(s - 1, corners)
 
         @pl.when(stage == 2)
         def third():
-            j = s - 2
-
-            def last(m):
-                self.y_corner(j, m).wait_recv()
-                self.z_corner(j, m).wait_recv()
-                self.core_copy(j, m, 3).start()
-
-            self.each(j, last, range(MEMBERS - 1))
-
-    def steps(self):
-        return 3 * (self.count + 2)
+            def last(i):
+                self.y_corner(i).wait_recv()
+                self.z_corner(i).wait_recv()
+                self.core_copy(i, 3).start()
+
+            self.each(s - 2, last)
+
+    def pass_on(self, n, m):
+        for i in ALONE:
+            if ORDER[i][1] == m:
+
+                @pl.when(n == ORDER[i][0])
+                def member(i=i):
+                    self.x_copy(i).wait_recv()
+                    self.core_copy(i, 0).start()
 
     def ready(self, n, m):
-        i = n * MEMBERS + m
-        self.local(i, m).wait_recv()
-        for which in range(1 if m == MEMBERS - 1 else 4):
-            self.core_copy(i, m, which).wait_recv()
+        for i in range(len(ORDER)):
+            if ORDER[i][1] == m:
+
+                @pl.when(n == ORDER[i][0])
+                def member(i=i):
+                    self.local(i).wait_recv()
+                    for which in range(4 if i not in ALONE else 1):
+                        self.core_copy(i, which).wait_recv()
 
     def drain(self):
-        def one(i, carry):
-            def go(m):
-                self.local(i, m).wait_send()
-                self.x_copy(i, m).wait_send()
-                if m < MEMBERS - 1:
-                    for copy in (self.y_copy, self.z_copy, self.y_corner, self.z_corner):
-                        copy(i, m).wait_send()
-                for which in range(1 if m == MEMBERS - 1 else 4):
-                    self.core_copy(i, m, which).wait_send()
-
-            self.each(i, go)
-            return carry
-
-        lax.fori_loop(0, self.count, one, 0)
-
-
-def gather_scratch(count):
+        for i in range(len(ORDER)):
+            self.local(i).wait_send()
+            self.x_copy(i).wait_send()
+            if i not in ALONE:
+                for copy in (self.y_copy, self.z_copy, self.y_corner, self.z_corner):
+                    copy(i).wait_send()
+            for which in range(4 if i not in ALONE else 1):
+                self.core_copy(i, which).wait_send()
+
+
+def gather_scratch():
     dma = pltpu.SemaphoreType.DMA
-    return [dma((count * MEMBERS,))] * 12 + [dma((count * MEMBERS, 4))] * 2
+    return [dma((len(ORDER),))] * 12 + [dma((len(ORDER), 4))] * 2
 
 
 def head_columns(first, index):
@@ -651,8 +644,8 @@
 
 BUFFERS = 4
 SCHEDULE = (
-    (9, 12, 15, 16, 18, 19, 20, 21, 23, 24, 25, 26, 27, 28, 29),
-    (30, 33, 36, 37, 39, 40, 41, 42, 43, 44, 45, 46, 47, 47, 48),
+    (9, 12, 15, 16, 20, 21, 22, 23, 28, 29, 31, 32, 33, 34, 35, 36),
+    (37, 37, 38, 38, 42, 43, 44, 45, 46, 46, 46, 47, 48, 49, 49, 50),
 )
 
 
@@ -669,11 +662,11 @@
         refs[:7], refs[7:]
     )
     (output, live, cosine, sine, key_place, query_cap), refs = refs[:6], refs[6:]
-    sizes = len(gather_scratch(count))
-    gather = Gatherer(sources, weights, refs[:sizes], count)
-    (wide_mine, wide_other, head_mine, head_other, stream, middle, pre, low, attn_low, hidden_low, gate_up, cols_w, rows_w,
+    sizes = len(gather_scratch())
+    gather = Gatherer(sources, weights, refs[:sizes])
+    (wide_mine, wide_other, head_mine, head_other, stream, middle, pre, low, attn_low, hidden_low, both, cols_w, rows_w,
      kept, kept_out, kept_log, send, osend, orecv, vt,
-     pack_sem, cols_sem, rows_sem, gate_sem, save_sem,
+     pack_sem, cols_sem, rows_sem, save_sem,
      q_s, q_r, k_s, k_r, o_s, o_r) = refs[sizes:]
     c = lax.axis_index("ctx")
     x = lax.axis_index("fsdp")
@@ -762,14 +755,14 @@
 
     saves = (
         (stream, entry_out), (pre, pre_out), (middle, middle_out), (kept_out, kept_out_hbm),
-        (kept_log, kept_log_hbm),
+        (kept_log, kept_log_hbm), (both, both_out),
     )
 
     def save(n, k):
         return pltpu.make_async_copy(saves[k][0], saves[k][1].at[n], save_sem.at[k])
 
     def save_kept(n):
-        return pltpu.make_async_copy(kept.at[n], kept_hbm.at[n], save_sem.at[5])
+        return pltpu.make_async_copy(kept.at[n], kept_hbm.at[n], save_sem.at[6])
 
     def turn(source, target, n, blocks):
         def one(j, carry):
@@ -974,58 +967,45 @@
 
         lax.fori_loop(1, PEERS, settle, 0)
 
-    def gate_copy(n, i, slot, k):
-        columns = pl.ds(pl.multiple_of(k * 3072 + i * 512, 512), 512)
-        return pltpu.make_async_copy(
-            gate_up.at[slot, k], both_out.at[n, :, columns], gate_sem.at[slot, k]
-        )
-
-    def widen(n, part):
+    def widen(n, base, part):
+        def body(i, slot):
+            columns = pl.ds(pl.multiple_of(base + i * 512, 512), 512)
+            result = jnp.dot(low[...], cols_w[slot], preferred_element_type=jnp.float32)
+            both[:, columns] = result
+            if base > 0:
+                inner = pl.ds(pl.multiple_of(i * 512, 512), 512)
+                gate = both[:, inner]
+                hidden_low[:, inner] = (gate * jax.nn.sigmoid(gate) * result).astype(jnp.bfloat16)
+
+        stream_blocks(
+            3 * part,
+            3,
+            BUFFERS,
+            lambda i, slot: cols_copy(wide_w, n, base + i * 512, slot).start(),
+            lambda i, slot: cols_copy(wide_w, n, base + i * 512, slot).wait(),
+            body,
+        )
+
+    def gate_part(n, part):
         @pl.when(part == 0)
         def opening():
             gather.ready(n, 4)
+
+        widen(n, 0, part)
+
+    def up_part(n, part):
+        @pl.when(part == 0)
+        def opening():
             gather.ready(n, 5)
 
-        def column(i):
-            return i % 2 * 3072 + i // 2 * 512
-
-        def body(i, slot):
-            k = i % 2
-            at = i // 2
-            held = at % 2
-
-            @pl.when(i >= 4)
-            def settle():
-                gate_copy(n, at - 2, held, k).wait()
-
-            gate_up[held, k] = jnp.dot(
-                low[...], cols_w[slot], preferred_element_type=jnp.float32
-            )
-            gate_copy(n, at, held, k).start()
-
-            @pl.when(k == 1)
-            def finish():
-                gate = gate_up[held, 0]
-                columns = pl.ds(pl.multiple_of(at * 512, 512), 512)
-                hidden_low[:, columns] = (
-                    gate * jax.nn.sigmoid(gate) * gate_up[held, 1]
-                ).astype(jnp.bfloat16)
-
-        stream_blocks(
-            4 * part,
-            4,
-            BUFFERS,
-            lambda i, slot: cols_copy(wide_w, n, column(i), slot).start(),
-            lambda i, slot: cols_copy(wide_w, n, column(i), slot).wait(),
-            body,
-        )
-        @pl.when(part == 2)
+        widen(n, 3072, part)
+
+        @pl.when(part == 1)
         def closing():
-            for at in (4, 5):
-                for k in range(2):
-                    gate_copy(n, at, at % 2, k).wait()
+            save(n, 5).start()
 
     def turn_hidden(n):
+        gather.pass_on(n, 6)
         turn(hidden_low, hidden_t, n, 24)
 
     def narrow(n):
@@ -1046,7 +1026,7 @@
             lambda i, slot: rows_copy(down_w, n, i, slot).wait(),
             body,
         )
-        for k in range(1, 5):
+        for k in range(1, 6):
             save(n, k).wait()
         save_kept(n).wait()
 
@@ -1065,8 +1045,8 @@
         n = jnp.where(u >= SCHEDULE[1][0], 1, 0)
         pieces = (
             (1, keys_part), (1, values_part), (1, queries_part), (1, spread_queries),
-            (4, attention), (1, close_attention), (1, middle_norm), (3, widen), (1, turn_hidden),
-            (1, narrow),
+            (4, attention), (1, close_attention), (1, middle_norm), (2, gate_part),
+            (2, up_part), (1, turn_hidden), (1, narrow),
         )
         index = 0
         for blocks, work in pieces:
@@ -1116,7 +1096,7 @@
         out_shape=[jax.ShapeDtypeStruct(s, d) for s, d in results],
         in_specs=[anywhere] * MEMBERS + [near] * 5 + [pl.BlockSpec(memory_space=pltpu.SMEM)] * 2,
         out_specs=[anywhere] * 11 + [near] * 13,
-        scratch_shapes=gather_scratch(count)
+        scratch_shapes=gather_scratch()
         + [
             pltpu.VMEM((2, count, 512), wide),
             pltpu.VMEM((2, count, 512), wide),
@@ -1128,7 +1108,7 @@
             pltpu.VMEM((128, 1024), low),
             pltpu.VMEM((128, 2048), low),
             pltpu.VMEM((128, 3072), low),
-            pltpu.VMEM((2, 2, 128, 512), wide),
+            pltpu.VMEM((128, 6144), wide),
             pltpu.VMEM((BUFFERS, 1024, 512), low),
             pltpu.VMEM((BUFFERS, 512, 1024), low),
             pltpu.VMEM((count, PEERS, 4, 128, HEAD_SIZE), low),
@@ -1138,7 +1118,7 @@
             pair,
             pair,
             pltpu.VMEM((PEERS, HEAD_SIZE, 128), low),
-            dma((4,)), dma((BUFFERS,)), dma((BUFFERS,)), dma((2, 2)), dma((6,)),
+            dma((4,)), dma((BUFFERS,)), dma((BUFFERS,)), dma((7,)),
         ]
         + [dma((PEERS,))] * 6,
         compiler_params=pltpu.CompilerParams(

time: 460 us -> 444 us (0.965)
  Pallas kernels: 457 us -> 441 us
    pallas_call x1, Pallas kernels: 198 us -> 185 us  [forward(): pl.pallas_call(forward_kernel, out_shape=[jax.ShapeDtypeStruct(s, d) for...]
where the time goes in v7:
time: 444 us; the launch traced here: 443 us
  Pallas kernels  441 us (99%)
    pallas_call x1, Pallas kernels, backward(): pl.pallas_call(backward_kernel, out_shape=[jax.ShapeDtypeStruct((count,)...  250 us
    pallas_call x1, Pallas kernels, forward(): pl.pallas_call(forward_kernel, out_shape=[jax.ShapeDtypeStruct(s, d) for...  185 us

profile of v7, /device:TPU:0, one launch (start us, length us, event | category | flops | bytes accessed | tf_op | source)
XLA Modules:
  0.0 443.0 jit_solution(391398296790111524)
XLA Ops:
  0.6 1.4 copy.28.refs_12_
  2.0 185.1 %forward.1 = (bf16[2,1024,4096]{2,1,0:T(8,128)(2,1)}, bf16[2,2048,1024]{2,1,0:T(8,128)(2,1)}, bf16[2,1024,6144]{2,1,0:T(8,128)(2,1)}, bf16[2,3072,1024]{2,1,0:T(...) custom-call(bf16[2,512,1024]{2,1,0:T(8,128)(2,1)} %refs_0_.1, ...), custom_call_target="tpu_custom_call" | custom-call | tf_op jit(solution)/shard_map/forward/pallas_call | solution.py:1094
  187.1 250.2 %backward.1 = (f32[2,32,2048]{2,1,0:T(8,128)}, f32[2,32,1024]{2,1,0:T(8,128)}, f32[2,32,1024]{2,1,0:T(8,128)}, f32[2,64,1024]{2,1,0:T(8,128)}, f32[2,32,3072]{2,...) custom-call(bf16[2,4,2,2,2,3,32,128]{7,6,5,4,3,2,1,0:T(8,128)(2,1)} , ...), custom_call_target="tpu_custom_call" | custom-call | tf_op jit(solution)/shard_map/backward/pallas_call | solution.py:1524
  437.3 5.7 %finish.1 = (bf16[128,1024]{1,0:T(8,128)(2,1)}, f32[128,1024]{1,0:T(8,128)}, f32[2,32,2048]{2,1,0:T(8,128)}, f32[2,32,1024]{2,1,0:T(8,128)}, f32[2,32,1024]{2,1,...) custom-call(bf16[128,1024]{1,0:T(8,128)(2,1)} %get-tuple-element.46., ...), custom_call_target="tpu_custom_call" | custom-call | tf_op jit(solution)/shard_map/finish/pallas_call | solution.py:1604

commit v8 on v7

--- a/solution.py
+++ b/solution.py
@@ -645,7 +645,7 @@
 BUFFERS = 4
 SCHEDULE = (
     (9, 12, 15, 16, 20, 21, 22, 23, 28, 29, 31, 32, 33, 34, 35, 36),
-    (37, 37, 38, 38, 42, 43, 44, 45, 46, 46, 46, 47, 48, 49, 49, 50),
+    (37, 37, 38, 38, 41, 42, 43, 44, 45, 45, 45, 46, 47, 48, 48, 49),
 )
 
 

time: 444 us -> 444 us (level)
  no operation moved by 1% of the time
where the time goes in v8:
time: 444 us; the launch traced here: 443 us
  Pallas kernels  441 us (99%)
    pallas_call x1, Pallas kernels, backward(): pl.pallas_call(backward_kernel, out_shape=[jax.ShapeDtypeStruct((count,)...  251 us
    pallas_call x1, Pallas kernels, forward(): pl.pallas_call(forward_kernel, out_shape=[jax.ShapeDtypeStruct(s, d) for...  184 us

profile of v8, /device:TPU:0, one launch (start us, length us, event | category | flops | bytes accessed | tf_op | source)
XLA Modules:
  0.0 442.8 jit_solution(6188716471015360967)
XLA Ops:
  0.6 1.4 copy.28.refs_12_
  2.0 184.5 %forward.1 = (bf16[2,1024,4096]{2,1,0:T(8,128)(2,1)}, bf16[2,2048,1024]{2,1,0:T(8,128)(2,1)}, bf16[2,1024,6144]{2,1,0:T(8,128)(2,1)}, bf16[2,3072,1024]{2,1,0:T(...) custom-call(bf16[2,512,1024]{2,1,0:T(8,128)(2,1)} %refs_0_.1, ...), custom_call_target="tpu_custom_call" | custom-call | tf_op jit(solution)/shard_map/forward/pallas_call | solution.py:1094
  186.5 250.6 %backward.1 = (f32[2,32,2048]{2,1,0:T(8,128)}, f32[2,32,1024]{2,1,0:T(8,128)}, f32[2,32,1024]{2,1,0:T(8,128)}, f32[2,64,1024]{2,1,0:T(8,128)}, f32[2,32,3072]{2,...) custom-call(bf16[2,4,2,2,2,3,32,128]{7,6,5,4,3,2,1,0:T(8,128)(2,1)} , ...), custom_call_target="tpu_custom_call" | custom-call | tf_op jit(solution)/shard_map/backward/pallas_call | solution.py:1524
  437.1 5.7 %finish.1 = (bf16[128,1024]{1,0:T(8,128)(2,1)}, f32[128,1024]{1,0:T(8,128)}, f32[2,32,2048]{2,1,0:T(8,128)}, f32[2,32,1024]{2,1,0:T(8,128)}, f32[2,32,1024]{2,1,...) custom-call(bf16[128,1024]{1,0:T(8,128)(2,1)} %get-tuple-element.46., ...), custom_call_target="tpu_custom_call" | custom-call | tf_op jit(solution)/shard_map/finish/pallas_call | solution.py:1604
